TPU v7x, 256 devices: a whole 4x4x8 slice. The times are simulated.
256 devices in a mesh: vp: 4 (over x), cp: 8 (over z_hi, core), ga: 8 (over y, z_lo).
Axes of the slice: x: 4, y: 4, z: 8 (z_hi: 4, z_lo: 2; z = z_hi * 2 + z_lo), core: 2. Of those that a mesh axis runs over, the one named last changes fastest.
Arguments:
- valence_wavefunction: bfloat16 [512, 24576], P(('vp', 'cp'), 'ga'), may hold values from -6 to 6
- cond_wave: bfloat16 [512, 24576], P(('vp', 'cp'), 'ga'), may hold values from -6 to 6
- screen_basis: bfloat16 [24576, 1024], P('ga'), may hold values from -0.0390625 to 0.0390625
- screen: float32 [1024], replicated, may hold values from 0.01 to 0.1
- coulomb: float32 [1024], replicated, may hold values from 0.02 to 0.2
- window_rows: int32 [2], replicated, may hold values from 0 to 1023
- tile_owner: int32 [192], P(('vp', 'cp')), may hold values from 0 to 4095, as said below
Outputs:
- kernel: float32 [2, 192, 4096], P(None, ('vp', 'cp'), 'ga')
Inputs may be any that keep to these rules, and one draw needn't show every extreme that they name: `tile_owner`: distinct pair-block indices; 0 and 4095 both occur.
All inputs are finite; a program needn't handle non-finite values.
Results may differ from a plain program's by a relative error of at most 0.02.
Values may be sent and summed in bfloat16 or wider, within the bound.
No kernel may reach another device: no remote copies, remote signals or barrier semaphores. Data moves between devices by JAX's collectives and lax.ppermute only.
A program may use at most 64 MiB of HBM per device.

v0:
```python
import jax
import jax.numpy as jnp
from jax import lax
from jax.sharding import PartitionSpec as P

R = 1024
TV = 8
TC = 8
NCT = 64


def sent_together(arrays, axis, dim, along):
    widths = [a.shape[along] for a in arrays]
    both = jnp.concatenate(arrays, axis=along)
    result = lax.all_gather(both, axis, axis=dim, tiled=True)
    return tuple(jnp.split(result, [sum(widths[:k]) for k in range(1, len(widths))], axis=along))


def in_one_piece(arrays, axis, dim, along):
    both = jnp.concatenate(arrays, axis=along)
    result, at, done = (lax.psum_scatter(both, axis, scatter_dimension=dim, tiled=True), 0, [])
    for a in arrays:
        done.append(lax.slice_in_dim(result, at, at + a.shape[along], axis=along))
        at += a.shape[along]
    return tuple(done)


def in_blocks(array, dim, size):
    lengths = array.shape
    pieces = array.reshape(*lengths[:dim], size, lengths[dim] // size, *lengths[dim + 1 :])
    return jnp.moveaxis(pieces, dim, 0)


def sum_at_owner(array, axis, dim):
    pieces = in_blocks(array, dim, lax.axis_size(axis))
    arrived = lax.all_to_all(pieces, axis, split_axis=0, concat_axis=0, tiled=True)
    return arrived.astype(jnp.float32).sum(axis=0)


def select_bands(wanted, shard_part):
    row_ids = jnp.arange(shard_part.shape[0], dtype=jnp.int32)
    chooser = (wanted[:, None] == row_ids[None, :]).astype(jnp.bfloat16)
    return jnp.dot(chooser, shard_part, preferred_element_type=jnp.float32)


def outer_rows(left_wavefunction, right_wave):
    product = (
        left_wavefunction.astype(jnp.float32)[..., :, None, :]
        * right_wave.astype(jnp.float32)[..., None, :, :]
    )
    return product.astype(jnp.bfloat16)


def contract(row_proj, col_proj, val_proj, cond_proj, screen_part, coulomb_part):
    exchange_term = jnp.einsum("qacr,svdr->qsacvd", row_proj * coulomb_part, col_proj)
    direct_term = jnp.einsum("qsavr,qscdr->qsacvd", val_proj * screen_part, cond_proj)
    total = 2.0 * exchange_term - direct_term
    return total.reshape(total.shape[0], total.shape[1], -1)


def shards(valence_wavefunction, cond_wave, screen_basis, screen, coulomb, window_rows, tile_owner):
    slot_count = tile_owner.shape[0]
    grid_count = valence_wavefunction.shape[1]
    pair_tiles = jnp.concatenate([window_rows, tile_owner])
    val_wanted = (
        (pair_tiles // NCT)[:, None] * TV + jnp.arange(TV, dtype=jnp.int32)[None, :]
    ).reshape(-1)
    conduction_wanted = (
        (pair_tiles % NCT)[:, None] * TC + jnp.arange(TC, dtype=jnp.int32)[None, :]
    ).reshape(-1)
    pieces = sent_together((valence_wavefunction, cond_wave), ("vp", "cp"), 0, 1)
    picked_val = select_bands(val_wanted, pieces[0])
    picked_cond = select_bands(conduction_wanted, pieces[1])
    picked_val = picked_val.astype(jnp.bfloat16).reshape(2 + slot_count, TV, grid_count)
    picked_cond = picked_cond.astype(jnp.bfloat16).reshape(2 + slot_count, TC, grid_count)
    row_val = picked_val[:2]
    slot_valence = picked_val[2:]
    row_cond = picked_cond[:2]
    slot_cond = picked_cond[2:]
    row_rho = outer_rows(row_val, row_cond).reshape(2 * TV * TC, grid_count)
    col_rho = outer_rows(slot_valence, slot_cond).reshape(slot_count * TV * TC, grid_count)
    val_rho = outer_rows(row_val[:, None], slot_valence[None]).reshape(
        2 * slot_count * TV * TV, grid_count
    )
    cond_rho = outer_rows(row_cond[:, None], slot_cond[None]).reshape(
        2 * slot_count * TC * TC, grid_count
    )
    row_part = jnp.dot(row_rho, screen_basis, preferred_element_type=jnp.float32)
    col_part = jnp.dot(col_rho, screen_basis, preferred_element_type=jnp.float32)
    val_part = jnp.dot(val_rho, screen_basis, preferred_element_type=jnp.float32)
    cond_part = jnp.dot(cond_rho, screen_basis, preferred_element_type=jnp.float32)
    live_tile = (tile_owner[None, :] >= window_rows[:, None])[:, :, None]
    grid_groups = lax.axis_size("ga")
    rank_span = R // grid_groups
    rank_first = lax.axis_index("ga") * rank_span
    row_sum, col_sum, val_sum, cond_sum = tuple(
        (
            part.astype(jnp.float32)
            for part in in_one_piece(
                (
                    row_part.astype(jnp.bfloat16),
                    col_part.astype(jnp.bfloat16),
                    val_part.astype(jnp.bfloat16),
                    cond_part.astype(jnp.bfloat16),
                ),
                "ga",
                1,
                0,
            )
        )
    )
    screen_part = lax.dynamic_slice_in_dim(screen, rank_first, rank_span, 0)
    coulomb_part = lax.dynamic_slice_in_dim(coulomb, rank_first, rank_span, 0)
    kernel = contract(
        row_sum.reshape(2, TV, TC, rank_span),
        col_sum.reshape(slot_count, TV, TC, rank_span),
        val_sum.reshape(2, slot_count, TV, TV, rank_span),
        cond_sum.reshape(2, slot_count, TC, TC, rank_span),
        screen_part,
        coulomb_part,
    )
    kernel = jnp.where(live_tile, kernel, jnp.zeros_like(kernel))
    return sum_at_owner(kernel.astype(jnp.bfloat16), "ga", 2)


def solution(mesh):
    in_specs = (
        P(("vp", "cp"), "ga"),
        P(("vp", "cp"), "ga"),
        P("ga", None),
        P(),
        P(),
        P(),
        P(("vp", "cp")),
    )
    out_specs = P(None, ("vp", "cp"), "ga")
    return jax.shard_map(shards, mesh=mesh, in_specs=in_specs, out_specs=out_specs, check_vma=False)
```

profile of v0, /device:TPU:1, one launch (start us, length us, event | category | flops | bytes accessed | tf_op | source)
XLA Modules:
  0.0 239.7 jit_solution(8601180034710010542)
XLA Ops:
  6.5 0.0 all-gather.2.cloned.1.call-start
  6.5 1.6 pad_maximum_fusion.1
  8.2 0.0 all-gather.2.cloned.1.call-update
  8.2 0.0 reduce-scatter.4.cloned.1.call-start
  8.2 0.8 fusion.13
  9.0 0.1 iota_add_fusion
  9.1 0.1 add.69
  9.2 0.1 iota_add_fusion.1
  9.2 0.1 add.64
  9.3 73.8 %all-gather.2.cloned.1.call-done = bf16[512,6144]{1,0:T(8,128)(2,1)} async-done(((bf16[16,6144]{1,0:T(8,128)(2,1)}), bf16[512,6144]{1,0:T(8,128)(2,1)}) %all-gather.2.cloned.1.call-update) | async-done | bytes 6291472 | tf_op jit(solution)/shard_map/all_gather | solution.py:15
  83.1 2.6 %convolution_convert_fusion = bf16[64,3072]{1,0:T(8,128)(2,1)S(1)} fusion(bf16[512,6144]{1,0:T(8,128)(2,1)} %all-gather.2.cloned.1.call-done, s32[64]{0:T(128)S(1)} %add.69), kind=kOutput, calls=%fused_computation.4 | convolution fusion | flops 201555968 | bytes 3539200 | tf_op jit(solution)/shard_map/dot_general | solution.py:43
  85.7 2.6 %convolution_convert_fusion.1 = bf16[64,3072]{1,0:T(8,128)(2,1)S(1)} fusion(bf16[512,6144]{1,0:T(8,128)(2,1)} %all-gather.2.cloned.1.call-done, s32[64]{0:T(128)S(1)} %add.64), kind=kOutput, calls=%fused_computation.5 | convolution fusion | flops 201555968 | bytes 3539200 | tf_op jit(solution)/shard_map/dot_general | solution.py:43
  88.3 0.1 fusion.4
  88.4 0.1 multiply_convert_fusion.3
  88.5 0.0 slice-start
  88.6 1.0 multiply_convert_fusion.1
  89.6 0.0 slice-start.1
  89.6 0.4 multiply_convert_fusion.2
  90.0 1.0 multiply_convert_fusion
  91.1 0.5 slice-done.1
  91.7 1.0 convolution_convert_fusion.5
  92.7 2.6 %convolution_convert_fusion.4 = bf16[384,1024]{1,0:T(8,128)(2,1)S(1)} fusion(bf16[384,3072]{1,0:T(8,128)(2,1)S(1)} %bitcast.73, bf16[3072,1024]{1,0:T(8,128)(2,1)S(1)} %bitcast.69), kind=kOutput, calls=%fused_computation.12 | convolution fusion | flops 2416312320 | bytes 9437184 | tf_op jit(solution)/shard_map/dot_general | solution.py:89
  95.3 5.1 %convolution_convert_fusion.3 = bf16[768,1024]{1,0:T(8,128)(2,1)S(1)} fusion(bf16[768,3072]{1,0:T(8,128)(2,1)S(1)} %bitcast.70, bf16[3072,1024]{1,0:T(8,128)(2,1)S(1)} %bitcast.69), kind=kOutput, calls=%fused_computation.10 | convolution fusion | flops 4832624640 | bytes 12582912 | tf_op jit(solution)/shard_map/dot_general | solution.py:90
  100.4 5.2 %convolution_convert_fusion.2 = bf16[768,1024]{1,0:T(8,128)(2,1)S(1)} fusion(bf16[768,3072]{1,0:T(8,128)(2,1)S(1)} %bitcast.71, bf16[3072,1024]{1,0:T(8,128)(2,1)S(1)} %bitcast.69), kind=kOutput, calls=%fused_computation.9 | convolution fusion | flops 4832624640 | bytes 12582912 | tf_op jit(solution)/shard_map/dot_general | solution.py:91
  105.6 2.3 pad_maximum_fusion
  107.9 6.6 %copy.30 = bf16[2048,1024]{0,1:T(8,128)(2,1)} copy(bf16[2048,1024]{1,0:T(8,128)(2,1)} %pad_maximum_fusion) | data formatting | bytes 8388608
  114.5 0.0 reduce-scatter.4.cloned.1.call-update
  114.5 0.8 dynamic_slice.7
  115.3 0.8 dynamic_slice.6
  116.1 0.1 broadcast_compare_fusion
  116.1 89.8 %reduce-scatter.4.cloned.1.call-done = bf16[128,2048]{1,0:T(8,128)(2,1)} async-done(((bf16[1024,2048]{1,0:T(8,128)(2,1)}), bf16[128,2048]{1,0:T(8,128)(2,1)}) %reduce-scatter.4.cloned.1.call-update) | async-done | bytes 524304
  206.0 0.8 slice.41
  206.7 0.9 slice.40
  207.6 1.1 fusion.14
  208.7 0.1 copy.33
  208.8 0.2 copy.35
  209.0 0.1 copy.32
  209.1 0.2 copy.34
  209.3 2.9 %fusion.2 = f32[2,6,8,8,8,8]{5,3,4,2,1,0:T(8,128)} fusion(bf16[2,6,8,8,128,1]{4,3,5,2,1,0:T(8,128)(2,1)S(1)} %bitcast.75, bf16[2,6,8,8,128]{4,3,2,1,0:T(8,128)(2,1)S(1)} %bitcast.74, f32[128]{0:T(128)S(1)} %dynamic_slice.7), kind=kOutput, calls=%fused_computation.14 | convolution fusion | flops 12779520 | bytes 590336 | tf_op jit(solution)/shard_map/qsavr,qscdr->qsacvd/dot_general | solution.py:56
  212.2 4.3 %copy.21 = f32[2,6,8,8,8,8]{2,3,4,0,5,1:T(8,128)S(1)} copy(f32[2,6,8,8,8,8]{5,3,4,2,1,0:T(8,128)} %fusion.2) | data formatting | bytes 393216 | tf_op jit(solution)/shard_map/qsavr,qscdr->qsacvd/dot_general | solution.py:56
  216.5 1.7 bitcast_subtract_fusion
  218.3 2.1 copy.22
  220.4 2.6 %reshape.288 = bf16[2,6,8,512]{3,2,1,0:T(8,128)(2,1)S(1)} reshape(bf16[2,6,8,8,8,8]{5,4,3,2,1,0:T(8,128)(2,1)S(1)} %copy.22) | data formatting | bytes 196608 | tf_op jit(solution)/shard_map/reshape | solution.py:58
  223.0 0.1 fusion.7
  223.1 0.1 copy.23
  223.2 8.9 %all_to_all.5 = bf16[8,2,6,512]{3,1,2,0:T(2,128)(2,1)S(1)} all-to-all(bf16[8,2,6,512]{3,1,2,0:T(2,128)(2,1)S(1)} %copy.23), channel_id=1, replica_groups=mesh['vp'=4,'cp'=8,'ga'=8] {'ga'}, dimensions={0} | all-to-all | bytes 196608 | tf_op jit(solution)/shard_map/all_to_all | solution.py:36
  232.2 0.1 convert_reduce_fusion
  232.2 0.6 copy.25
  (9 shorter events, 0.1 us)
Async XLA Ops:
  6.5 76.5 %all-gather.2.cloned.1.call-start = ((), (), s32[]{:S(2)}) async-start(), calls=%async_computation.2 | async-start | bytes 6488064 | tf_op jit(solution)/shard_map/all_gather | solution.py:15
  8.2 197.8 %reduce-scatter.4.cloned.1.call-start = ((), (), s32[]{:S(2)}) async-start(), calls=%async_computation.3 | async-start | bytes 4718592
  88.5 2.6 %slice-start = ((s8[6291456]{0:T(1024)(128)(4,1)}), s8[4194304]{0:T(1024)(128)(4,1)S(1)}, s32[]{:S(2)}) async-start(s8[6291456]{0:T(1024)(128)(4,1)} %bitcast.68), calls=%async_computation.4 | async-start | bytes 8388608
  89.6 2.0 slice-start.1
  107.9 8.1 %copy-start = (s32[6]{0:T(128)S(1)}, s32[6]{0:T(128)}, u32[]{:S(2)}) copy-start(s32[6]{0:T(128)} %param.13) | copy-start | bytes 76
  107.9 8.1 %copy-start.1 = (s32[2]{0:T(128)S(1)}, s32[2]{0:T(128)}, u32[]{:S(2)}) copy-start(s32[2]{0:T(128)} %param.12) | copy-start | bytes 28
Sparse Core Ops, SparseCore 0:
  9.9 73.1 all-gather.1
  114.6 91.2 reduce-scatter.3
where the time goes:
time: 241 us; the launch traced here: 240 us
  waiting for transfers between devices  164 us (68%)
  matrix products  23.8 us (10%)
  local copies, waits for them, and re-layouts  21.9 us (9%)
  between operations  13.6 us (6%)
  blocking collectives  8.95 us (4%)
  other arithmetic  7.81 us (3%)
    unnamed x3, waiting for transfers between devices  89.9 us
    all_gather x1, waiting for transfers between devices, sent_together(): result = lax.all_gather(both, axis, axis=dim, tiled=True)  73.8 us
    all_to_all x1, blocking collectives, sum_at_owner(): lax.all_to_all(pieces, axis, split_axis=0, concat_axis=0, tiled=True)  8.95 us
    unnamed x13, local copies, waits for them, and re-layouts  7.73 us
    dot_general x1, matrix products, shards(): jnp.dot(cond_rho, screen_basis, preferred_element_type=jnp.float32)  5.23 us
    dot_general x2, matrix products, select_bands(): return jnp.dot(chooser, shard_part, preferred_element_type=jnp.float32)  5.18 us
    dot_general x1, matrix products, shards(): jnp.dot(val_rho, screen_basis, preferred_element_type=jnp.float32)  5.05 us
  transfers between devices with their start and end apart: 2, of which 2 were waited for; matrix products, arithmetic and copies ran while one was open for 1% of the time, Pallas kernels for 0%

commit v1 on v0

v1 whole, which is shorter than its diff:
```python
import functools
import jax
import jax.numpy as jnp
from jax import lax
from jax.experimental import pallas as pl
from jax.experimental.pallas import tpu as pltpu
from jax.sharding import PartitionSpec as P

R = 1024
TV = 8
TC = 8
NCT = 64
F32 = jnp.float32
BF16 = jnp.bfloat16


def shift(array, axis, send_to):
    size = lax.axis_size(axis)
    return lax.ppermute(array, axis, [(n, send_to(n)) for n in range(size)])


def bands_of(tile):
    device = tile // 2
    return device // 8, device % 8, tile % 2


def pick_rows(columns, window_rows, j):
    picked = []
    for first, tiles in ((0, window_rows // NCT), (16, window_rows % NCT)):
        for q in range(2):
            at, column, half = bands_of(tiles[q])
            rows = lax.dynamic_slice(
                columns, (at, first + 8 * half, 0), (1, 8, columns.shape[2])
            )[0]
            picked.append(jnp.where(column == j, rows, jnp.zeros_like(rows)))
    return jnp.concatenate(picked, axis=0)


def spread_over_columns(rows, core):
    half = rows.shape[1] // 2
    low, high = rows[:, :half], rows[:, half:]
    mine = jnp.where(core == 0, low, high)
    other = jnp.where(core == 0, high, low)
    mine = mine + shift(other, "cp", lambda n: n ^ 1)
    parts = [shift(mine, "cp", lambda n, s=s: (n + 2 * s) % 8) for s in (1, 2, 3)]
    mine = mine + parts[0] + parts[1] + parts[2]
    other = shift(mine, "cp", lambda n: n ^ 1)
    return jnp.where(
        core == 0,
        jnp.concatenate([mine, other], axis=1),
        jnp.concatenate([other, mine], axis=1),
    )


def pair_block(left, right):
    product = left.astype(F32)[:, None, :] * right.astype(F32)[None, :, :]
    return product.reshape(-1, left.shape[1])


def exchange_kernel(ids_ref, val_ref, cond_ref, w_ref, out_ref):
    slots = ids_ref.shape[0]
    together = 4

    def band_rows(ref, tile):
        at, column, half = bands_of(tile)
        both = ref[column * 4 + at].astype(F32)
        return jnp.where(half == 0, both[:8], both[8:])

    def body(step, carry):
        pairs = []
        for n in range(together):
            owner = ids_ref[step * together + n]
            left = band_rows(val_ref, owner // NCT)
            right = band_rows(cond_ref, owner % NCT)
            pairs.append(pair_block(left, right).astype(BF16))
        pair = jnp.concatenate(pairs, axis=0)
        result = lax.dot_general(
            w_ref[...], pair, (((1,), (1,)), ((), ())), preferred_element_type=F32
        )
        for n in range(together):
            tile = result[:, n * 64 : (n + 1) * 64]
            out_ref[step * together + n] = jnp.concatenate(
                [tile[c * 16 : (c + 1) * 16] for c in range(8)], axis=1
            )
        return carry

    lax.fori_loop(0, slots // together, body, 0)


def exchange_tiles(ids, val_waves, cond_waves, potential):
    slots = ids.shape[0]
    vmem = pl.BlockSpec(memory_space=pltpu.VMEM)
    return pl.pallas_call(
        exchange_kernel,
        out_shape=jax.ShapeDtypeStruct((slots, 16, 512), F32),
        in_specs=[pl.BlockSpec(memory_space=pltpu.SMEM), vmem, vmem, vmem],
        out_specs=vmem,
        compiler_params=pltpu.CompilerParams(vmem_limit_bytes=32 * 2**20),
        cost_estimate=pl.CostEstimate(
            flops=2 * slots * 64 * 128 * 768, bytes_accessed=2**22, transcendentals=0
        ),
    )(ids, val_waves, cond_waves, potential)


def direct_kernel(ids_ref, val_ref, cond_ref, order_ref, exchange_ref, out_ref, held_ref):
    slots = ids_ref.shape[0]
    lane = lax.broadcasted_iota(jnp.int32, (8, 128), 1)

    def lanes_of(ref, tile):
        at, column, half = bands_of(tile)
        first = pl.multiple_of((at * 2 + half) * 128, 128)
        return ref[column, :, pl.ds(first, 128)]

    def body(slot, carry):
        owner = ids_ref[slot]
        left = lanes_of(val_ref, owner // NCT)
        right = lanes_of(cond_ref, owner % NCT)
        tile = lax.dot_general(
            left, right, (((0,), (0,)), ((), ())), preferred_element_type=F32
        )
        rows = []
        for q in range(2):
            blocks = []
            for m in range(4):
                even = tile[q * 64 + m * 16 : q * 64 + m * 16 + 8]
                odd = tile[q * 64 + m * 16 + 8 : q * 64 + m * 16 + 16]
                if q == 0:
                    odd = pltpu.roll(odd, 64, 1)
                else:
                    even = pltpu.roll(even, 64, 1)
                blocks.append(jnp.where(lane < 64, even, odd))
            rows.append(jnp.concatenate(blocks, axis=1))
        held_ref[slot] = jnp.concatenate(rows, axis=0).astype(BF16)
        return carry

    lax.fori_loop(0, slots, body, 0)
    for part in range(4):
        few = slots // 4
        direct = jnp.dot(
            held_ref[part * few : (part + 1) * few].reshape(few * 16, 512),
            order_ref[...],
            preferred_element_type=F32,
        ).reshape(few, 16, 512)
        total = 2.0 * exchange_ref[part * few : (part + 1) * few] - direct
        out_ref[part * few : (part + 1) * few] = total.astype(BF16)


def kernel_tiles(ids, val_proj, cond_proj, order, exchange):
    slots = ids.shape[0]
    vmem = pl.BlockSpec(memory_space=pltpu.VMEM)
    return pl.pallas_call(
        direct_kernel,
        out_shape=jax.ShapeDtypeStruct((slots, 16, 512), BF16),
        in_specs=[pl.BlockSpec(memory_space=pltpu.SMEM), vmem, vmem, vmem, vmem],
        out_specs=vmem,
        scratch_shapes=[pltpu.VMEM((slots, 16, 512), BF16)],
        compiler_params=pltpu.CompilerParams(vmem_limit_bytes=32 * 2**20),
    )(ids, val_proj, cond_proj, order, exchange)


def gather_columns(array):
    step = [array] + [
        shift(array, "cp", lambda n, s=s: (n + 2 * s) % 8) for s in (1, 2, 3)
    ]
    swapped = [shift(a, "cp", lambda n: n ^ 1) for a in step]
    return step, swapped


def shards(valence_wavefunction, cond_wave, screen_basis, screen, coulomb, window_rows, tile_owner):
    i = lax.axis_index("vp")
    j = lax.axis_index("cp")
    k = lax.axis_index("ga")
    core = j % 2
    own_slots = tile_owner.shape[0]
    grid_count = valence_wavefunction.shape[1]
    quarter = grid_count // 4
    rank_quarter = R // 4
    rank_part = rank_quarter // 8

    from_others = jnp.stack(
        [tile_owner] + [shift(tile_owner, "vp", lambda n, s=s: (n + s) % 4) for s in (1, 2, 3)]
    )
    ids = jnp.take(from_others, (i - jnp.arange(4)) % 4, axis=0).reshape(-1)
    waves = jnp.concatenate([valence_wavefunction, cond_wave], axis=0)
    columns = lax.all_gather(waves, "vp", axis=0)

    rows = spread_over_columns(pick_rows(columns, window_rows, j), core)

    quarter_waves = lax.dynamic_slice_in_dim(columns, i * quarter, quarter, 2)
    quarter_waves, rows = lax.optimization_barrier((quarter_waves, rows))
    val_waves = lax.all_gather(quarter_waves[:, :16], "cp", axis=0)
    cond_waves = lax.all_gather(quarter_waves[:, 16:], "cp", axis=0)

    row_val = rows[:16].reshape(2, TV, grid_count).astype(F32)
    row_cond = rows[16:].reshape(2, TC, grid_count).astype(F32)
    col_val = columns[:, :16].reshape(8, TV, grid_count).astype(F32)
    col_cond = columns[:, 16:].reshape(8, TC, grid_count).astype(F32)
    basis_ranks = lax.dynamic_slice_in_dim(screen_basis, i * rank_quarter, rank_quarter, 1)

    def project(pairs, basis):
        flat = pairs.astype(BF16).reshape(-1, grid_count)
        return lax.dot_general(
            basis, flat, (((0,), (1,)), ((), ())), preferred_element_type=F32
        ).astype(BF16)

    val_part = project(col_val[:, None, :, None] * row_val[None, :, None, :], basis_ranks)
    cond_part = project(row_cond[None, :, :, None] * col_cond[:, None, None, :], basis_ranks)
    row_part = project(
        jnp.swapaxes(row_cond, 0, 1)[:, :, None] * row_val[None], screen_basis
    )
    row_part = row_part.reshape(8, 4, rank_part, 128)
    row_part = jnp.swapaxes(row_part, 1, 2).reshape(8, rank_part, 512)
    sent = jnp.concatenate(
        [
            val_part.reshape(8, rank_part, 1024),
            cond_part.reshape(8, rank_part, 1024),
            row_part,
        ],
        axis=2,
    )
    arrived = lax.all_to_all(sent, "ga", split_axis=0, concat_axis=0, tiled=True)
    summed = arrived.astype(F32).sum(axis=0)

    screen_part = lax.dynamic_slice_in_dim(
        screen, i * rank_quarter + k * rank_part, rank_part, 0
    )
    coulomb_part = lax.dynamic_slice_in_dim(coulomb, k * (R // 8), R // 8, 0)
    val_sum = (summed[:, :1024] * screen_part[:, None]).astype(BF16)
    cond_sum = summed[:, 1024:2048].astype(BF16)
    row_sum = summed[:, 2048:].reshape(rank_part, 4, 128)
    row_sum = (row_sum * coulomb_part.reshape(4, rank_part).T[:, :, None]).astype(BF16)

    step, swapped = gather_columns(jnp.stack([val_sum, cond_sum]))

    row_sum = row_sum.reshape(rank_part, 512)
    row_all = lax.all_to_all(
        jnp.broadcast_to(row_sum[None], (8, rank_part, 512)),
        "ga", split_axis=0, concat_axis=0, tiled=True,
    )
    row_all = jnp.swapaxes(row_all.reshape(8, rank_part, 4, 128), 1, 2).reshape(R, 128)
    basis_rows = lax.dynamic_slice_in_dim(screen_basis, i * quarter, quarter, 0)
    potential = lax.dot_general(
        row_all, basis_rows, (((0,), (1,)), ((), ())), preferred_element_type=F32
    ).astype(BF16)
    exchange = exchange_tiles(
        ids,
        val_waves.reshape(32, 16, quarter),
        cond_waves.reshape(32, 16, quarter),
        potential,
    )

    listed = jnp.stack([a for two in zip(step, swapped) for a in two])
    at = jnp.arange(8, dtype=jnp.int32)
    where_from = ((j // 2 - at // 2) % 4) * 2 + ((j + at) % 2)
    place = jnp.argmax((where_from[None, :] == at[:, None]).astype(jnp.int32), axis=1)
    all_proj = jnp.take(listed, place, axis=0)
    order = jnp.arange(512, dtype=jnp.int32)
    source = (order // 8 % 8) * 64 + (order // 64) * 8 + order % 8
    order = (order[:, None] == source[None, :]).astype(BF16)
    tiles = kernel_tiles(ids, all_proj[:, 0], all_proj[:, 1], order, exchange)

    tiles = tiles.reshape(4, own_slots, 2, 8, 512)
    tiles = jnp.transpose(tiles, (0, 3, 2, 1, 4)).reshape(32, 2 * own_slots, 512)
    got = lax.all_to_all(tiles, ("vp", "ga"), split_axis=0, concat_axis=0, tiled=True)
    kernel = got.astype(F32).sum(axis=0).reshape(2, own_slots, 512)
    live_tile = (tile_owner[None, :] >= window_rows[:, None])[:, :, None]
    return jnp.where(live_tile, kernel, jnp.zeros_like(kernel))


def solution(mesh):
    in_specs = (
        P(("vp", "cp"), "ga"),
        P(("vp", "cp"), "ga"),
        P("ga", None),
        P(),
        P(),
        P(),
        P(("vp", "cp")),
    )
    out_specs = P(None, ("vp", "cp"), "ga")
    return jax.shard_map(shards, mesh=mesh, in_specs=in_specs, out_specs=out_specs, check_vma=False)
```

time: 241 us -> 178 us (0.74)
  waiting for transfers between devices: 164 us -> 19.1 us
  starting transfers between devices: 0.04 us -> 49.4 us
  blocking collectives: 8.95 us -> 54.4 us
  matrix products: 23.8 us -> 9.67 us
  Pallas kernels: 0 us -> 10.7 us
  local copies, waits for them, and re-layouts: 21.9 us -> 15 us
  between operations: 13.6 us -> 11 us
    unnamed x3 -> x0, waiting for transfers between devices: 89.9 us -> none
    all_gather x1 -> x0, waiting for transfers between devices: 73.8 us -> none  [sent_together(): result = lax.all_gather(both, axis, axis=dim, tiled=True)]
    all_gather x0 -> x3, blocking collectives: none -> 54.4 us  [the longest x1 26.8 us: shards(): val_waves = lax.all_gather(quarter_waves[:, :16], 'cp', axis=0)]
    ppermute x0 -> x15, starting transfers between devices: none -> 29.6 us  [shift(): return lax.ppermute(array, axis, [(n, send_to(n)) for n in range(size)])]
    all_to_all x0 -> x3, starting transfers between devices: none -> 19.8 us  [the longest x1 9.1 us: shards(): lax.all_to_all(tiles, ('vp', 'ga'), split_axis=0, concat_axis=0, tiled=True)]
    dot_general x8 -> x4, matrix products: 23.8 us -> 9.67 us  [the longest x3 7.6 us: project(): lax.dot_general(basis, flat, (((0,), (1,)), ((), ())), preferred_element_...]
    all_to_all x0 -> x3, waiting for transfers between devices: none -> 11.7 us  [the longest x1 11.7 us: shards(): lax.all_to_all(tiles, ('vp', 'ga'), split_axis=0, concat_axis=0, tiled=True)]
    pallas_call x0 -> x2, Pallas kernels: none -> 10.7 us  [the longest x1 7.53 us: kernel_tiles(): pl.pallas_call(direct_kernel, out_shape=jax.ShapeDtypeStruct((slots, 16,...]
  transfers between devices with their start and end apart: 2 -> 18, of which waited for: 2 -> 4; matrix products, arithmetic and copies ran while one was open for 1% -> 15% of each run, Pallas kernels for 0% -> 0%
where the time goes in v1:
time: 178 us
  blocking collectives  54.4 us (31%)
  starting transfers between devices  49.4 us (28%)
  waiting for transfers between devices  19.1 us (11%)
  local copies, waits for them, and re-layouts  15 us (8%)
  between operations  11 us (6%)
  Pallas kernels  10.7 us (6%)
  matrix products  9.67 us (5%)
  other arithmetic  8.42 us (5%)
    ppermute x15, starting transfers between devices, shift(): return lax.ppermute(array, axis, [(n, send_to(n)) for n in range(size)])  29.6 us
    all_gather x1, blocking collectives, shards(): val_waves = lax.all_gather(quarter_waves[:, :16], 'cp', axis=0)  26.8 us
    all_gather x1, blocking collectives, shards(): cond_waves = lax.all_gather(quarter_waves[:, 16:], 'cp', axis=0)  15.5 us
    all_gather x1, blocking collectives, shards(): columns = lax.all_gather(waves, 'vp', axis=0)  12.1 us
    all_to_all x1, waiting for transfers between devices, shards(): lax.all_to_all(tiles, ('vp', 'ga'), split_axis=0, concat_axis=0, tiled=True)  11.7 us
    all_to_all x1, starting transfers between devices, shards(): lax.all_to_all(tiles, ('vp', 'ga'), split_axis=0, concat_axis=0, tiled=True)  9.1 us
    dot_general x3, matrix products, project(): lax.dot_general(basis, flat, (((0,), (1,)), ((), ())), preferred_element_...  7.6 us
    pallas_call x1, Pallas kernels, kernel_tiles(): pl.pallas_call(direct_kernel, out_shape=jax.ShapeDtypeStruct((slots, 16,...  7.53 us
  transfers between devices with their start and end apart: 18, of which 4 were waited for; matrix products, arithmetic and copies ran while one was open for 15% of the time, Pallas kernels for 0%

profile of v1, /device:TPU:1, one launch (start us, length us, event | category | flops | bytes accessed | tf_op | source)
XLA Modules:
  0.0 177.7 jit_solution(1656030456926215012)
XLA Ops:
  0.0 3.3 %collective-permute-start.2 = (s32[6]{0:T(128)}, s32[6]{0:T(128)S(1)}, u32[]{:S(2)}, u32[]{:S(2)}) collective-permute-start(s32[6]{0:T(128)} %param.13), channel_id=1, source_target_pairs={{0,192},{64,0},{128,64},{192,128},{1,193},{65,1},{129,65},{193,129... | collective-permute-start | bytes 80 | tf_op jit(solution)/shard_map/ppermute | solution.py:19
  3.8 0.7 and_select_fusion.1
  4.5 0.7 fusion.48
  15.7 1.0 pad_maximum_fusion.1
  16.7 12.1 %all-gather = bf16[128,3072]{1,0:T(8,128)(2,1)S(1)} all-gather(bf16[32,3072]{1,0:T(8,128)(2,1)S(1)} %pad_maximum_fusion.1), channel_id=2, replica_groups=mesh['vp'=4,'cp'=8,'ga'=8] {'vp'}, dimensions={0}, use_global_device_ids=true | all-gather | bytes 983040 | tf_op jit(solution)/shard_map/all_gather | solution.py:185
  28.8 3.5 %collective-permute-start.3 = (bf16[32,1536]{1,0:T(8,128)(2,1)S(1)}, bf16[32,1536]{1,0:T(8,128)(2,1)S(1)}, u32[]{:S(2)}, u32[]{:S(2)}) collective-permute-start(bf16[32,1536]{1,0:T(8,128)(2,1)S(1)} %broadcast_select_fusion), channel_id=1, source_target_pairs={{0,8},{8,0},{16,24},{24,16},{32,40},{40,32},{48,56},{56,48},{1,9},... | collective-permute-start | bytes 294920 | tf_op jit(solution)/shard_map/ppermute | solution.py:19
  32.4 0.7 constant_dynamic-slice_fusion
  33.3 6.2 %collective-permute-start.6 = (bf16[32,1536]{1,0:T(8,128)(2,1)S(1)}, bf16[32,1536]{1,0:T(8,128)(2,1)S(1)}, u32[]{:S(2)}, u32[]{:S(2)}) collective-permute-start(bf16[32,1536]{1,0:T(8,128)(2,1)S(1)} %select_add_fusion), channel_id=1, source_target_pairs={{0,48},{8,56},{16,0},{24,8},{32,16},{40,24},{48,32},{56,40},{1,49}... | collective-permute-start | bytes 294920 | tf_op jit(solution)/shard_map/ppermute | solution.py:19
  39.6 1.0 collective-permute-start.5
  40.6 2.3 %collective-permute-start.4 = (bf16[32,1536]{1,0:T(8,128)(2,1)S(1)}, bf16[32,1536]{1,0:T(8,128)(2,1)S(1)}, u32[]{:S(2)}, u32[]{:S(2)}) collective-permute-start(bf16[32,1536]{1,0:T(8,128)(2,1)S(1)} %select_add_fusion), channel_id=1, source_target_pairs={{0,16},{8,24},{16,32},{24,40},{32,48},{40,56},{48,0},{56,8},{1,17}... | collective-permute-start | bytes 294920 | tf_op jit(solution)/shard_map/ppermute | solution.py:19
  42.8 4.8 %collective-permute-done.6 = bf16[32,1536]{1,0:T(8,128)(2,1)S(1)} collective-permute-done((bf16[32,1536]{1,0:T(8,128)(2,1)S(1)}, bf16[32,1536]{1,0:T(8,128)(2,1)S(1)}, u32[]{:S(2)}, u32[]{:S(2)}) %collective-permute-start.6) | collective-permute-done | bytes 98336 | tf_op jit(solution)/shard_map/ppermute | solution.py:19
  47.6 1.6 collective-permute-done.5
  49.3 3.4 %collective-permute-start.7 = (bf16[32,1536]{1,0:T(8,128)(2,1)S(1)}, bf16[32,1536]{1,0:T(8,128)(2,1)S(1)}, u32[]{:S(2)}, u32[]{:S(2)}) collective-permute-start(bf16[32,1536]{1,0:T(8,128)(2,1)S(1)} %add_add_fusion), channel_id=1, source_target_pairs={{0,8},{8,0},{16,24},{24,16},{32,40},{40,32},{48,56},{56,48},{1,9},... | collective-permute-start | bytes 294920 | tf_op jit(solution)/shard_map/ppermute | solution.py:19
  52.7 0.9 collective-permute-done.7
  54.0 3.8 %fusion.15 = bf16[1024,128]{0,1:T(8,128)(2,1)S(1)} fusion(bf16[128,3072]{1,0:T(8,128)(2,1)S(1)} %bitcast.96, bf16[3072,1024]{1,0:T(8,128)(2,1)} %param.9), kind=kOutput, calls=%fused_computation.17 | convolution fusion | flops 805437440 | bytes 7340032 | tf_op jit(solution)/shard_map/dot_general | solution.py:202
  58.1 1.2 multiply_convert_fusion.1
  59.4 1.7 multiply_convert_fusion
  61.1 1.9 %fusion.9 = bf16[256,1024]{1,0:T(8,128)(2,1)S(1)} fusion(bf16[1024,3072]{1,0:T(8,128)(2,1)S(1)} %bitcast.92, bf16[3072,1024]{1,0:T(8,128)(2,1)S(1)} %bitcast.90, s32[]{:T(128)S(6)} %select_n.302), kind=kOutput, calls=%fused_computation.14 | convolution fusion | flops 1610874880 | bytes 8388612 | tf_op jit(solution)/shard_map/dot_general | solution.py:202
  63.0 1.9 %fusion.6 = bf16[256,1024]{1,0:T(8,128)(2,1)S(1)} fusion(bf16[1024,3072]{1,0:T(8,128)(2,1)S(1)} %bitcast.91, bf16[3072,1024]{1,0:T(8,128)(2,1)S(1)} %bitcast.90, s32[]{:T(128)S(6)} %select_n.302), kind=kOutput, calls=%fused_computation.13 | convolution fusion | flops 1610874880 | bytes 8388612 | tf_op jit(solution)/shard_map/dot_general | solution.py:202
  64.9 1.2 pad_maximum_fusion
  66.1 4.2 %all-to-all-start = ((bf16[8,32,2560]{2,1,0:T(8,128)(2,1)}), bf16[8,32,2560]{2,1,0:T(8,128)(2,1)S(1)}, u32[]{:S(2)}, u32[]{:S(2)}) async-start(bf16[8,32,2560]{2,1,0:T(8,128)(2,1)} %pad_maximum_fusion), calls=%async_computation | async-start | bytes 2621440 | tf_op jit(solution)/shard_map/all_to_all | solution.py:221
  70.3 0.8 dynamic_slice.34
  71.2 0.8 dynamic_slice.33
  73.6 26.8 %all-gather.1.val_ref = bf16[32,16,768]{2,1,0:T(8,128)(2,1)S(1)} all-gather(bf16[4,16,768]{2,1,0:T(8,128)(2,1)S(1)} %get-tuple-element.20), channel_id=3, replica_groups=mesh['vp'=4,'cp'=8,'ga'=8] {'cp'}, dimensions={0}, use_global_device_ids=true | all-gather | bytes 884736 | tf_op jit(solution)/shard_map/all_gather | solution.py:191
  100.4 15.5 %all-gather.2.cond_ref = bf16[32,16,768]{2,1,0:T(8,128)(2,1)S(1)} all-gather(bf16[4,16,768]{2,1,0:T(8,128)(2,1)S(1)} %get-tuple-element.19), channel_id=4, replica_groups=mesh['vp'=4,'cp'=8,'ga'=8] {'cp'}, dimensions={0}, use_global_device_ids=true | all-gather | bytes 884736 | tf_op jit(solution)/shard_map/all_gather | solution.py:192
  116.5 3.1 %collective-permute-start.11 = (bf16[2,32,1024]{2,1,0:T(8,128)(2,1)S(1)}, bf16[2,32,1024]{2,1,0:T(8,128)(2,1)S(1)}, u32[]{:S(2)}, u32[]{:S(2)}) collective-permute-start(bf16[2,32,1024]{2,1,0:T(8,128)(2,1)S(1)} %pad_maximum_fusion.3), channel_id=1, source_target_pairs={{0,32},{8,40},{16,48},{24,56},{32,0},{40,8},{48,16},{56,24},{1,33}... | collective-permute-start | bytes 393224 | tf_op jit(solution)/shard_map/ppermute | solution.py:19
  119.7 2.5 %collective-permute-start.13 = (bf16[2,32,1024]{2,1,0:T(8,128)(2,1)S(1)}, bf16[2,32,1024]{2,1,0:T(8,128)(2,1)S(1)}, u32[]{:S(2)}, u32[]{:S(2)}) collective-permute-start(bf16[2,32,1024]{2,1,0:T(8,128)(2,1)S(1)} %pad_maximum_fusion.3), channel_id=1, source_target_pairs={{0,48},{8,56},{16,0},{24,8},{32,16},{40,24},{48,32},{56,40},{1,49}... | collective-permute-start | bytes 393224 | tf_op jit(solution)/shard_map/ppermute | solution.py:19
  122.2 0.7 broadcast_in_dim.57
  123.0 6.5 %all-to-all-start.1 = ((bf16[8,32,512]{2,1,0:T(8,128)(2,1)}), bf16[8,32,512]{2,1,0:T(8,128)(2,1)S(1)}, u32[]{:S(2)}, u32[]{:S(2)}) async-start(bf16[8,32,512]{2,1,0:T(8,128)(2,1)} %broadcast_in_dim.57), calls=%async_computation.1 | async-start | bytes 524288 | tf_op jit(solution)/shard_map/all_to_all | solution.py:236
  129.4 0.7 bitcast_dynamic-update-slice_fusion.7
  130.1 1.5 collective-permute-start.10
  131.7 1.9 %collective-permute-start.14 = (bf16[2,32,1024]{2,1,0:T(8,128)(2,1)S(1)}, bf16[2,32,1024]{2,1,0:T(8,128)(2,1)S(1)}, u32[]{:S(2)}, u32[]{:S(2)}) collective-permute-start(bf16[2,32,1024]{2,1,0:T(8,128)(2,1)S(1)} %collective-permute-done.13), channel_id=1, source_target_pairs={{0,8},{8,0},{16,24},{24,16},{32,40},{40,32},{48,56},{56,48},{1,9},... | collective-permute-start | bytes 393224 | tf_op jit(solution)/shard_map/ppermute | solution.py:19
  133.5 0.7 bitcast_dynamic-update-slice_fusion.6
  134.2 0.7 bitcast_dynamic-update-slice_fusion.5
  134.9 0.7 bitcast_dynamic-update-slice_fusion.4
  135.5 0.7 bitcast_dynamic-update-slice_fusion.3
  136.2 0.7 bitcast_dynamic-update-slice_fusion.2
  136.8 0.7 bitcast_dynamic-update-slice_fusion.1
  137.5 0.7 bitcast_dynamic-update-slice_fusion
  138.2 1.8 %gather_fusion.1 = bf16[8,2,32,1024]{3,2,1,0:T(8,128)(2,1)S(1)} fusion(bf16[8,2,32,1024]{3,2,1,0:T(8,128)(2,1)} %bitcast_dynamic-update-slice_fusion, s32[1024]{0:T(1024)S(1)} %pad_clamp_fusion), kind=kCustom, calls=%fused_computation.1 | custom fusion | bytes 2097184 | tf_op jit(solution)/shard_map/jit(_take)/gather | solution.py:256
  140.3 0.8 reshape.293
  141.1 1.0 copy.39
  142.1 2.1 %fusion.12.w_ref = bf16[128,768]{1,0:T(8,128)(2,1)S(1)} fusion(bf16[1024,128]{1,0:T(8,128)(2,1)S(1)} %bitcast.101, bf16[3072,1024]{1,0:T(8,128)(2,1)} %param.9, s32[]{:T(128)S(6)} %select_n.303), kind=kOutput, calls=%fused_computation.16 | convolution fusion | flops 201424896 | bytes 2031620 | tf_op jit(solution)/shard_map/dot_general | solution.py:242
  144.1 3.2 %shard_map.73.exchange_ref = f32[24,16,512]{2,1,0:T(8,128)S(1)} custom-call(s32[24]{0:T(128)S(1)} %select_n.296.ids_ref, bf16[32,16,768]{2,1,0:T(8,128)(2,1)S(1)} %all-gather.1.val_ref, bf16[32,16,768]{2,1,0:T(8,128)(2,1)S(1)} %all-gather.2.cond_ref, bf16[128,768]{1,0:T(8,128)(2,1)S(1)} %fusion.12.w_ref), custom_call_target="tpu_custom_call" | custom-call | flops 301989888 | bytes 4194304 | tf_op jit(solution)/shard_map/pallas_call | solution.py:93
  147.4 7.5 %shard_map.74 = bf16[24,16,512]{2,1,0:T(8,128)(2,1)S(1)} custom-call(s32[24]{0:T(128)S(1)} %select_n.296.ids_ref, bf16[8,32,1024]{2,1,0:T(8,128)(2,1)S(1)} %get-tuple-element.12.val_ref, bf16[8,32,1024]{2,1,0:T(8,128)(2,1)S(1)} %get-tuple-element.11.cond_ref, bf16[512,512]{1,0:T(8,128)(2,1)S(1)} %fusion.16.order_ref, f32[24,16,512]{2,1,0:T(8,128)S(1)} %shard_map.73.exchange_ref), custom_call_target="tpu_custom_call" | custom-call | tf_op jit(solution)/shard_map/pallas_call | solution.py:151
  154.9 1.0 copy.41
  156.0 9.1 %all-to-all-start.2 = ((bf16[32,12,512]{2,1,0:T(8,128)(2,1)}), bf16[32,12,512]{2,1,0:T(8,128)(2,1)S(1)}, u32[]{:S(2)}, u32[]{:S(2)}) async-start(bf16[32,12,512]{2,1,0:T(8,128)(2,1)} %copy.41), calls=%async_computation.2 | async-start | bytes 1048576 | tf_op jit(solution)/shard_map/all_to_all | solution.py:264
  165.2 11.7 %all-to-all-done.2 = bf16[32,12,512]{2,1,0:T(8,128)(2,1)S(1)} async-done(((bf16[32,12,512]{2,1,0:T(8,128)(2,1)}), bf16[32,12,512]{2,1,0:T(8,128)(2,1)S(1)}, u32[]{:S(2)}, u32[]{:S(2)}) %all-to-all-start.2) | async-done | bytes 393248 | tf_op jit(solution)/shard_map/all_to_all | solution.py:264
  (75 shorter events, 5.2 us)
Async XLA Ops:
  0.0 47.6 %copy-start.1 = (s32[6]{0:T(128)S(1)}, s32[6]{0:T(128)}, u32[]{:S(2)}) copy-start(s32[6]{0:T(128)} %param.13) | copy-start | bytes 76
  0.0 72.8 %collective-permute-start.2 = (s32[6]{0:T(128)}, s32[6]{0:T(128)S(1)}, u32[]{:S(2)}, u32[]{:S(2)}) collective-permute-start(s32[6]{0:T(128)} %param.13), channel_id=1, source_target_pairs={{0,192},{64,0},{128,64},{192,128},{1,193},{65,1},{129,65},{193,129... | collective-permute-start | bytes 80 | tf_op jit(solution)/shard_map/ppermute | solution.py:19
  3.3 69.5 %collective-permute-start.1 = (s32[6]{0:T(128)}, s32[6]{0:T(128)S(1)}, u32[]{:S(2)}, u32[]{:S(2)}) collective-permute-start(s32[6]{0:T(128)} %param.13), channel_id=1, source_target_pairs={{0,128},{64,192},{128,0},{192,64},{1,129},{65,193},{129,1},{193,65... | collective-permute-start | bytes 80 | tf_op jit(solution)/shard_map/ppermute | solution.py:19
  28.8 4.4 %collective-permute-start.3 = (bf16[32,1536]{1,0:T(8,128)(2,1)S(1)}, bf16[32,1536]{1,0:T(8,128)(2,1)S(1)}, u32[]{:S(2)}, u32[]{:S(2)}) collective-permute-start(bf16[32,1536]{1,0:T(8,128)(2,1)S(1)} %broadcast_select_fusion), channel_id=1, source_target_pairs={{0,8},{8,0},{16,24},{24,16},{32,40},{40,32},{48,56},{56,48},{1,9},... | collective-permute-start | bytes 294920 | tf_op jit(solution)/shard_map/ppermute | solution.py:19
  33.3 14.3 %collective-permute-start.6 = (bf16[32,1536]{1,0:T(8,128)(2,1)S(1)}, bf16[32,1536]{1,0:T(8,128)(2,1)S(1)}, u32[]{:S(2)}, u32[]{:S(2)}) collective-permute-start(bf16[32,1536]{1,0:T(8,128)(2,1)S(1)} %select_add_fusion), channel_id=1, source_target_pairs={{0,48},{8,56},{16,0},{24,8},{32,16},{40,24},{48,32},{56,40},{1,49}... | collective-permute-start | bytes 294920 | tf_op jit(solution)/shard_map/ppermute | solution.py:19
  39.6 9.7 %collective-permute-start.5 = (bf16[32,1536]{1,0:T(8,128)(2,1)S(1)}, bf16[32,1536]{1,0:T(8,128)(2,1)S(1)}, u32[]{:S(2)}, u32[]{:S(2)}) collective-permute-start(bf16[32,1536]{1,0:T(8,128)(2,1)S(1)} %select_add_fusion), channel_id=1, source_target_pairs={{0,32},{8,40},{16,48},{24,56},{32,0},{40,8},{48,16},{56,24},{1,33}... | collective-permute-start | bytes 294920 | tf_op jit(solution)/shard_map/ppermute | solution.py:19
  40.6 8.7 %collective-permute-start.4 = (bf16[32,1536]{1,0:T(8,128)(2,1)S(1)}, bf16[32,1536]{1,0:T(8,128)(2,1)S(1)}, u32[]{:S(2)}, u32[]{:S(2)}) collective-permute-start(bf16[32,1536]{1,0:T(8,128)(2,1)S(1)} %select_add_fusion), channel_id=1, source_target_pairs={{0,16},{8,24},{16,32},{24,40},{32,48},{40,56},{48,0},{56,8},{1,17}... | collective-permute-start | bytes 294920 | tf_op jit(solution)/shard_map/ppermute | solution.py:19
  47.6 25.1 %collective-permute-start = (s32[6]{0:T(128)S(1)}, s32[6]{0:T(128)S(1)}, u32[]{:S(2)}, u32[]{:S(2)}) collective-permute-start(s32[6]{0:T(128)S(1)} %copy-done.1), channel_id=1, source_target_pairs={{0,64},{64,128},{128,192},{192,0},{1,65},{65,129},{129,193},{193,1... | collective-permute-start | bytes 80 | tf_op jit(solution)/shard_map/ppermute | solution.py:19
  49.3 4.4 %collective-permute-start.7 = (bf16[32,1536]{1,0:T(8,128)(2,1)S(1)}, bf16[32,1536]{1,0:T(8,128)(2,1)S(1)}, u32[]{:S(2)}, u32[]{:S(2)}) collective-permute-start(bf16[32,1536]{1,0:T(8,128)(2,1)S(1)} %add_add_fusion), channel_id=1, source_target_pairs={{0,8},{8,0},{16,24},{24,16},{32,40},{40,32},{48,56},{56,48},{1,9},... | collective-permute-start | bytes 294920 | tf_op jit(solution)/shard_map/ppermute | solution.py:19
  58.0 3.0 %slice-start = ((s8[6291456]{0:T(1024)(128)(4,1)}), s8[4194304]{0:T(1024)(128)(4,1)S(1)}, s32[]{:S(2)}) async-start(s8[6291456]{0:T(1024)(128)(4,1)} %bitcast.89), calls=%async_computation.3 | async-start | bytes 8388608
  58.1 2.9 %slice-start.1 = ((s8[6291456]{0:T(1024)(128)(4,1)}), s8[2097152]{0:T(1024)(128)(4,1)S(1)}, s32[]{:S(2)}) async-start(s8[6291456]{0:T(1024)(128)(4,1)} %bitcast.89), calls=%async_computation.4 | async-start | bytes 4194304
  63.0 10.6 %copy-start = (bf16[4,32,768]{2,1,0:T(8,128)(2,1)S(1)}, bf16[4,32,768]{2,1,0:T(8,128)(2,1)}, u32[]{:S(2)}) copy-start(bf16[4,32,768]{2,1,0:T(8,128)(2,1)} %constant_dynamic-slice_fusion) | copy-start | bytes 589828
  66.1 49.8 %all-to-all-start = ((bf16[8,32,2560]{2,1,0:T(8,128)(2,1)}), bf16[8,32,2560]{2,1,0:T(8,128)(2,1)S(1)}, u32[]{:S(2)}, u32[]{:S(2)}) async-start(bf16[8,32,2560]{2,1,0:T(8,128)(2,1)} %pad_maximum_fusion), calls=%async_computation | async-start | bytes 2621440 | tf_op jit(solution)/shard_map/all_to_all | solution.py:221
  116.2 17.4 %collective-permute-start.8 = (bf16[2,32,1024]{2,1,0:T(8,128)(2,1)S(1)}, bf16[2,32,1024]{2,1,0:T(8,128)(2,1)S(1)}, u32[]{:S(2)}, u32[]{:S(2)}) collective-permute-start(bf16[2,32,1024]{2,1,0:T(8,128)(2,1)S(1)} %pad_maximum_fusion.3), channel_id=1, source_target_pairs={{0,8},{8,0},{16,24},{24,16},{32,40},{40,32},{48,56},{56,48},{1,9},... | collective-permute-start | bytes 393224 | tf_op jit(solution)/shard_map/ppermute | solution.py:19
  116.4 13.7 %collective-permute-start.9 = (bf16[2,32,1024]{2,1,0:T(8,128)(2,1)S(1)}, bf16[2,32,1024]{2,1,0:T(8,128)(2,1)S(1)}, u32[]{:S(2)}, u32[]{:S(2)}) collective-permute-start(bf16[2,32,1024]{2,1,0:T(8,128)(2,1)S(1)} %pad_maximum_fusion.3), channel_id=1, source_target_pairs={{0,16},{8,24},{16,32},{24,40},{32,48},{40,56},{48,0},{56,8},{1,17}... | collective-permute-start | bytes 393224 | tf_op jit(solution)/shard_map/ppermute | solution.py:19
  116.5 15.1 %collective-permute-start.11 = (bf16[2,32,1024]{2,1,0:T(8,128)(2,1)S(1)}, bf16[2,32,1024]{2,1,0:T(8,128)(2,1)S(1)}, u32[]{:S(2)}, u32[]{:S(2)}) collective-permute-start(bf16[2,32,1024]{2,1,0:T(8,128)(2,1)S(1)} %pad_maximum_fusion.3), channel_id=1, source_target_pairs={{0,32},{8,40},{16,48},{24,56},{32,0},{40,8},{48,16},{56,24},{1,33}... | collective-permute-start | bytes 393224 | tf_op jit(solution)/shard_map/ppermute | solution.py:19
  119.7 12.0 %collective-permute-start.13 = (bf16[2,32,1024]{2,1,0:T(8,128)(2,1)S(1)}, bf16[2,32,1024]{2,1,0:T(8,128)(2,1)S(1)}, u32[]{:S(2)}, u32[]{:S(2)}) collective-permute-start(bf16[2,32,1024]{2,1,0:T(8,128)(2,1)S(1)} %pad_maximum_fusion.3), channel_id=1, source_target_pairs={{0,48},{8,56},{16,0},{24,8},{32,16},{40,24},{48,32},{56,40},{1,49}... | collective-permute-start | bytes 393224 | tf_op jit(solution)/shard_map/ppermute | solution.py:19
  123.0 17.3 %all-to-all-start.1 = ((bf16[8,32,512]{2,1,0:T(8,128)(2,1)}), bf16[8,32,512]{2,1,0:T(8,128)(2,1)S(1)}, u32[]{:S(2)}, u32[]{:S(2)}) async-start(bf16[8,32,512]{2,1,0:T(8,128)(2,1)} %broadcast_in_dim.57), calls=%async_computation.1 | async-start | bytes 524288 | tf_op jit(solution)/shard_map/all_to_all | solution.py:236
  130.1 4.8 %collective-permute-start.10 = (bf16[2,32,1024]{2,1,0:T(8,128)(2,1)S(1)}, bf16[2,32,1024]{2,1,0:T(8,128)(2,1)S(1)}, u32[]{:S(2)}, u32[]{:S(2)}) collective-permute-start(bf16[2,32,1024]{2,1,0:T(8,128)(2,1)S(1)} %collective-permute-done.9), channel_id=1, source_target_pairs={{0,8},{8,0},{16,24},{24,16},{32,40},{40,32},{48,56},{56,48},{1,9},... | collective-permute-start | bytes 393224 | tf_op jit(solution)/shard_map/ppermute | solution.py:19
  131.6 4.6 %collective-permute-start.12 = (bf16[2,32,1024]{2,1,0:T(8,128)(2,1)S(1)}, bf16[2,32,1024]{2,1,0:T(8,128)(2,1)S(1)}, u32[]{:S(2)}, u32[]{:S(2)}) collective-permute-start(bf16[2,32,1024]{2,1,0:T(8,128)(2,1)S(1)} %collective-permute-done.11), channel_id=1, source_target_pairs={{0,8},{8,0},{16,24},{24,16},{32,40},{40,32},{48,56},{56,48},{1,9},... | collective-permute-start | bytes 393224 | tf_op jit(solution)/shard_map/ppermute | solution.py:19
  131.7 5.8 %collective-permute-start.14 = (bf16[2,32,1024]{2,1,0:T(8,128)(2,1)S(1)}, bf16[2,32,1024]{2,1,0:T(8,128)(2,1)S(1)}, u32[]{:S(2)}, u32[]{:S(2)}) collective-permute-start(bf16[2,32,1024]{2,1,0:T(8,128)(2,1)S(1)} %collective-permute-done.13), channel_id=1, source_target_pairs={{0,8},{8,0},{16,24},{24,16},{32,40},{40,32},{48,56},{56,48},{1,9},... | collective-permute-start | bytes 393224 | tf_op jit(solution)/shard_map/ppermute | solution.py:19
  140.2 24.9 %copy-start.2 = (s32[2]{0:T(128)S(1)}, s32[2]{0:T(128)}, u32[]{:S(2)}) copy-start(s32[2]{0:T(128)} %param.12) | copy-start | bytes 28
  156.0 20.9 %all-to-all-start.2 = ((bf16[32,12,512]{2,1,0:T(8,128)(2,1)}), bf16[32,12,512]{2,1,0:T(8,128)(2,1)S(1)}, u32[]{:S(2)}, u32[]{:S(2)}) async-start(bf16[32,12,512]{2,1,0:T(8,128)(2,1)} %copy.41), calls=%async_computation.2 | async-start | bytes 1048576 | tf_op jit(solution)/shard_map/all_to_all | solution.py:264

commit v2 on v1

v2 whole, which is shorter than its diff:
```python
import functools
import jax
import jax.numpy as jnp
from jax import lax
from jax.experimental import pallas as pl
from jax.experimental.pallas import tpu as pltpu
from jax.sharding import PartitionSpec as P

R = 1024
TV = 8
TC = 8
NCT = 64
F32 = jnp.float32
BF16 = jnp.bfloat16


def shift(array, axis, send_to):
    size = lax.axis_size(axis)
    return lax.ppermute(array, axis, [(n, send_to(n)) for n in range(size)])


def bands_of(tile):
    device = tile // 2
    return device // 8, device % 8, tile % 2


def pick_kernel(meta_ref, window_ref, columns_ref, mine_ref, other_ref):
    i, j = meta_ref[0], meta_ref[1]
    width = 2 * mine_ref.shape[1]
    first_lane = pl.multiple_of(i * width, 128)
    picked = []
    for first in (0, 16):
        for q in range(2):
            block = window_ref[q]
            at, column, half = bands_of(block // NCT if first == 0 else block % NCT)
            both = columns_ref[at, first : first + 16, pl.ds(first_lane, width)].astype(F32)
            rows = jnp.where(half == 0, both[:8], both[8:])
            picked.append(jnp.where(column == j, rows, jnp.zeros_like(rows)))
    rows = jnp.concatenate(picked, axis=0)
    low, high = rows[:, : width // 2], rows[:, width // 2 :]
    mine_ref[...] = jnp.where(j % 2 == 0, low, high).astype(BF16)
    other_ref[...] = jnp.where(j % 2 == 0, high, low).astype(BF16)


def place_kernel(meta_ref, *refs):
    i, j = meta_ref[0], meta_ref[1]
    out_ref = refs[-1]
    width = refs[0].shape[1]
    for n in range(4):
        start = ((i + 4 - n) % 4) * 2
        for flip in range(2):
            first = pl.multiple_of((start + (j + flip) % 2) * width, 128)
            out_ref[:, pl.ds(first, width)] = refs[4 * flip + n][...]


def row_tiles(meta, window_rows, columns):
    width = columns.shape[2] // 8
    smem, vmem = (pl.BlockSpec(memory_space=m) for m in (pltpu.SMEM, pltpu.VMEM))
    part = jax.ShapeDtypeStruct((32, width), BF16)
    mine, other = pl.pallas_call(
        pick_kernel,
        out_shape=(part, part),
        in_specs=[smem, smem, vmem],
        out_specs=(vmem, vmem),
        compiler_params=pltpu.CompilerParams(vmem_limit_bytes=16 * 2**20),
    )(meta, window_rows, columns)
    mine = mine + shift(other, "cp", lambda n: n ^ 1)
    parts = [shift(mine, "cp", lambda n, s=s: (n + 2 * s) % 8) for s in (1, 2, 3)]
    mine = mine + parts[0] + parts[1] + parts[2]
    mine = [mine] + [shift(mine, "vp", lambda n, s=s: (n + s) % 4) for s in (1, 2, 3)]
    other = [shift(a, "cp", lambda n: n ^ 1) for a in mine]
    return pl.pallas_call(
        place_kernel,
        out_shape=jax.ShapeDtypeStruct((32, columns.shape[2]), BF16),
        in_specs=[smem] + [vmem] * 8,
        out_specs=vmem,
        compiler_params=pltpu.CompilerParams(vmem_limit_bytes=16 * 2**20),
    )(meta, *mine, *other)


def pair_block(left, right):
    product = left.astype(F32)[:, None, :] * right.astype(F32)[None, :, :]
    return product.reshape(-1, left.shape[1])


def owner_of(ids_ref, i, slot):
    own = ids_ref.shape[1]
    return ids_ref[(i + 4 - slot // own) % 4, slot % own]


def exchange_kernel(meta_ref, ids_ref, waves_ref, basis_ref, *refs):
    pieces, out_ref = refs[:8], refs[8]
    i, k = meta_ref[0], meta_ref[2]
    together = 4
    potential = None
    for flip in range(2):
        for n in range(4):
            source = ((k // 2 + 4 - n) % 4) * 2 + (k + flip) % 2
            piece = pieces[4 * flip + n][...]
            ranks = jnp.concatenate(
                [piece[:, m * 128 : (m + 1) * 128] for m in range(4)], axis=0
            )
            basis = basis_ref[:, pl.ds(pl.multiple_of(source * 128, 128), 128)]
            term = lax.dot_general(
                ranks, basis, (((0,), (1,)), ((), ())), preferred_element_type=F32
            )
            potential = term if potential is None else potential + term
    potential = potential.astype(BF16)

    def band_rows(first, tile):
        at, column, half = bands_of(tile)
        both = waves_ref[column * 4 + at, first : first + 16].astype(F32)
        return jnp.where(half == 0, both[:8], both[8:])

    for step in range(out_ref.shape[0] // together):
        pairs = []
        for n in range(together):
            owner = owner_of(ids_ref, i, step * together + n)
            left = band_rows(0, owner // NCT)
            right = band_rows(16, owner % NCT)
            pairs.append(pair_block(left, right).astype(BF16))
        pair = jnp.concatenate(pairs, axis=0)
        result = lax.dot_general(
            potential, pair, (((1,), (1,)), ((), ())), preferred_element_type=F32
        )
        for n in range(together):
            tile = result[:, n * 64 : (n + 1) * 64]
            out_ref[step * together + n] = jnp.concatenate(
                [tile[c * 16 : (c + 1) * 16] for c in range(8)], axis=1
            )


def exchange_tiles(meta, ids, waves, basis_rows, pieces):
    slots = 4 * ids.shape[1]
    smem, vmem = (pl.BlockSpec(memory_space=m) for m in (pltpu.SMEM, pltpu.VMEM))
    return pl.pallas_call(
        exchange_kernel,
        out_shape=jax.ShapeDtypeStruct((slots, 16, 512), F32),
        in_specs=[smem, smem, vmem, vmem] + [vmem] * 8,
        out_specs=vmem,
        compiler_params=pltpu.CompilerParams(vmem_limit_bytes=32 * 2**20),
        cost_estimate=pl.CostEstimate(
            flops=2 * slots * 64 * 128 * 768, bytes_accessed=2**22, transcendentals=0
        ),
    )(meta, ids, waves, basis_rows, *pieces)


def direct_kernel(meta_ref, ids_ref, order_ref, exchange_ref, *refs):
    pieces, (out_ref, proj_ref, held_ref, total_ref) = refs[:8], refs[8:]
    i, j = meta_ref[0], meta_ref[1]
    own = ids_ref.shape[1]
    slots = 4 * own
    lane = lax.broadcasted_iota(jnp.int32, (8, 128), 1)
    for flip in range(2):
        for n in range(4):
            source = ((j // 2 + 4 - n) % 4) * 2 + (j + flip) % 2
            proj_ref[source] = pieces[4 * flip + n][...]

    def lanes_of(part, tile):
        at, column, half = bands_of(tile)
        first = pl.multiple_of((at * 2 + half) * 128, 128)
        return proj_ref[column, part, :, pl.ds(first, 128)]

    for slot in range(slots):
        owner = owner_of(ids_ref, i, slot)
        left = lanes_of(0, owner // NCT)
        right = lanes_of(1, owner % NCT)
        tile = lax.dot_general(
            left, right, (((0,), (0,)), ((), ())), preferred_element_type=F32
        )
        rows = []
        for q in range(2):
            blocks = []
            for m in range(4):
                even = tile[q * 64 + m * 16 : q * 64 + m * 16 + 8]
                odd = tile[q * 64 + m * 16 + 8 : q * 64 + m * 16 + 16]
                if q == 0:
                    odd = pltpu.roll(odd, 64, 1)
                else:
                    even = pltpu.roll(even, 64, 1)
                blocks.append(jnp.where(lane < 64, even, odd))
            rows.append(jnp.concatenate(blocks, axis=1))
        held_ref[slot] = jnp.concatenate(rows, axis=0).astype(BF16)
    for part in range(4):
        direct = jnp.dot(
            held_ref[part * own : (part + 1) * own].reshape(own * 16, 512),
            order_ref[...],
            preferred_element_type=F32,
        ).reshape(own, 16, 512)
        total = 2.0 * exchange_ref[part * own : (part + 1) * own] - direct
        for n in range(own):
            for q in range(2):
                total_ref[part * 8 : (part + 1) * 8, q * own + n, :] = total[
                    n, q * 8 : (q + 1) * 8
                ]
    out_ref[...] = total_ref[...].astype(BF16)


def kernel_tiles(meta, ids, order, exchange, pieces):
    own = ids.shape[1]
    slots = 4 * own
    smem, vmem = (pl.BlockSpec(memory_space=m) for m in (pltpu.SMEM, pltpu.VMEM))
    return pl.pallas_call(
        direct_kernel,
        out_shape=jax.ShapeDtypeStruct((32, 2 * own, 512), BF16),
        in_specs=[smem, smem, vmem, vmem] + [vmem] * 8,
        out_specs=vmem,
        scratch_shapes=[
            pltpu.VMEM((8,) + pieces[0].shape, BF16),
            pltpu.VMEM((slots, 16, 512), BF16),
            pltpu.VMEM((32, 2 * own, 512), F32),
        ],
        compiler_params=pltpu.CompilerParams(vmem_limit_bytes=32 * 2**20),
    )(meta, ids, order, exchange, *pieces)


def gather_pieces(array, axis):
    step = [array] + [
        shift(array, axis, lambda n, s=s: (n + 2 * s) % 8) for s in (1, 2, 3)
    ]
    return step + [shift(a, axis, lambda n: n ^ 1) for a in step]


def shards(valence_wavefunction, cond_wave, screen_basis, screen, coulomb, window_rows, tile_owner):
    i = lax.axis_index("vp")
    j = lax.axis_index("cp")
    k = lax.axis_index("ga")
    meta = jnp.stack([i, j, k]).astype(jnp.int32)
    own_slots = tile_owner.shape[0]
    grid_count = valence_wavefunction.shape[1]
    quarter = grid_count // 4
    rank_quarter = R // 4
    rank_part = rank_quarter // 8

    ids = jnp.stack(
        [tile_owner] + [shift(tile_owner, "vp", lambda n, s=s: (n + s) % 4) for s in (1, 2, 3)]
    )
    waves = jnp.concatenate([valence_wavefunction, cond_wave], axis=0)
    columns = lax.all_gather(waves, "vp", axis=0)
    rows = row_tiles(meta, window_rows, columns)

    quarter_waves = lax.dynamic_slice_in_dim(columns, i * quarter, quarter, 2)
    all_waves = lax.all_gather(quarter_waves, "cp", axis=0)

    row_val = rows[:16].reshape(2, TV, grid_count).astype(F32)
    row_cond = rows[16:].reshape(2, TC, grid_count).astype(F32)
    col_val = columns[:, :16].reshape(8, TV, grid_count).astype(F32)
    col_cond = columns[:, 16:].reshape(8, TC, grid_count).astype(F32)
    basis_ranks = lax.dynamic_slice_in_dim(screen_basis, i * rank_quarter, rank_quarter, 1)

    def project(pairs, basis):
        flat = pairs.astype(BF16).reshape(-1, grid_count)
        return lax.dot_general(
            basis, flat, (((0,), (1,)), ((), ())), preferred_element_type=F32
        ).astype(BF16)

    val_part = project(col_val[:, None, :, None] * row_val[None, :, None, :], basis_ranks)
    cond_part = project(row_cond[None, :, :, None] * col_cond[:, None, None, :], basis_ranks)
    row_part = project(
        jnp.swapaxes(row_cond, 0, 1)[:, :, None] * row_val[None], screen_basis
    )
    row_part = row_part.reshape(8, 4, rank_part, 128)
    row_part = jnp.swapaxes(row_part, 1, 2).reshape(8, rank_part, 512)
    sent = jnp.concatenate(
        [
            val_part.reshape(8, rank_part, 1024),
            cond_part.reshape(8, rank_part, 1024),
            row_part,
        ],
        axis=2,
    )
    arrived = lax.all_to_all(sent, "ga", split_axis=0, concat_axis=0, tiled=True)
    summed = arrived.astype(F32).sum(axis=0)

    screen_part = lax.dynamic_slice_in_dim(
        screen, i * rank_quarter + k * rank_part, rank_part, 0
    )
    coulomb_part = lax.dynamic_slice_in_dim(coulomb, k * (R // 8), R // 8, 0)
    val_sum = (summed[:, :1024] * screen_part[:, None]).astype(BF16)
    cond_sum = summed[:, 1024:2048].astype(BF16)
    row_sum = summed[:, 2048:].reshape(rank_part, 4, 128)
    row_sum = (row_sum * coulomb_part.reshape(4, rank_part).T[:, :, None]).astype(BF16)

    proj_pieces = gather_pieces(jnp.stack([val_sum, cond_sum]), "cp")
    row_pieces = gather_pieces(row_sum.reshape(rank_part, 512), "ga")
    basis_rows = lax.dynamic_slice_in_dim(screen_basis, i * quarter, quarter, 0)
    exchange = exchange_tiles(
        meta, ids, all_waves.reshape(32, 32, quarter), basis_rows, row_pieces
    )

    order = jnp.arange(512, dtype=jnp.int32)
    source = (order // 8 % 8) * 64 + (order // 64) * 8 + order % 8
    order = (order[:, None] == source[None, :]).astype(BF16)
    tiles = kernel_tiles(meta, ids, order, exchange, proj_pieces)
    got = lax.all_to_all(tiles, ("vp", "ga"), split_axis=0, concat_axis=0, tiled=True)
    kernel = got.astype(F32).sum(axis=0).reshape(2, own_slots, 512)
    live_tile = (tile_owner[None, :] >= window_rows[:, None])[:, :, None]
    return jnp.where(live_tile, kernel, jnp.zeros_like(kernel))


def solution(mesh):
    in_specs = (
        P(("vp", "cp"), "ga"),
        P(("vp", "cp"), "ga"),
        P("ga", None),
        P(),
        P(),
        P(),
        P(("vp", "cp")),
    )
    out_specs = P(None, ("vp", "cp"), "ga")
    return jax.shard_map(shards, mesh=mesh, in_specs=in_specs, out_specs=out_specs, check_vma=False)
```

time: 178 us -> 150 us (0.84)
  blocking collectives: 54.4 us -> 12.9 us
  waiting for transfers between devices: 19.1 us -> 39 us
  starting transfers between devices: 49.4 us -> 58.9 us
  local copies, waits for them, and re-layouts: 15 us -> 7.17 us
  matrix products: 9.67 us -> 4.7 us
  Pallas kernels: 10.7 us -> 6.35 us
  between operations: 11 us -> 13.8 us
  other arithmetic: 8.42 us -> 6.09 us
    all_gather x2 -> x0, blocking collectives: 42.3 us -> none  [the longest x1 26.8 us: shards(): val_waves = lax.all_gather(quarter_waves[:, :16], 'cp', axis=0)]
    ppermute x15 -> x28, starting transfers between devices: 29.6 us -> 50.4 us  [shift(): return lax.ppermute(array, axis, [(n, send_to(n)) for n in range(size)])]
    all_to_all x1, waiting for transfers between devices: 0.01 us -> 15.3 us  [shards(): lax.all_to_all(sent, 'ga', split_axis=0, concat_axis=0, tiled=True)]
    all_to_all x1 -> x0, starting transfers between devices: 6.46 us -> none  [shards(): lax.all_to_all(jnp.broadcast_to(row_sum[None], (8, rank_part, 512)), 'ga'...]
    ppermute x15 -> x28, waiting for transfers between devices: 7.36 us -> 13.3 us  [shift(): return lax.ppermute(array, axis, [(n, send_to(n)) for n in range(size)])]
    all_to_all x1, starting transfers between devices: 9.1 us -> 3.89 us  [shards(): lax.all_to_all(tiles, ('vp', 'ga'), split_axis=0, concat_axis=0, tiled=True)]
    pallas_call x1 -> x3, Pallas kernels: 7.53 us -> 3.95 us  [the longest x1 2.76 us: kernel_tiles(): pl.pallas_call(direct_kernel, out_shape=jax.ShapeDtypeStruct((32, 2 * own...]
    dot_general x3, matrix products: 7.6 us -> 4.7 us  [project(): lax.dot_general(basis, flat, (((0,), (1,)), ((), ())), preferred_element_...]
  transfers between devices with their start and end apart: 18 -> 31, of which waited for: 4 -> 9; matrix products, arithmetic and copies ran while one was open for 15% -> 3% of each run, Pallas kernels for 0% -> 2%
where the time goes in v2:
time: 150 us; the launch traced here: 149 us
  starting transfers between devices  58.9 us (39%)
  waiting for transfers between devices  39 us (26%)
  between operations  13.8 us (9%)
  blocking collectives  12.9 us (9%)
  local copies, waits for them, and re-layouts  7.17 us (5%)
  Pallas kernels  6.35 us (4%)
  other arithmetic  6.09 us (4%)
  matrix products  4.7 us (3%)
    ppermute x28, starting transfers between devices, shift(): return lax.ppermute(array, axis, [(n, send_to(n)) for n in range(size)])  50.4 us
    all_to_all x1, waiting for transfers between devices, shards(): lax.all_to_all(sent, 'ga', split_axis=0, concat_axis=0, tiled=True)  15.3 us
    ppermute x28, waiting for transfers between devices, shift(): return lax.ppermute(array, axis, [(n, send_to(n)) for n in range(size)])  13.3 us
    all_gather x1, blocking collectives, shards(): columns = lax.all_gather(waves, 'vp', axis=0)  12.9 us
    all_to_all x1, waiting for transfers between devices, shards(): lax.all_to_all(tiles, ('vp', 'ga'), split_axis=0, concat_axis=0, tiled=True)  10.4 us
    dot_general x3, matrix products, project(): lax.dot_general(basis, flat, (((0,), (1,)), ((), ())), preferred_element_...  4.7 us
    all_to_all x1, starting transfers between devices, shards(): lax.all_to_all(sent, 'ga', split_axis=0, concat_axis=0, tiled=True)  4.64 us
    all_to_all x1, starting transfers between devices, shards(): lax.all_to_all(tiles, ('vp', 'ga'), split_axis=0, concat_axis=0, tiled=True)  3.89 us
  transfers between devices with their start and end apart: 31, of which 9 were waited for; matrix products, arithmetic and copies ran while one was open for 3% of the time, Pallas kernels for 2%

profile of v2, /device:TPU:1, one launch (start us, length us, event | category | flops | bytes accessed | tf_op | source)
XLA Modules:
  0.0 149.0 jit_solution(7711829330407580796)
XLA Ops:
  6.5 1.0 pad_maximum_fusion.1
  7.5 12.9 %all-gather = bf16[128,3072]{1,0:T(8,128)(2,1)S(1)} all-gather(bf16[32,3072]{1,0:T(8,128)(2,1)S(1)} %pad_maximum_fusion.1), channel_id=2, replica_groups=mesh['vp'=4,'cp'=8,'ga'=8] {'vp'}, dimensions={0}, use_global_device_ids=true | all-gather | bytes 983040 | tf_op jit(solution)/shard_map/all_gather | solution.py:239
  20.5 0.7 copy-done.1
  21.2 0.6 shard_map.73
  21.8 4.4 %collective-permute-start.3 = (bf16[32,384]{1,0:T(8,128)(2,1)S(1)}, bf16[32,384]{1,0:T(8,128)(2,1)S(1)}, u32[]{:S(2)}, u32[]{:S(2)}) collective-permute-start(bf16[32,384]{1,0:T(8,128)(2,1)S(1)} %get-tuple-element.8), channel_id=1, source_target_pairs={{0,8},{8,0},{16,24},{24,16},{32,40},{40,32},{48,56},{56,48},{1,9},... | collective-permute-start | bytes 73736 | tf_op jit(solution)/shard_map/ppermute | solution.py:19
  26.1 0.8 collective-permute-done.3
  27.0 1.0 collective-permute-start.4
  28.0 5.1 %collective-permute-start.5 = (bf16[32,384]{1,0:T(8,128)(2,1)S(1)}, bf16[32,384]{1,0:T(8,128)(2,1)S(1)}, u32[]{:S(2)}, u32[]{:S(2)}) collective-permute-start(bf16[32,384]{1,0:T(8,128)(2,1)S(1)} %add.76), channel_id=1, source_target_pairs={{0,32},{8,40},{16,48},{24,56},{32,0},{40,8},{48,16},{56,24},{1,33}... | collective-permute-start | bytes 73736 | tf_op jit(solution)/shard_map/ppermute | solution.py:19
  33.1 2.4 %collective-permute-start.6 = (bf16[32,384]{1,0:T(8,128)(2,1)S(1)}, bf16[32,384]{1,0:T(8,128)(2,1)S(1)}, u32[]{:S(2)}, u32[]{:S(2)}) collective-permute-start(bf16[32,384]{1,0:T(8,128)(2,1)S(1)} %add.76), channel_id=1, source_target_pairs={{0,48},{8,56},{16,0},{24,8},{32,16},{40,24},{48,32},{56,40},{1,49}... | collective-permute-start | bytes 73736 | tf_op jit(solution)/shard_map/ppermute | solution.py:19
  35.5 1.2 collective-permute-done.6
  36.7 1.8 %collective-permute-start.7 = (bf16[32,384]{1,0:T(8,128)(2,1)S(1)}, bf16[32,384]{1,0:T(8,128)(2,1)S(1)}, u32[]{:S(2)}, u32[]{:S(2)}) collective-permute-start(bf16[32,384]{1,0:T(8,128)(2,1)S(1)} %add_add_fusion.refs_0_), channel_id=1, source_target_pairs={{0,64},{64,128},{128,192},{192,0},{1,65},{65,129},{129,193},{193,1... | collective-permute-start | bytes 73736 | tf_op jit(solution)/shard_map/ppermute | solution.py:19
  38.5 2.4 %collective-permute-start.8 = (bf16[32,384]{1,0:T(8,128)(2,1)S(1)}, bf16[32,384]{1,0:T(8,128)(2,1)S(1)}, u32[]{:S(2)}, u32[]{:S(2)}) collective-permute-start(bf16[32,384]{1,0:T(8,128)(2,1)S(1)} %add_add_fusion.refs_0_), channel_id=1, source_target_pairs={{0,128},{64,192},{128,0},{192,64},{1,129},{65,193},{129,1},{193,65... | collective-permute-start | bytes 73736 | tf_op jit(solution)/shard_map/ppermute | solution.py:19
  41.0 2.6 %collective-permute-start.10 = (bf16[32,384]{1,0:T(8,128)(2,1)S(1)}, bf16[32,384]{1,0:T(8,128)(2,1)S(1)}, u32[]{:S(2)}, u32[]{:S(2)}) collective-permute-start(bf16[32,384]{1,0:T(8,128)(2,1)S(1)} %add_add_fusion.refs_0_), channel_id=1, source_target_pairs={{0,8},{8,0},{16,24},{24,16},{32,40},{40,32},{48,56},{56,48},{1,9},... | collective-permute-start | bytes 73736 | tf_op jit(solution)/shard_map/ppermute | solution.py:19
  43.9 2.3 %collective-permute-start.12 = (bf16[32,384]{1,0:T(8,128)(2,1)S(1)}, bf16[32,384]{1,0:T(8,128)(2,1)S(1)}, u32[]{:S(2)}, u32[]{:S(2)}) collective-permute-start(bf16[32,384]{1,0:T(8,128)(2,1)S(1)} %collective-permute-done.8.refs_2_), channel_id=1, source_target_pairs={{0,8},{8,0},{16,24},{24,16},{32,40},{40,32},{48,56},{56,48},{1,9},... | collective-permute-start | bytes 73736 | tf_op jit(solution)/shard_map/ppermute | solution.py:19
  46.2 1.2 collective-permute-start.13
  47.6 0.6 collective-permute-done.13.refs_7_
  48.2 0.6 shard_map.74
  48.9 1.3 multiply_convert_fusion.1
  50.1 1.7 %multiply_convert_fusion = bf16[8,2,8,8,3072]{4,3,2,1,0:T(8,128)(2,1)S(1)} fusion(f32[8,8,3072]{2,1,0:T(8,128)S(1)} %convert.11, f32[2,8,3072]{2,1,0:T(8,128)S(1)} %get-tuple-element.11), kind=kLoop, calls=%fused_computation | loop fusion | flops 6291456 | bytes 7274496 | tf_op jit(solution)/shard_map/convert_element_type | solution.py:252
  51.8 1.9 %fusion.4 = bf16[256,1024]{1,0:T(8,128)(2,1)S(1)} fusion(bf16[1024,3072]{1,0:T(8,128)(2,1)S(1)} %bitcast.60, bf16[3072,1024]{1,0:T(8,128)(2,1)S(1)} %bitcast.58, s32[]{:T(128)S(6)} %select_n.57), kind=kOutput, calls=%fused_computation.9 | convolution fusion | flops 1610874880 | bytes 8388612 | tf_op jit(solution)/shard_map/dot_general | solution.py:253
  53.7 1.9 %fusion.7 = bf16[256,1024]{1,0:T(8,128)(2,1)S(1)} fusion(bf16[1024,3072]{1,0:T(8,128)(2,1)S(1)} %bitcast.59, bf16[3072,1024]{1,0:T(8,128)(2,1)S(1)} %bitcast.58, s32[]{:T(128)S(6)} %select_n.57), kind=kOutput, calls=%fused_computation.10 | convolution fusion | flops 1610874880 | bytes 8388612 | tf_op jit(solution)/shard_map/dot_general | solution.py:253
  55.9 1.0 fusion.10
  57.1 1.2 pad_maximum_fusion
  58.3 4.6 %all-to-all-start = ((bf16[8,32,2560]{2,1,0:T(8,128)(2,1)}), bf16[8,32,2560]{2,1,0:T(8,128)(2,1)S(1)}, u32[]{:S(2)}, u32[]{:S(2)}) async-start(bf16[8,32,2560]{2,1,0:T(8,128)(2,1)} %pad_maximum_fusion), calls=%async_computation | async-start | bytes 2621440 | tf_op jit(solution)/shard_map/all_to_all | solution.py:272
  62.9 0.7 constant_dynamic-slice_fusion.1
  63.8 0.8 dynamic_slice.18
  64.7 0.8 dynamic_slice.19
  65.6 15.3 %all-to-all-done = bf16[8,32,2560]{2,1,0:T(8,128)(2,1)S(1)} async-done(((bf16[8,32,2560]{2,1,0:T(8,128)(2,1)}), bf16[8,32,2560]{2,1,0:T(8,128)(2,1)S(1)}, u32[]{:S(2)}, u32[]{:S(2)}) %all-to-all-start) | async-done | bytes 1310752 | tf_op jit(solution)/shard_map/all_to_all | solution.py:272
  81.3 2.2 %collective-permute-start.15 = (bf16[32,512]{1,0:T(8,128)(2,1)S(1)}, bf16[32,512]{1,0:T(8,128)(2,1)S(1)}, u32[]{:S(2)}, u32[]{:S(2)}) collective-permute-start(bf16[32,512]{1,0:T(8,128)(2,1)S(1)} %fusion.17.refs_0_), channel_id=1, source_target_pairs={{0,4},{1,5},{2,6},{3,7},{4,0},{5,1},{6,2},{7,3},{8,12},{9,13},{10,... | collective-permute-start | bytes 98312 | tf_op jit(solution)/shard_map/ppermute | solution.py:19
  83.5 0.4 collective-permute-start.16
  84.0 1.6 %collective-permute-start.17 = (bf16[32,512]{1,0:T(8,128)(2,1)S(1)}, bf16[32,512]{1,0:T(8,128)(2,1)S(1)}, u32[]{:S(2)}, u32[]{:S(2)}) collective-permute-start(bf16[32,512]{1,0:T(8,128)(2,1)S(1)} %fusion.17.refs_0_), channel_id=1, source_target_pairs={{0,1},{1,0},{2,3},{3,2},{4,5},{5,4},{6,7},{7,6},{8,9},{9,8},{10,11... | collective-permute-start | bytes 98312 | tf_op jit(solution)/shard_map/ppermute | solution.py:19
  85.7 1.8 %collective-permute-start.1 = (s32[6]{0:T(128)S(1)}, s32[6]{0:T(128)S(1)}, u32[]{:S(2)}, u32[]{:S(2)}) collective-permute-start(s32[6]{0:T(128)S(1)} %copy-done.3), channel_id=1, source_target_pairs={{0,128},{64,192},{128,0},{192,64},{1,129},{65,193},{129,1},{193,65... | collective-permute-start | bytes 80 | tf_op jit(solution)/shard_map/ppermute | solution.py:19
  87.5 2.2 %collective-permute-done.1 = s32[6]{0:T(128)S(1)} collective-permute-done((s32[6]{0:T(128)S(1)}, s32[6]{0:T(128)S(1)}, u32[]{:S(2)}, u32[]{:S(2)}) %collective-permute-start.1) | collective-permute-done | bytes 56 | tf_op jit(solution)/shard_map/ppermute | solution.py:19
  89.7 1.5 %collective-permute-start.2 = (s32[6]{0:T(128)S(1)}, s32[6]{0:T(128)S(1)}, u32[]{:S(2)}, u32[]{:S(2)}) collective-permute-start(s32[6]{0:T(128)S(1)} %copy-done.3), channel_id=1, source_target_pairs={{0,192},{64,0},{128,64},{192,128},{1,193},{65,1},{129,65},{193,129... | collective-permute-start | bytes 80 | tf_op jit(solution)/shard_map/ppermute | solution.py:19
  91.2 1.3 collective-permute-done.2
  92.5 2.1 %collective-permute-start.21 = (bf16[2,32,1024]{2,1,0:T(8,128)(2,1)S(1)}, bf16[2,32,1024]{2,1,0:T(8,128)(2,1)S(1)}, u32[]{:S(2)}, u32[]{:S(2)}) collective-permute-start(bf16[2,32,1024]{2,1,0:T(8,128)(2,1)S(1)} %pad_maximum_fusion.2.refs_0_), channel_id=1, source_target_pairs={{0,16},{8,24},{16,32},{24,40},{32,48},{40,56},{48,0},{56,8},{1,17}... | collective-permute-start | bytes 393224 | tf_op jit(solution)/shard_map/ppermute | solution.py:19
  94.6 5.4 %collective-permute-start.22 = (bf16[2,32,1024]{2,1,0:T(8,128)(2,1)S(1)}, bf16[2,32,1024]{2,1,0:T(8,128)(2,1)S(1)}, u32[]{:S(2)}, u32[]{:S(2)}) collective-permute-start(bf16[2,32,1024]{2,1,0:T(8,128)(2,1)S(1)} %pad_maximum_fusion.2.refs_0_), channel_id=1, source_target_pairs={{0,32},{8,40},{16,48},{24,56},{32,0},{40,8},{48,16},{56,24},{1,33}... | collective-permute-start | bytes 393224 | tf_op jit(solution)/shard_map/ppermute | solution.py:19
  100.0 1.6 %collective-permute-start.18 = (bf16[32,512]{1,0:T(8,128)(2,1)S(1)}, bf16[32,512]{1,0:T(8,128)(2,1)S(1)}, u32[]{:S(2)}, u32[]{:S(2)}) collective-permute-start(bf16[32,512]{1,0:T(8,128)(2,1)S(1)} %collective-permute-done.14.refs_1_), channel_id=1, source_target_pairs={{0,1},{1,0},{2,3},{3,2},{4,5},{5,4},{6,7},{7,6},{8,9},{9,8},{10,11... | collective-permute-start | bytes 98312 | tf_op jit(solution)/shard_map/ppermute | solution.py:19
  101.7 1.5 %constant_dynamic-slice_fusion.basis_ref = bf16[768,1024]{1,0:T(8,128)(2,1)S(1)} fusion(bf16[3072,1024]{1,0:T(8,128)(2,1)} %param.9, s32[]{:T(128)S(6)} %select_n.56), kind=kLoop, calls=%fused_computation.59 | loop fusion | bytes 3145732 | tf_op jit(solution)/shard_map/dynamic_slice | solution.py:286
  103.2 5.2 %collective-permute-done.18.refs_5_ = bf16[32,512]{1,0:T(8,128)(2,1)S(1)} collective-permute-done((bf16[32,512]{1,0:T(8,128)(2,1)S(1)}, bf16[32,512]{1,0:T(8,128)(2,1)S(1)}, u32[]{:S(2)}, u32[]{:S(2)}) %collective-permute-start.18) | collective-permute-done | bytes 32800 | tf_op jit(solution)/shard_map/ppermute | solution.py:19
  108.5 9.1 %collective-permute-start.24 = (bf16[2,32,1024]{2,1,0:T(8,128)(2,1)S(1)}, bf16[2,32,1024]{2,1,0:T(8,128)(2,1)S(1)}, u32[]{:S(2)}, u32[]{:S(2)}) collective-permute-start(bf16[2,32,1024]{2,1,0:T(8,128)(2,1)S(1)} %pad_maximum_fusion.2.refs_0_), channel_id=1, source_target_pairs={{0,8},{8,0},{16,24},{24,16},{32,40},{40,32},{48,56},{56,48},{1,9},... | collective-permute-start | bytes 393224 | tf_op jit(solution)/shard_map/ppermute | solution.py:19
  118.5 1.9 %collective-permute-done.20.refs_7_ = bf16[32,512]{1,0:T(8,128)(2,1)S(1)} collective-permute-done((bf16[32,512]{1,0:T(8,128)(2,1)S(1)}, bf16[32,512]{1,0:T(8,128)(2,1)S(1)}, u32[]{:S(2)}, u32[]{:S(2)}) %collective-permute-start.20) | collective-permute-done | bytes 32800 | tf_op jit(solution)/shard_map/ppermute | solution.py:19
  120.3 1.4 copy-done
  121.7 2.4 %shard_map.75.exchange_ref = f32[24,16,512]{2,1,0:T(8,128)S(1)} custom-call(s32[3]{0:T(128)S(1)} %pad_add_fusion.1.meta_ref, s32[4,6]{1,0:T(4,128)S(1)} %pad_add_fusion.ids_ref, bf16[32,32,768]{2,1,0:T(8,128)(2,1)S(1)} %copy-done, bf16[768,1024]{1,0:T(8,128)(2,1)S(1)} %constant_dynamic-slice_fusion.basis_ref, bf16[32,512]{1,0:T(8,128)(2,1)S(1)} %fusion.17.refs_0_, ...), custom_call_target="tpu_custom_call" | custom-call | flops 301989888 | bytes 4194304 | tf_op jit(solution)/shard_map/pallas_call | solution.py:136
  124.2 2.8 %shard_map.76 = bf16[32,12,512]{2,1,0:T(8,128)(2,1)} custom-call(s32[3]{0:T(128)S(1)} %pad_add_fusion.1.meta_ref, s32[4,6]{1,0:T(4,128)S(1)} %pad_add_fusion.ids_ref, bf16[512,512]{1,0:T(8,128)(2,1)S(1)} %fusion.11.order_ref, f32[24,16,512]{2,1,0:T(8,128)S(1)} %shard_map.75.exchange_ref, bf16[2,32,1024]{2,1,0:T(8,128)(2,1)S(1)} %pad_maximum_fusion.2.refs_0_, ...), custom_call_target="tpu_custom_call" | custom-call | tf_op jit(solution)/shard_map/pallas_call | solution.py:203
  127.0 3.9 %all-to-all-start.1 = ((bf16[32,12,512]{2,1,0:T(8,128)(2,1)}), bf16[32,12,512]{2,1,0:T(8,128)(2,1)S(1)}, u32[]{:S(2)}, u32[]{:S(2)}) async-start(bf16[32,12,512]{2,1,0:T(8,128)(2,1)} %shard_map.76), calls=%async_computation.1 | async-start | bytes 1048576 | tf_op jit(solution)/shard_map/all_to_all | solution.py:295
  130.9 10.4 %all-to-all-done.1 = bf16[32,12,512]{2,1,0:T(8,128)(2,1)S(1)} async-done(((bf16[32,12,512]{2,1,0:T(8,128)(2,1)}), bf16[32,12,512]{2,1,0:T(8,128)(2,1)S(1)}, u32[]{:S(2)}, u32[]{:S(2)}) %all-to-all-start.1) | async-done | bytes 393248 | tf_op jit(solution)/shard_map/all_to_all | solution.py:295
  141.5 0.6 copy.24
  (71 shorter events, 3.4 us)
Async XLA Ops:
  20.5 0.7 copy-start.1
  21.8 5.2 %collective-permute-start.3 = (bf16[32,384]{1,0:T(8,128)(2,1)S(1)}, bf16[32,384]{1,0:T(8,128)(2,1)S(1)}, u32[]{:S(2)}, u32[]{:S(2)}) collective-permute-start(bf16[32,384]{1,0:T(8,128)(2,1)S(1)} %get-tuple-element.8), channel_id=1, source_target_pairs={{0,8},{8,0},{16,24},{24,16},{32,40},{40,32},{48,56},{56,48},{1,9},... | collective-permute-start | bytes 73736 | tf_op jit(solution)/shard_map/ppermute | solution.py:19
  27.0 8.5 %collective-permute-start.4 = (bf16[32,384]{1,0:T(8,128)(2,1)S(1)}, bf16[32,384]{1,0:T(8,128)(2,1)S(1)}, u32[]{:S(2)}, u32[]{:S(2)}) collective-permute-start(bf16[32,384]{1,0:T(8,128)(2,1)S(1)} %add.76), channel_id=1, source_target_pairs={{0,16},{8,24},{16,32},{24,40},{32,48},{40,56},{48,0},{56,8},{1,17}... | collective-permute-start | bytes 73736 | tf_op jit(solution)/shard_map/ppermute | solution.py:19
  28.0 7.5 %collective-permute-start.5 = (bf16[32,384]{1,0:T(8,128)(2,1)S(1)}, bf16[32,384]{1,0:T(8,128)(2,1)S(1)}, u32[]{:S(2)}, u32[]{:S(2)}) collective-permute-start(bf16[32,384]{1,0:T(8,128)(2,1)S(1)} %add.76), channel_id=1, source_target_pairs={{0,32},{8,40},{16,48},{24,56},{32,0},{40,8},{48,16},{56,24},{1,33}... | collective-permute-start | bytes 73736 | tf_op jit(solution)/shard_map/ppermute | solution.py:19
  33.1 3.6 %collective-permute-start.6 = (bf16[32,384]{1,0:T(8,128)(2,1)S(1)}, bf16[32,384]{1,0:T(8,128)(2,1)S(1)}, u32[]{:S(2)}, u32[]{:S(2)}) collective-permute-start(bf16[32,384]{1,0:T(8,128)(2,1)S(1)} %add.76), channel_id=1, source_target_pairs={{0,48},{8,56},{16,0},{24,8},{32,16},{40,24},{48,32},{56,40},{1,49}... | collective-permute-start | bytes 73736 | tf_op jit(solution)/shard_map/ppermute | solution.py:19
  36.7 6.9 %collective-permute-start.7 = (bf16[32,384]{1,0:T(8,128)(2,1)S(1)}, bf16[32,384]{1,0:T(8,128)(2,1)S(1)}, u32[]{:S(2)}, u32[]{:S(2)}) collective-permute-start(bf16[32,384]{1,0:T(8,128)(2,1)S(1)} %add_add_fusion.refs_0_), channel_id=1, source_target_pairs={{0,64},{64,128},{128,192},{192,0},{1,65},{65,129},{129,193},{193,1... | collective-permute-start | bytes 73736 | tf_op jit(solution)/shard_map/ppermute | solution.py:19
  38.5 5.4 %collective-permute-start.8 = (bf16[32,384]{1,0:T(8,128)(2,1)S(1)}, bf16[32,384]{1,0:T(8,128)(2,1)S(1)}, u32[]{:S(2)}, u32[]{:S(2)}) collective-permute-start(bf16[32,384]{1,0:T(8,128)(2,1)S(1)} %add_add_fusion.refs_0_), channel_id=1, source_target_pairs={{0,128},{64,192},{128,0},{192,64},{1,129},{65,193},{129,1},{193,65... | collective-permute-start | bytes 73736 | tf_op jit(solution)/shard_map/ppermute | solution.py:19
  40.9 5.3 %collective-permute-start.9 = (bf16[32,384]{1,0:T(8,128)(2,1)S(1)}, bf16[32,384]{1,0:T(8,128)(2,1)S(1)}, u32[]{:S(2)}, u32[]{:S(2)}) collective-permute-start(bf16[32,384]{1,0:T(8,128)(2,1)S(1)} %add_add_fusion.refs_0_), channel_id=1, source_target_pairs={{0,192},{64,0},{128,64},{192,128},{1,193},{65,1},{129,65},{193,129... | collective-permute-start | bytes 73736 | tf_op jit(solution)/shard_map/ppermute | solution.py:19
  41.0 6.5 %collective-permute-start.10 = (bf16[32,384]{1,0:T(8,128)(2,1)S(1)}, bf16[32,384]{1,0:T(8,128)(2,1)S(1)}, u32[]{:S(2)}, u32[]{:S(2)}) collective-permute-start(bf16[32,384]{1,0:T(8,128)(2,1)S(1)} %add_add_fusion.refs_0_), channel_id=1, source_target_pairs={{0,8},{8,0},{16,24},{24,16},{32,40},{40,32},{48,56},{56,48},{1,9},... | collective-permute-start | bytes 73736 | tf_op jit(solution)/shard_map/ppermute | solution.py:19
  43.6 3.9 %collective-permute-start.11 = (bf16[32,384]{1,0:T(8,128)(2,1)S(1)}, bf16[32,384]{1,0:T(8,128)(2,1)S(1)}, u32[]{:S(2)}, u32[]{:S(2)}) collective-permute-start(bf16[32,384]{1,0:T(8,128)(2,1)S(1)} %collective-permute-done.7.refs_1_), channel_id=1, source_target_pairs={{0,8},{8,0},{16,24},{24,16},{32,40},{40,32},{48,56},{56,48},{1,9},... | collective-permute-start | bytes 73736 | tf_op jit(solution)/shard_map/ppermute | solution.py:19
  43.9 3.7 %collective-permute-start.12 = (bf16[32,384]{1,0:T(8,128)(2,1)S(1)}, bf16[32,384]{1,0:T(8,128)(2,1)S(1)}, u32[]{:S(2)}, u32[]{:S(2)}) collective-permute-start(bf16[32,384]{1,0:T(8,128)(2,1)S(1)} %collective-permute-done.8.refs_2_), channel_id=1, source_target_pairs={{0,8},{8,0},{16,24},{24,16},{32,40},{40,32},{48,56},{56,48},{1,9},... | collective-permute-start | bytes 73736 | tf_op jit(solution)/shard_map/ppermute | solution.py:19
  46.2 2.0 %collective-permute-start.13 = (bf16[32,384]{1,0:T(8,128)(2,1)S(1)}, bf16[32,384]{1,0:T(8,128)(2,1)S(1)}, u32[]{:S(2)}, u32[]{:S(2)}) collective-permute-start(bf16[32,384]{1,0:T(8,128)(2,1)S(1)} %collective-permute-done.9.refs_3_), channel_id=1, source_target_pairs={{0,8},{8,0},{16,24},{24,16},{32,40},{40,32},{48,56},{56,48},{1,9},... | collective-permute-start | bytes 73736 | tf_op jit(solution)/shard_map/ppermute | solution.py:19
  48.8 3.0 %slice-start = ((s8[6291456]{0:T(1024)(128)(4,1)}), s8[4194304]{0:T(1024)(128)(4,1)S(1)}, s32[]{:S(2)}) async-start(s8[6291456]{0:T(1024)(128)(4,1)} %bitcast.57), calls=%async_computation.3 | async-start | bytes 8388608
  48.9 3.0 %slice-start.1 = ((s8[6291456]{0:T(1024)(128)(4,1)}), s8[2097152]{0:T(1024)(128)(4,1)S(1)}, s32[]{:S(2)}) async-start(s8[6291456]{0:T(1024)(128)(4,1)} %bitcast.57), calls=%async_computation.4 | async-start | bytes 4194304
  55.9 7.8 %copy-start.3 = (s32[6]{0:T(128)S(1)}, s32[6]{0:T(128)}, u32[]{:S(2)}) copy-start(s32[6]{0:T(128)} %param.13) | copy-start | bytes 76
  58.3 22.7 %all-to-all-start = ((bf16[8,32,2560]{2,1,0:T(8,128)(2,1)}), bf16[8,32,2560]{2,1,0:T(8,128)(2,1)S(1)}, u32[]{:S(2)}, u32[]{:S(2)}) async-start(bf16[8,32,2560]{2,1,0:T(8,128)(2,1)} %pad_maximum_fusion), calls=%async_computation | async-start | bytes 2621440 | tf_op jit(solution)/shard_map/all_to_all | solution.py:272
  62.9 57.4 %all-gather.4.cloned.1.call-start = ((), (), s32[]{:S(2)}) async-start(), calls=%async_computation.2 | async-start | bytes 1769472 | tf_op jit(solution)/shard_map/all_gather | solution.py:243
  63.7 22.0 %collective-permute-start = (s32[6]{0:T(128)S(1)}, s32[6]{0:T(128)S(1)}, u32[]{:S(2)}, u32[]{:S(2)}) collective-permute-start(s32[6]{0:T(128)S(1)} %copy-done.3), channel_id=1, source_target_pairs={{0,64},{64,128},{128,192},{192,0},{1,65},{65,129},{129,193},{193,1... | collective-permute-start | bytes 80 | tf_op jit(solution)/shard_map/ppermute | solution.py:19
  81.1 49.8 %copy-start.2 = (s32[2]{0:T(128)S(1)}, s32[2]{0:T(128)}, u32[]{:S(2)}) copy-start(s32[2]{0:T(128)} %window_ref.1) | copy-start | bytes 28
  81.2 13.4 %collective-permute-start.14 = (bf16[32,512]{1,0:T(8,128)(2,1)S(1)}, bf16[32,512]{1,0:T(8,128)(2,1)S(1)}, u32[]{:S(2)}, u32[]{:S(2)}) collective-permute-start(bf16[32,512]{1,0:T(8,128)(2,1)S(1)} %fusion.17.refs_0_), channel_id=1, source_target_pairs={{0,2},{1,3},{2,4},{3,5},{4,6},{5,7},{6,0},{7,1},{8,10},{9,11},{10,... | collective-permute-start | bytes 98312 | tf_op jit(solution)/shard_map/ppermute | solution.py:19
  81.3 18.7 %collective-permute-start.15 = (bf16[32,512]{1,0:T(8,128)(2,1)S(1)}, bf16[32,512]{1,0:T(8,128)(2,1)S(1)}, u32[]{:S(2)}, u32[]{:S(2)}) collective-permute-start(bf16[32,512]{1,0:T(8,128)(2,1)S(1)} %fusion.17.refs_0_), channel_id=1, source_target_pairs={{0,4},{1,5},{2,6},{3,7},{4,0},{5,1},{6,2},{7,3},{8,12},{9,13},{10,... | collective-permute-start | bytes 98312 | tf_op jit(solution)/shard_map/ppermute | solution.py:19
  83.5 16.5 %collective-permute-start.16 = (bf16[32,512]{1,0:T(8,128)(2,1)S(1)}, bf16[32,512]{1,0:T(8,128)(2,1)S(1)}, u32[]{:S(2)}, u32[]{:S(2)}) collective-permute-start(bf16[32,512]{1,0:T(8,128)(2,1)S(1)} %fusion.17.refs_0_), channel_id=1, source_target_pairs={{0,6},{1,7},{2,0},{3,1},{4,2},{5,3},{6,4},{7,5},{8,14},{9,15},{10,... | collective-permute-start | bytes 98312 | tf_op jit(solution)/shard_map/ppermute | solution.py:19
  84.0 17.6 %collective-permute-start.17 = (bf16[32,512]{1,0:T(8,128)(2,1)S(1)}, bf16[32,512]{1,0:T(8,128)(2,1)S(1)}, u32[]{:S(2)}, u32[]{:S(2)}) collective-permute-start(bf16[32,512]{1,0:T(8,128)(2,1)S(1)} %fusion.17.refs_0_), channel_id=1, source_target_pairs={{0,1},{1,0},{2,3},{3,2},{4,5},{5,4},{6,7},{7,6},{8,9},{9,8},{10,11... | collective-permute-start | bytes 98312 | tf_op jit(solution)/shard_map/ppermute | solution.py:19
  85.7 4.0 %collective-permute-start.1 = (s32[6]{0:T(128)S(1)}, s32[6]{0:T(128)S(1)}, u32[]{:S(2)}, u32[]{:S(2)}) collective-permute-start(s32[6]{0:T(128)S(1)} %copy-done.3), channel_id=1, source_target_pairs={{0,128},{64,192},{128,0},{192,64},{1,129},{65,193},{129,1},{193,65... | collective-permute-start | bytes 80 | tf_op jit(solution)/shard_map/ppermute | solution.py:19
  89.7 2.8 %collective-permute-start.2 = (s32[6]{0:T(128)S(1)}, s32[6]{0:T(128)S(1)}, u32[]{:S(2)}, u32[]{:S(2)}) collective-permute-start(s32[6]{0:T(128)S(1)} %copy-done.3), channel_id=1, source_target_pairs={{0,192},{64,0},{128,64},{192,128},{1,193},{65,1},{129,65},{193,129... | collective-permute-start | bytes 80 | tf_op jit(solution)/shard_map/ppermute | solution.py:19
  92.5 25.1 %collective-permute-start.21 = (bf16[2,32,1024]{2,1,0:T(8,128)(2,1)S(1)}, bf16[2,32,1024]{2,1,0:T(8,128)(2,1)S(1)}, u32[]{:S(2)}, u32[]{:S(2)}) collective-permute-start(bf16[2,32,1024]{2,1,0:T(8,128)(2,1)S(1)} %pad_maximum_fusion.2.refs_0_), channel_id=1, source_target_pairs={{0,16},{8,24},{16,32},{24,40},{32,48},{40,56},{48,0},{56,8},{1,17}... | collective-permute-start | bytes 393224 | tf_op jit(solution)/shard_map/ppermute | solution.py:19
  94.6 23.3 %collective-permute-start.22 = (bf16[2,32,1024]{2,1,0:T(8,128)(2,1)S(1)}, bf16[2,32,1024]{2,1,0:T(8,128)(2,1)S(1)}, u32[]{:S(2)}, u32[]{:S(2)}) collective-permute-start(bf16[2,32,1024]{2,1,0:T(8,128)(2,1)S(1)} %pad_maximum_fusion.2.refs_0_), channel_id=1, source_target_pairs={{0,32},{8,40},{16,48},{24,56},{32,0},{40,8},{48,16},{56,24},{1,33}... | collective-permute-start | bytes 393224 | tf_op jit(solution)/shard_map/ppermute | solution.py:19
  100.0 18.2 %collective-permute-start.23 = (bf16[2,32,1024]{2,1,0:T(8,128)(2,1)S(1)}, bf16[2,32,1024]{2,1,0:T(8,128)(2,1)S(1)}, u32[]{:S(2)}, u32[]{:S(2)}) collective-permute-start(bf16[2,32,1024]{2,1,0:T(8,128)(2,1)S(1)} %pad_maximum_fusion.2.refs_0_), channel_id=1, source_target_pairs={{0,48},{8,56},{16,0},{24,8},{32,16},{40,24},{48,32},{56,40},{1,49}... | collective-permute-start | bytes 393224 | tf_op jit(solution)/shard_map/ppermute | solution.py:19
  100.0 8.5 %collective-permute-start.18 = (bf16[32,512]{1,0:T(8,128)(2,1)S(1)}, bf16[32,512]{1,0:T(8,128)(2,1)S(1)}, u32[]{:S(2)}, u32[]{:S(2)}) collective-permute-start(bf16[32,512]{1,0:T(8,128)(2,1)S(1)} %collective-permute-done.14.refs_1_), channel_id=1, source_target_pairs={{0,1},{1,0},{2,3},{3,2},{4,5},{5,4},{6,7},{7,6},{8,9},{9,8},{10,11... | collective-permute-start | bytes 98312 | tf_op jit(solution)/shard_map/ppermute | solution.py:19
  101.6 16.0 %collective-permute-start.19 = (bf16[32,512]{1,0:T(8,128)(2,1)S(1)}, bf16[32,512]{1,0:T(8,128)(2,1)S(1)}, u32[]{:S(2)}, u32[]{:S(2)}) collective-permute-start(bf16[32,512]{1,0:T(8,128)(2,1)S(1)} %collective-permute-done.15.refs_2_), channel_id=1, source_target_pairs={{0,1},{1,0},{2,3},{3,2},{4,5},{5,4},{6,7},{7,6},{8,9},{9,8},{10,11... | collective-permute-start | bytes 98312 | tf_op jit(solution)/shard_map/ppermute | solution.py:19
  108.5 15.7 %collective-permute-start.24 = (bf16[2,32,1024]{2,1,0:T(8,128)(2,1)S(1)}, bf16[2,32,1024]{2,1,0:T(8,128)(2,1)S(1)}, u32[]{:S(2)}, u32[]{:S(2)}) collective-permute-start(bf16[2,32,1024]{2,1,0:T(8,128)(2,1)S(1)} %pad_maximum_fusion.2.refs_0_), channel_id=1, source_target_pairs={{0,8},{8,0},{16,24},{24,16},{32,40},{40,32},{48,56},{56,48},{1,9},... | collective-permute-start | bytes 393224 | tf_op jit(solution)/shard_map/ppermute | solution.py:19
  117.6 2.8 %collective-permute-start.20 = (bf16[32,512]{1,0:T(8,128)(2,1)S(1)}, bf16[32,512]{1,0:T(8,128)(2,1)S(1)}, u32[]{:S(2)}, u32[]{:S(2)}) collective-permute-start(bf16[32,512]{1,0:T(8,128)(2,1)S(1)} %collective-permute-done.16.refs_3_), channel_id=1, source_target_pairs={{0,1},{1,0},{2,3},{3,2},{4,5},{5,4},{6,7},{7,6},{8,9},{9,8},{10,11... | collective-permute-start | bytes 98312 | tf_op jit(solution)/shard_map/ppermute | solution.py:19
  117.6 6.6 %collective-permute-start.25 = (bf16[2,32,1024]{2,1,0:T(8,128)(2,1)S(1)}, bf16[2,32,1024]{2,1,0:T(8,128)(2,1)S(1)}, u32[]{:S(2)}, u32[]{:S(2)}) collective-permute-start(bf16[2,32,1024]{2,1,0:T(8,128)(2,1)S(1)} %collective-permute-done.21.refs_1_), channel_id=1, source_target_pairs={{0,8},{8,0},{16,24},{24,16},{32,40},{40,32},{48,56},{56,48},{1,9},... | collective-permute-start | bytes 393224 | tf_op jit(solution)/shard_map/ppermute | solution.py:19
  117.9 6.3 %collective-permute-start.26 = (bf16[2,32,1024]{2,1,0:T(8,128)(2,1)S(1)}, bf16[2,32,1024]{2,1,0:T(8,128)(2,1)S(1)}, u32[]{:S(2)}, u32[]{:S(2)}) collective-permute-start(bf16[2,32,1024]{2,1,0:T(8,128)(2,1)S(1)} %collective-permute-done.22.refs_2_), channel_id=1, source_target_pairs={{0,8},{8,0},{16,24},{24,16},{32,40},{40,32},{48,56},{56,48},{1,9},... | collective-permute-start | bytes 393224 | tf_op jit(solution)/shard_map/ppermute | solution.py:19
  118.2 6.0 %collective-permute-start.27 = (bf16[2,32,1024]{2,1,0:T(8,128)(2,1)S(1)}, bf16[2,32,1024]{2,1,0:T(8,128)(2,1)S(1)}, u32[]{:S(2)}, u32[]{:S(2)}) collective-permute-start(bf16[2,32,1024]{2,1,0:T(8,128)(2,1)S(1)} %collective-permute-done.23.refs_3_), channel_id=1, source_target_pairs={{0,8},{8,0},{16,24},{24,16},{32,40},{40,32},{48,56},{56,48},{1,9},... | collective-permute-start | bytes 393224 | tf_op jit(solution)/shard_map/ppermute | solution.py:19
  120.3 1.4 copy-start
  127.0 14.4 %all-to-all-start.1 = ((bf16[32,12,512]{2,1,0:T(8,128)(2,1)}), bf16[32,12,512]{2,1,0:T(8,128)(2,1)S(1)}, u32[]{:S(2)}, u32[]{:S(2)}) async-start(bf16[32,12,512]{2,1,0:T(8,128)(2,1)} %shard_map.76), calls=%async_computation.1 | async-start | bytes 1048576 | tf_op jit(solution)/shard_map/all_to_all | solution.py:295
Sparse Core Ops, SparseCore 0:
  65.6 31.5 all-gather.3

commit v3 on v2

--- a/solution.py
+++ b/solution.py
@@ -24,7 +24,7 @@
     return device // 8, device % 8, tile % 2
 
 
-def pick_kernel(meta_ref, window_ref, columns_ref, mine_ref, other_ref):
+def pick_kernel(meta_ref, window_ref, columns_ref, mine_ref, other_ref, quarter_ref):
     i, j = meta_ref[0], meta_ref[1]
     width = 2 * mine_ref.shape[1]
     first_lane = pl.multiple_of(i * width, 128)
@@ -36,46 +36,51 @@
             both = columns_ref[at, first : first + 16, pl.ds(first_lane, width)].astype(F32)
             rows = jnp.where(half == 0, both[:8], both[8:])
             picked.append(jnp.where(column == j, rows, jnp.zeros_like(rows)))
+    quarter_ref[...] = columns_ref[:, :, pl.ds(first_lane, width)]
     rows = jnp.concatenate(picked, axis=0)
     low, high = rows[:, : width // 2], rows[:, width // 2 :]
     mine_ref[...] = jnp.where(j % 2 == 0, low, high).astype(BF16)
     other_ref[...] = jnp.where(j % 2 == 0, high, low).astype(BF16)
 
 
-def place_kernel(meta_ref, *refs):
+def place_kernel(meta_ref, near_ref, next_ref, far_ref, out_ref):
     i, j = meta_ref[0], meta_ref[1]
-    out_ref = refs[-1]
-    width = refs[0].shape[1]
-    for n in range(4):
-        start = ((i + 4 - n) % 4) * 2
-        for flip in range(2):
-            first = pl.multiple_of((start + (j + flip) % 2) * width, 128)
-            out_ref[:, pl.ds(first, width)] = refs[4 * flip + n][...]
+    width = out_ref.shape[1] // 8
+    for n, flip in enumerate((0, 1, 3, 2)):
+        for half in range(2):
+            start = (i ^ flip) * 2 + (j + half) % 2
+            ref, at = ((near_ref, 0), (next_ref, 0), (far_ref, 0), (far_ref, 2))[n]
+            at = (at + half) * width
+            first = pl.multiple_of(start * width, 128)
+            out_ref[:, pl.ds(first, width)] = ref[:, at : at + width]
 
 
 def row_tiles(meta, window_rows, columns):
     width = columns.shape[2] // 8
     smem, vmem = (pl.BlockSpec(memory_space=m) for m in (pltpu.SMEM, pltpu.VMEM))
     part = jax.ShapeDtypeStruct((32, width), BF16)
-    mine, other = pl.pallas_call(
+    mine, other, quarter = pl.pallas_call(
         pick_kernel,
-        out_shape=(part, part),
+        out_shape=(part, part, jax.ShapeDtypeStruct((4, 32, 2 * width), BF16)),
         in_specs=[smem, smem, vmem],
-        out_specs=(vmem, vmem),
+        out_specs=(vmem, vmem, vmem),
         compiler_params=pltpu.CompilerParams(vmem_limit_bytes=16 * 2**20),
     )(meta, window_rows, columns)
     mine = mine + shift(other, "cp", lambda n: n ^ 1)
-    parts = [shift(mine, "cp", lambda n, s=s: (n + 2 * s) % 8) for s in (1, 2, 3)]
-    mine = mine + parts[0] + parts[1] + parts[2]
-    mine = [mine] + [shift(mine, "vp", lambda n, s=s: (n + s) % 4) for s in (1, 2, 3)]
-    other = [shift(a, "cp", lambda n: n ^ 1) for a in mine]
-    return pl.pallas_call(
+    mine = mine + shift(mine, "cp", lambda n: n ^ 2)
+    mine = mine + shift(mine, "cp", lambda n: n ^ 6)
+    quarter, mine = lax.optimization_barrier((quarter, mine))
+    near = jnp.concatenate([mine, shift(mine, "cp", lambda n: n ^ 1)], axis=1)
+    beside = shift(near, "vp", lambda n: n ^ 1)
+    far = shift(jnp.concatenate([near, beside], axis=1), "vp", lambda n: n ^ 3)
+    rows = pl.pallas_call(
         place_kernel,
         out_shape=jax.ShapeDtypeStruct((32, columns.shape[2]), BF16),
-        in_specs=[smem] + [vmem] * 8,
+        in_specs=[smem] + [vmem] * 3,
         out_specs=vmem,
         compiler_params=pltpu.CompilerParams(vmem_limit_bytes=16 * 2**20),
-    )(meta, *mine, *other)
+    )(meta, near, beside, far)
+    return rows, quarter
 
 
 def pair_block(left, right):
@@ -88,23 +93,24 @@
     return ids_ref[(i + 4 - slot // own) % 4, slot % own]
 
 
-def exchange_kernel(meta_ref, ids_ref, waves_ref, basis_ref, *refs):
-    pieces, out_ref = refs[:8], refs[8]
-    i, k = meta_ref[0], meta_ref[2]
+def exchange_kernel(meta_ref, ids_ref, basis_ref, near_ref, far_ref, *refs):
+    pieces, (out_ref, waves_ref) = refs[:8], refs[8:]
+    i, j, k = meta_ref[0], meta_ref[1], meta_ref[2]
     together = 4
     potential = None
+    for n in range(8):
+        source = k ^ (n % 2) ^ (n // 2 % 2 * 2) ^ (n // 4 * 6)
+        piece = near_ref[n] if n < 4 else far_ref[n - 4]
+        ranks = jnp.concatenate([piece[:, m * 128 : (m + 1) * 128] for m in range(4)], axis=0)
+        basis = basis_ref[:, pl.ds(pl.multiple_of(source * 128, 128), 128)]
+        term = lax.dot_general(
+            ranks, basis, (((0,), (1,)), ((), ())), preferred_element_type=F32
+        )
+        potential = term if potential is None else potential + term
     for flip in range(2):
         for n in range(4):
-            source = ((k // 2 + 4 - n) % 4) * 2 + (k + flip) % 2
-            piece = pieces[4 * flip + n][...]
-            ranks = jnp.concatenate(
-                [piece[:, m * 128 : (m + 1) * 128] for m in range(4)], axis=0
-            )
-            basis = basis_ref[:, pl.ds(pl.multiple_of(source * 128, 128), 128)]
-            term = lax.dot_general(
-                ranks, basis, (((0,), (1,)), ((), ())), preferred_element_type=F32
-            )
-            potential = term if potential is None else potential + term
+            source = ((j // 2 + 4 - n) % 4) * 2 + (j + flip) % 2
+            waves_ref[pl.ds(source * 4, 4)] = pieces[4 * flip + n][...]
     potential = potential.astype(BF16)
 
     def band_rows(first, tile):
@@ -130,19 +136,20 @@
             )
 
 
-def exchange_tiles(meta, ids, waves, basis_rows, pieces):
+def exchange_tiles(meta, ids, basis_rows, near, far, pieces):
     slots = 4 * ids.shape[1]
     smem, vmem = (pl.BlockSpec(memory_space=m) for m in (pltpu.SMEM, pltpu.VMEM))
     return pl.pallas_call(
         exchange_kernel,
         out_shape=jax.ShapeDtypeStruct((slots, 16, 512), F32),
-        in_specs=[smem, smem, vmem, vmem] + [vmem] * 8,
+        in_specs=[smem, smem, vmem, vmem, vmem] + [vmem] * 8,
         out_specs=vmem,
+        scratch_shapes=[pltpu.VMEM((32,) + pieces[0].shape[1:], BF16)],
         compiler_params=pltpu.CompilerParams(vmem_limit_bytes=32 * 2**20),
         cost_estimate=pl.CostEstimate(
             flops=2 * slots * 64 * 128 * 768, bytes_accessed=2**22, transcendentals=0
         ),
-    )(meta, ids, waves, basis_rows, *pieces)
+    )(meta, ids, basis_rows, near, far, *pieces)
 
 
 def direct_kernel(meta_ref, ids_ref, order_ref, exchange_ref, *refs):
@@ -237,10 +244,8 @@
     )
     waves = jnp.concatenate([valence_wavefunction, cond_wave], axis=0)
     columns = lax.all_gather(waves, "vp", axis=0)
-    rows = row_tiles(meta, window_rows, columns)
-
-    quarter_waves = lax.dynamic_slice_in_dim(columns, i * quarter, quarter, 2)
-    all_waves = lax.all_gather(quarter_waves, "cp", axis=0)
+    rows, quarter_waves = row_tiles(meta, window_rows, columns)
+    wave_pieces = gather_pieces(quarter_waves, "cp")
 
     row_val = rows[:16].reshape(2, TV, grid_count).astype(F32)
     row_cond = rows[16:].reshape(2, TC, grid_count).astype(F32)
@@ -282,11 +287,12 @@
     row_sum = (row_sum * coulomb_part.reshape(4, rank_part).T[:, :, None]).astype(BF16)
 
     proj_pieces = gather_pieces(jnp.stack([val_sum, cond_sum]), "cp")
-    row_pieces = gather_pieces(row_sum.reshape(rank_part, 512), "ga")
+    near = row_sum.reshape(1, rank_part, 512)
+    for bits in (1, 2):
+        near = jnp.concatenate([near, shift(near, "ga", lambda n, bits=bits: n ^ bits)])
+    far = shift(near, "ga", lambda n: n ^ 6)
     basis_rows = lax.dynamic_slice_in_dim(screen_basis, i * quarter, quarter, 0)
-    exchange = exchange_tiles(
-        meta, ids, all_waves.reshape(32, 32, quarter), basis_rows, row_pieces
-    )
+    exchange = exchange_tiles(meta, ids, basis_rows, near, far, wave_pieces)
 
     order = jnp.arange(512, dtype=jnp.int32)
     source = (order // 8 % 8) * 64 + (order // 64) * 8 + order % 8

time: 150 us -> 151 us (level)
  starting transfers between devices: 58.9 us -> 76 us
  between operations: 13.8 us -> 0.37 us
  local copies, waits for them, and re-layouts: 7.17 us -> 5.08 us
    all_to_all x1, waiting for transfers between devices: 15.3 us -> 0.01 us  [shards(): lax.all_to_all(sent, 'ga', split_axis=0, concat_axis=0, tiled=True)]
    ppermute x28 -> x26, waiting for transfers between devices: 13.3 us -> 27.5 us  [shift(): return lax.ppermute(array, axis, [(n, send_to(n)) for n in range(size)])]
    ppermute x28 -> x26, starting transfers between devices: 50.4 us -> 64.1 us  [shift(): return lax.ppermute(array, axis, [(n, send_to(n)) for n in range(size)])]
    all_to_all x1, starting transfers between devices: 3.89 us -> 7.32 us  [shards(): lax.all_to_all(tiles, ('vp', 'ga'), split_axis=0, concat_axis=0, tiled=True)]
  transfers between devices with their start and end apart: 31 -> 28, of which waited for: 9 -> 14; matrix products, arithmetic and copies ran while one was open for 3% -> 3% of each run, Pallas kernels for 2% -> 2%
where the time goes in v3:
time: 151 us
  starting transfers between devices  76 us (50%)
  waiting for transfers between devices  39.2 us (26%)
  blocking collectives  12.9 us (9%)
  Pallas kernels  6.47 us (4%)
  other arithmetic  6.13 us (4%)
  local copies, waits for them, and re-layouts  5.08 us (3%)
  matrix products  4.73 us (3%)
    ppermute x26, starting transfers between devices, shift(): return lax.ppermute(array, axis, [(n, send_to(n)) for n in range(size)])  64.1 us
    ppermute x26, waiting for transfers between devices, shift(): return lax.ppermute(array, axis, [(n, send_to(n)) for n in range(size)])  27.5 us
    all_gather x1, blocking collectives, shards(): columns = lax.all_gather(waves, 'vp', axis=0)  12.9 us
    all_to_all x1, waiting for transfers between devices, shards(): lax.all_to_all(tiles, ('vp', 'ga'), split_axis=0, concat_axis=0, tiled=True)  11.7 us
    all_to_all x1, starting transfers between devices, shards(): lax.all_to_all(tiles, ('vp', 'ga'), split_axis=0, concat_axis=0, tiled=True)  7.32 us
    dot_general x3, matrix products, project(): lax.dot_general(basis, flat, (((0,), (1,)), ((), ())), preferred_element_...  4.73 us
    all_to_all x1, starting transfers between devices, shards(): lax.all_to_all(sent, 'ga', split_axis=0, concat_axis=0, tiled=True)  4.65 us
    convert_element_type x3, other arithmetic, project(): flat = pairs.astype(BF16).reshape(-1, grid_count)  3.04 us
  transfers between devices with their start and end apart: 28, of which 14 were waited for; matrix products, arithmetic and copies ran while one was open for 3% of the time, Pallas kernels for 2%

profile of v3, /device:TPU:1, one launch (start us, length us, event | category | flops | bytes accessed | tf_op | source)
XLA Modules:
  0.0 150.9 jit_solution(10395737399232083699)
XLA Ops:
  0.0 1.0 pad_maximum_fusion.1
  1.0 12.9 %all-gather = bf16[128,3072]{1,0:T(8,128)(2,1)S(1)} all-gather(bf16[32,3072]{1,0:T(8,128)(2,1)S(1)} %pad_maximum_fusion.1), channel_id=2, replica_groups=mesh['vp'=4,'cp'=8,'ga'=8] {'vp'}, dimensions={0}, use_global_device_ids=true | all-gather | bytes 983040 | tf_op jit(solution)/shard_map/all_gather | solution.py:246
  15.3 4.4 %collective-permute-start.3 = (bf16[32,384]{1,0:T(8,128)(2,1)S(1)}, bf16[32,384]{1,0:T(8,128)(2,1)S(1)}, u32[]{:S(2)}, u32[]{:S(2)}) collective-permute-start(bf16[32,384]{1,0:T(8,128)(2,1)S(1)} %get-tuple-element.12), channel_id=1, source_target_pairs={{0,8},{8,0},{16,24},{24,16},{32,40},{40,32},{48,56},{56,48},{1,9},... | collective-permute-start | bytes 73736 | tf_op jit(solution)/shard_map/ppermute | solution.py:19
  19.6 0.8 collective-permute-done.3
  20.5 1.0 collective-permute-start.4
  21.5 2.8 %collective-permute-done.4 = bf16[32,384]{1,0:T(8,128)(2,1)S(1)} collective-permute-done((bf16[32,384]{1,0:T(8,128)(2,1)S(1)}, bf16[32,384]{1,0:T(8,128)(2,1)S(1)}, u32[]{:S(2)}, u32[]{:S(2)}) %collective-permute-start.4) | collective-permute-done | bytes 24608 | tf_op jit(solution)/shard_map/ppermute | solution.py:19
  24.4 3.9 %collective-permute-start.5 = (bf16[32,384]{1,0:T(8,128)(2,1)S(1)}, bf16[32,384]{1,0:T(8,128)(2,1)S(1)}, u32[]{:S(2)}, u32[]{:S(2)}) collective-permute-start(bf16[32,384]{1,0:T(8,128)(2,1)S(1)} %add.73), channel_id=1, source_target_pairs={{0,48},{8,56},{16,32},{24,40},{32,16},{40,24},{48,0},{56,8},{1,49}... | collective-permute-start | bytes 73736 | tf_op jit(solution)/shard_map/ppermute | solution.py:19
  28.2 1.2 collective-permute-done.5
  29.5 2.5 %collective-permute-start.6 = (bf16[32,384]{1,0:T(8,128)(2,1)S(1)}, bf16[32,384]{1,0:T(8,128)(2,1)S(1)}, u32[]{:S(2)}, u32[]{:S(2)}) collective-permute-start(bf16[32,384]{1,0:T(8,128)(2,1)S(1)} %add.74), channel_id=1, source_target_pairs={{0,8},{8,0},{16,24},{24,16},{32,40},{40,32},{48,56},{56,48},{1,9},... | collective-permute-start | bytes 73736 | tf_op jit(solution)/shard_map/ppermute | solution.py:19
  31.9 0.8 collective-permute-done.6
  32.8 1.7 %collective-permute-start.7 = (bf16[32,768]{1,0:T(8,128)(2,1)S(1)}, bf16[32,768]{1,0:T(8,128)(2,1)S(1)}, u32[]{:S(2)}, u32[]{:S(2)}) collective-permute-start(bf16[32,768]{1,0:T(8,128)(2,1)S(1)} %constant_dynamic-update-slice_fusion.near_ref), channel_id=1, source_target_pairs={{0,64},{64,0},{128,192},{192,128},{1,65},{65,1},{129,193},{193,129... | collective-permute-start | bytes 147464 | tf_op jit(solution)/shard_map/ppermute | solution.py:19
  34.5 1.5 collective-permute-done.7.next_ref
  36.0 2.8 %collective-permute-start.8 = (bf16[32,1536]{1,0:T(8,128)(2,1)S(1)}, bf16[32,1536]{1,0:T(8,128)(2,1)S(1)}, u32[]{:S(2)}, u32[]{:S(2)}) collective-permute-start(bf16[32,1536]{1,0:T(8,128)(2,1)S(1)} %pad_maximum_fusion.4), channel_id=1, source_target_pairs={{0,192},{64,128},{128,64},{192,0},{1,193},{65,129},{129,65},{193,1... | collective-permute-start | bytes 294920 | tf_op jit(solution)/shard_map/ppermute | solution.py:19
  38.9 1.8 %collective-permute-done.8.far_ref = bf16[32,1536]{1,0:T(8,128)(2,1)S(1)} collective-permute-done((bf16[32,1536]{1,0:T(8,128)(2,1)S(1)}, bf16[32,1536]{1,0:T(8,128)(2,1)S(1)}, u32[]{:S(2)}, u32[]{:S(2)}) %collective-permute-start.8) | collective-permute-done | bytes 98336 | tf_op jit(solution)/shard_map/ppermute | solution.py:19
  41.4 1.3 multiply_convert_fusion.1
  42.7 1.7 %multiply_convert_fusion = bf16[8,2,8,8,3072]{4,3,2,1,0:T(8,128)(2,1)S(1)} fusion(f32[8,8,3072]{2,1,0:T(8,128)S(1)} %convert.11, f32[2,8,3072]{2,1,0:T(8,128)S(1)} %get-tuple-element.17), kind=kLoop, calls=%fused_computation | loop fusion | flops 6291456 | bytes 7274496 | tf_op jit(solution)/shard_map/convert_element_type | solution.py:257
  44.3 1.9 %fusion.4 = bf16[256,1024]{1,0:T(8,128)(2,1)S(1)} fusion(bf16[1024,3072]{1,0:T(8,128)(2,1)S(1)} %bitcast.63, bf16[3072,1024]{1,0:T(8,128)(2,1)S(1)} %bitcast.61, s32[]{:T(128)S(6)} %select_n.56), kind=kOutput, calls=%fused_computation.9 | convolution fusion | flops 1610874880 | bytes 8388612 | tf_op jit(solution)/shard_map/dot_general | solution.py:258
  46.2 1.9 %fusion.7 = bf16[256,1024]{1,0:T(8,128)(2,1)S(1)} fusion(bf16[1024,3072]{1,0:T(8,128)(2,1)S(1)} %bitcast.62, bf16[3072,1024]{1,0:T(8,128)(2,1)S(1)} %bitcast.61, s32[]{:T(128)S(6)} %select_n.56), kind=kOutput, calls=%fused_computation.10 | convolution fusion | flops 1610874880 | bytes 8388612 | tf_op jit(solution)/shard_map/dot_general | solution.py:258
  48.4 1.0 fusion.10
  49.6 1.2 pad_maximum_fusion
  50.8 4.6 %all-to-all-start = ((bf16[8,32,2560]{2,1,0:T(8,128)(2,1)}), bf16[8,32,2560]{2,1,0:T(8,128)(2,1)S(1)}, u32[]{:S(2)}, u32[]{:S(2)}) async-start(bf16[8,32,2560]{2,1,0:T(8,128)(2,1)} %pad_maximum_fusion), calls=%async_computation | async-start | bytes 2621440 | tf_op jit(solution)/shard_map/all_to_all | solution.py:277
  56.4 0.8 dynamic_slice.15
  57.2 1.9 %collective-permute-start.12 = (bf16[4,32,768]{2,1,0:T(8,128)(2,1)S(1)}, bf16[4,32,768]{2,1,0:T(8,128)(2,1)S(1)}, u32[]{:S(2)}, u32[]{:S(2)}) collective-permute-start(bf16[4,32,768]{2,1,0:T(8,128)(2,1)S(1)} %get-tuple-element.14.refs_0_), channel_id=1, source_target_pairs={{0,16},{8,24},{16,32},{24,40},{32,48},{40,56},{48,0},{56,8},{1,17}... | collective-permute-start | bytes 589832 | tf_op jit(solution)/shard_map/ppermute | solution.py:19
  59.1 4.2 %collective-permute-start.13 = (bf16[4,32,768]{2,1,0:T(8,128)(2,1)S(1)}, bf16[4,32,768]{2,1,0:T(8,128)(2,1)S(1)}, u32[]{:S(2)}, u32[]{:S(2)}) collective-permute-start(bf16[4,32,768]{2,1,0:T(8,128)(2,1)S(1)} %get-tuple-element.14.refs_0_), channel_id=1, source_target_pairs={{0,32},{8,40},{16,48},{24,56},{32,0},{40,8},{48,16},{56,24},{1,33}... | collective-permute-start | bytes 589832 | tf_op jit(solution)/shard_map/ppermute | solution.py:19
  63.4 2.5 %collective-permute-start.14 = (bf16[4,32,768]{2,1,0:T(8,128)(2,1)S(1)}, bf16[4,32,768]{2,1,0:T(8,128)(2,1)S(1)}, u32[]{:S(2)}, u32[]{:S(2)}) collective-permute-start(bf16[4,32,768]{2,1,0:T(8,128)(2,1)S(1)} %get-tuple-element.14.refs_0_), channel_id=1, source_target_pairs={{0,48},{8,56},{16,0},{24,8},{32,16},{40,24},{48,32},{56,40},{1,49}... | collective-permute-start | bytes 589832 | tf_op jit(solution)/shard_map/ppermute | solution.py:19
  65.9 3.5 %collective-permute-start.15 = (bf16[4,32,768]{2,1,0:T(8,128)(2,1)S(1)}, bf16[4,32,768]{2,1,0:T(8,128)(2,1)S(1)}, u32[]{:S(2)}, u32[]{:S(2)}) collective-permute-start(bf16[4,32,768]{2,1,0:T(8,128)(2,1)S(1)} %get-tuple-element.14.refs_0_), channel_id=1, source_target_pairs={{0,8},{8,0},{16,24},{24,16},{32,40},{40,32},{48,56},{56,48},{1,9},... | collective-permute-start | bytes 589832 | tf_op jit(solution)/shard_map/ppermute | solution.py:19
  69.4 11.0 %collective-permute-done.12.refs_1_ = bf16[4,32,768]{2,1,0:T(8,128)(2,1)S(1)} collective-permute-done((bf16[4,32,768]{2,1,0:T(8,128)(2,1)S(1)}, bf16[4,32,768]{2,1,0:T(8,128)(2,1)S(1)}, u32[]{:S(2)}, u32[]{:S(2)}) %collective-permute-start.12) | collective-permute-done | bytes 196640 | tf_op jit(solution)/shard_map/ppermute | solution.py:19
  80.4 7.4 %collective-permute-start.16 = (bf16[4,32,768]{2,1,0:T(8,128)(2,1)S(1)}, bf16[4,32,768]{2,1,0:T(8,128)(2,1)S(1)}, u32[]{:S(2)}, u32[]{:S(2)}) collective-permute-start(bf16[4,32,768]{2,1,0:T(8,128)(2,1)S(1)} %collective-permute-done.12.refs_1_), channel_id=1, source_target_pairs={{0,8},{8,0},{16,24},{24,16},{32,40},{40,32},{48,56},{56,48},{1,9},... | collective-permute-start | bytes 589832 | tf_op jit(solution)/shard_map/ppermute | solution.py:19
  87.8 3.3 %collective-permute-start.17 = (bf16[4,32,768]{2,1,0:T(8,128)(2,1)S(1)}, bf16[4,32,768]{2,1,0:T(8,128)(2,1)S(1)}, u32[]{:S(2)}, u32[]{:S(2)}) collective-permute-start(bf16[4,32,768]{2,1,0:T(8,128)(2,1)S(1)} %collective-permute-done.13.refs_2_), channel_id=1, source_target_pairs={{0,8},{8,0},{16,24},{24,16},{32,40},{40,32},{48,56},{56,48},{1,9},... | collective-permute-start | bytes 589832 | tf_op jit(solution)/shard_map/ppermute | solution.py:19
  91.6 2.7 %collective-permute-done.9 = bf16[1,32,512]{2,1,0:T(8,128)(2,1)S(1)} collective-permute-done((bf16[1,32,512]{2,1,0:T(8,128)(2,1)S(1)}, bf16[1,32,512]{2,1,0:T(8,128)(2,1)S(1)}, u32[]{:S(2)}, u32[]{:S(2)}) %collective-permute-start.9) | collective-permute-done | bytes 32800 | tf_op jit(solution)/shard_map/ppermute | solution.py:19
  94.4 1.7 %collective-permute-start.10 = (bf16[2,32,512]{2,1,0:T(8,128)(2,1)S(1)}, bf16[2,32,512]{2,1,0:T(8,128)(2,1)S(1)}, u32[]{:S(2)}, u32[]{:S(2)}) collective-permute-start(bf16[2,32,512]{2,1,0:T(8,128)(2,1)S(1)} %pad_maximum_fusion.5), channel_id=1, source_target_pairs={{0,2},{1,3},{2,0},{3,1},{4,6},{5,7},{6,4},{7,5},{8,10},{9,11},{10,... | collective-permute-start | bytes 196616 | tf_op jit(solution)/shard_map/ppermute | solution.py:19
  96.6 1.1 collective-permute-done.10
  97.7 2.1 %collective-permute-start.18 = (bf16[4,32,768]{2,1,0:T(8,128)(2,1)S(1)}, bf16[4,32,768]{2,1,0:T(8,128)(2,1)S(1)}, u32[]{:S(2)}, u32[]{:S(2)}) collective-permute-start(bf16[4,32,768]{2,1,0:T(8,128)(2,1)S(1)} %collective-permute-done.14.refs_3_), channel_id=1, source_target_pairs={{0,8},{8,0},{16,24},{24,16},{32,40},{40,32},{48,56},{56,48},{1,9},... | collective-permute-start | bytes 589832 | tf_op jit(solution)/shard_map/ppermute | solution.py:19
  100.0 2.1 %collective-permute-start.1 = (s32[6]{0:T(128)S(1)}, s32[6]{0:T(128)S(1)}, u32[]{:S(2)}, u32[]{:S(2)}) collective-permute-start(s32[6]{0:T(128)S(1)} %copy-done.2), channel_id=1, source_target_pairs={{0,128},{64,192},{128,0},{192,64},{1,129},{65,193},{129,1},{193,65... | collective-permute-start | bytes 80 | tf_op jit(solution)/shard_map/ppermute | solution.py:19
  102.1 1.8 %collective-permute-done.1 = s32[6]{0:T(128)S(1)} collective-permute-done((s32[6]{0:T(128)S(1)}, s32[6]{0:T(128)S(1)}, u32[]{:S(2)}, u32[]{:S(2)}) %collective-permute-start.1) | collective-permute-done | bytes 56 | tf_op jit(solution)/shard_map/ppermute | solution.py:19
  103.9 2.9 %collective-permute-start.2 = (s32[6]{0:T(128)S(1)}, s32[6]{0:T(128)S(1)}, u32[]{:S(2)}, u32[]{:S(2)}) collective-permute-start(s32[6]{0:T(128)S(1)} %copy-done.2), channel_id=1, source_target_pairs={{0,192},{64,0},{128,64},{192,128},{1,193},{65,1},{129,65},{193,129... | collective-permute-start | bytes 80 | tf_op jit(solution)/shard_map/ppermute | solution.py:19
  107.5 2.9 %collective-permute-start.19 = (bf16[2,32,1024]{2,1,0:T(8,128)(2,1)S(1)}, bf16[2,32,1024]{2,1,0:T(8,128)(2,1)S(1)}, u32[]{:S(2)}, u32[]{:S(2)}) collective-permute-start(bf16[2,32,1024]{2,1,0:T(8,128)(2,1)S(1)} %pad_maximum_fusion.3.refs_0_), channel_id=1, source_target_pairs={{0,16},{8,24},{16,32},{24,40},{32,48},{40,56},{48,0},{56,8},{1,17}... | collective-permute-start | bytes 393224 | tf_op jit(solution)/shard_map/ppermute | solution.py:19
  110.4 1.2 collective-permute-start.20
  111.7 2.1 %collective-permute-start.21 = (bf16[2,32,1024]{2,1,0:T(8,128)(2,1)S(1)}, bf16[2,32,1024]{2,1,0:T(8,128)(2,1)S(1)}, u32[]{:S(2)}, u32[]{:S(2)}) collective-permute-start(bf16[2,32,1024]{2,1,0:T(8,128)(2,1)S(1)} %pad_maximum_fusion.3.refs_0_), channel_id=1, source_target_pairs={{0,48},{8,56},{16,0},{24,8},{32,16},{40,24},{48,32},{56,40},{1,49}... | collective-permute-start | bytes 393224 | tf_op jit(solution)/shard_map/ppermute | solution.py:19
  113.7 2.8 %collective-permute-start.11 = (bf16[4,32,512]{2,1,0:T(8,128)(2,1)S(1)}, bf16[4,32,512]{2,1,0:T(8,128)(2,1)S(1)}, u32[]{:S(2)}, u32[]{:S(2)}) collective-permute-start(bf16[4,32,512]{2,1,0:T(8,128)(2,1)S(1)} %pad_maximum_fusion.2.near_ref), channel_id=1, source_target_pairs={{0,6},{1,7},{2,4},{3,5},{4,2},{5,3},{6,0},{7,1},{8,14},{9,15},{10,... | collective-permute-start | bytes 393224 | tf_op jit(solution)/shard_map/ppermute | solution.py:19
  116.6 1.5 %constant_dynamic-slice_fusion.basis_ref = bf16[768,1024]{1,0:T(8,128)(2,1)S(1)} fusion(bf16[3072,1024]{1,0:T(8,128)(2,1)} %param.9, s32[]{:T(128)S(6)} %select_n.55), kind=kLoop, calls=%fused_computation.65 | loop fusion | bytes 3145732 | tf_op jit(solution)/shard_map/dynamic_slice | solution.py:294
  118.1 3.4 %collective-permute-start.22 = (bf16[2,32,1024]{2,1,0:T(8,128)(2,1)S(1)}, bf16[2,32,1024]{2,1,0:T(8,128)(2,1)S(1)}, u32[]{:S(2)}, u32[]{:S(2)}) collective-permute-start(bf16[2,32,1024]{2,1,0:T(8,128)(2,1)S(1)} %pad_maximum_fusion.3.refs_0_), channel_id=1, source_target_pairs={{0,8},{8,0},{16,24},{24,16},{32,40},{40,32},{48,56},{56,48},{1,9},... | collective-permute-start | bytes 393224 | tf_op jit(solution)/shard_map/ppermute | solution.py:19
  121.6 1.0 collective-permute-done.20.refs_2_
  122.6 2.9 %collective-permute-start.24 = (bf16[2,32,1024]{2,1,0:T(8,128)(2,1)S(1)}, bf16[2,32,1024]{2,1,0:T(8,128)(2,1)S(1)}, u32[]{:S(2)}, u32[]{:S(2)}) collective-permute-start(bf16[2,32,1024]{2,1,0:T(8,128)(2,1)S(1)} %collective-permute-done.20.refs_2_), channel_id=1, source_target_pairs={{0,8},{8,0},{16,24},{24,16},{32,40},{40,32},{48,56},{56,48},{1,9},... | collective-permute-start | bytes 393224 | tf_op jit(solution)/shard_map/ppermute | solution.py:19
  125.7 2.5 %shard_map.75.exchange_ref = f32[24,16,512]{2,1,0:T(8,128)S(1)} custom-call(s32[3]{0:T(128)S(1)} %pad_add_fusion.1.meta_ref, s32[4,6]{1,0:T(4,128)S(1)} %pad_add_fusion.ids_ref, bf16[768,1024]{1,0:T(8,128)(2,1)S(1)} %constant_dynamic-slice_fusion.basis_ref, bf16[4,32,512]{2,1,0:T(8,128)(2,1)S(1)} %pad_maximum_fusion.2.near_ref, ...), custom_call_target="tpu_custom_call" | custom-call | flops 301989888 | bytes 4194304 | tf_op jit(solution)/shard_map/pallas_call | solution.py:142
  128.2 2.8 %shard_map.76 = bf16[32,12,512]{2,1,0:T(8,128)(2,1)} custom-call(s32[3]{0:T(128)S(1)} %pad_add_fusion.1.meta_ref, s32[4,6]{1,0:T(4,128)S(1)} %pad_add_fusion.ids_ref, bf16[512,512]{1,0:T(8,128)(2,1)S(1)} %fusion.11.order_ref, f32[24,16,512]{2,1,0:T(8,128)S(1)} %shard_map.75.exchange_ref, bf16[2,32,1024]{2,1,0:T(8,128)(2,1)S(1)} %pad_maximum_fusion.3.refs_0_, ...), custom_call_target="tpu_custom_call" | custom-call | tf_op jit(solution)/shard_map/pallas_call | solution.py:210
  131.0 7.3 %all-to-all-start.1 = ((bf16[32,12,512]{2,1,0:T(8,128)(2,1)}), bf16[32,12,512]{2,1,0:T(8,128)(2,1)S(1)}, u32[]{:S(2)}, u32[]{:S(2)}) async-start(bf16[32,12,512]{2,1,0:T(8,128)(2,1)} %shard_map.76), calls=%async_computation.1 | async-start | bytes 1048576 | tf_op jit(solution)/shard_map/all_to_all | solution.py:301
  138.4 11.7 %all-to-all-done.1 = bf16[32,12,512]{2,1,0:T(8,128)(2,1)S(1)} async-done(((bf16[32,12,512]{2,1,0:T(8,128)(2,1)}), bf16[32,12,512]{2,1,0:T(8,128)(2,1)S(1)}, u32[]{:S(2)}, u32[]{:S(2)}) %all-to-all-start.1) | async-done | bytes 393248 | tf_op jit(solution)/shard_map/all_to_all | solution.py:301
  (67 shorter events, 6.9 us)
Async XLA Ops:
  14.0 0.7 copy-start
  15.3 5.2 %collective-permute-start.3 = (bf16[32,384]{1,0:T(8,128)(2,1)S(1)}, bf16[32,384]{1,0:T(8,128)(2,1)S(1)}, u32[]{:S(2)}, u32[]{:S(2)}) collective-permute-start(bf16[32,384]{1,0:T(8,128)(2,1)S(1)} %get-tuple-element.12), channel_id=1, source_target_pairs={{0,8},{8,0},{16,24},{24,16},{32,40},{40,32},{48,56},{56,48},{1,9},... | collective-permute-start | bytes 73736 | tf_op jit(solution)/shard_map/ppermute | solution.py:19
  20.5 3.9 %collective-permute-start.4 = (bf16[32,384]{1,0:T(8,128)(2,1)S(1)}, bf16[32,384]{1,0:T(8,128)(2,1)S(1)}, u32[]{:S(2)}, u32[]{:S(2)}) collective-permute-start(bf16[32,384]{1,0:T(8,128)(2,1)S(1)} %add.72), channel_id=1, source_target_pairs={{0,16},{8,24},{16,0},{24,8},{32,48},{40,56},{48,32},{56,40},{1,17}... | collective-permute-start | bytes 73736 | tf_op jit(solution)/shard_map/ppermute | solution.py:19
  24.4 5.1 %collective-permute-start.5 = (bf16[32,384]{1,0:T(8,128)(2,1)S(1)}, bf16[32,384]{1,0:T(8,128)(2,1)S(1)}, u32[]{:S(2)}, u32[]{:S(2)}) collective-permute-start(bf16[32,384]{1,0:T(8,128)(2,1)S(1)} %add.73), channel_id=1, source_target_pairs={{0,48},{8,56},{16,32},{24,40},{32,16},{40,24},{48,0},{56,8},{1,49}... | collective-permute-start | bytes 73736 | tf_op jit(solution)/shard_map/ppermute | solution.py:19
  29.5 3.3 %collective-permute-start.6 = (bf16[32,384]{1,0:T(8,128)(2,1)S(1)}, bf16[32,384]{1,0:T(8,128)(2,1)S(1)}, u32[]{:S(2)}, u32[]{:S(2)}) collective-permute-start(bf16[32,384]{1,0:T(8,128)(2,1)S(1)} %add.74), channel_id=1, source_target_pairs={{0,8},{8,0},{16,24},{24,16},{32,40},{40,32},{48,56},{56,48},{1,9},... | collective-permute-start | bytes 73736 | tf_op jit(solution)/shard_map/ppermute | solution.py:19
  32.8 3.2 %collective-permute-start.7 = (bf16[32,768]{1,0:T(8,128)(2,1)S(1)}, bf16[32,768]{1,0:T(8,128)(2,1)S(1)}, u32[]{:S(2)}, u32[]{:S(2)}) collective-permute-start(bf16[32,768]{1,0:T(8,128)(2,1)S(1)} %constant_dynamic-update-slice_fusion.near_ref), channel_id=1, source_target_pairs={{0,64},{64,0},{128,192},{192,128},{1,65},{65,1},{129,193},{193,129... | collective-permute-start | bytes 147464 | tf_op jit(solution)/shard_map/ppermute | solution.py:19
  36.0 4.8 %collective-permute-start.8 = (bf16[32,1536]{1,0:T(8,128)(2,1)S(1)}, bf16[32,1536]{1,0:T(8,128)(2,1)S(1)}, u32[]{:S(2)}, u32[]{:S(2)}) collective-permute-start(bf16[32,1536]{1,0:T(8,128)(2,1)S(1)} %pad_maximum_fusion.4), channel_id=1, source_target_pairs={{0,192},{64,128},{128,64},{192,0},{1,193},{65,129},{129,65},{193,1... | collective-permute-start | bytes 294920 | tf_op jit(solution)/shard_map/ppermute | solution.py:19
  41.3 3.0 %slice-start = ((s8[6291456]{0:T(1024)(128)(4,1)}), s8[4194304]{0:T(1024)(128)(4,1)S(1)}, s32[]{:S(2)}) async-start(s8[6291456]{0:T(1024)(128)(4,1)} %bitcast.60), calls=%async_computation.2 | async-start | bytes 8388608
  41.4 3.0 %slice-start.1 = ((s8[6291456]{0:T(1024)(128)(4,1)}), s8[2097152]{0:T(1024)(128)(4,1)S(1)}, s32[]{:S(2)}) async-start(s8[6291456]{0:T(1024)(128)(4,1)} %bitcast.60), calls=%async_computation.3 | async-start | bytes 4194304
  49.4 46.7 %copy-start.2 = (s32[6]{0:T(128)S(1)}, s32[6]{0:T(128)}, u32[]{:S(2)}) copy-start(s32[6]{0:T(128)} %param.13) | copy-start | bytes 76
  50.8 40.3 %all-to-all-start = ((bf16[8,32,2560]{2,1,0:T(8,128)(2,1)}), bf16[8,32,2560]{2,1,0:T(8,128)(2,1)S(1)}, u32[]{:S(2)}, u32[]{:S(2)}) async-start(bf16[8,32,2560]{2,1,0:T(8,128)(2,1)} %pad_maximum_fusion), calls=%async_computation | async-start | bytes 2621440 | tf_op jit(solution)/shard_map/all_to_all | solution.py:277
  57.2 23.2 %collective-permute-start.12 = (bf16[4,32,768]{2,1,0:T(8,128)(2,1)S(1)}, bf16[4,32,768]{2,1,0:T(8,128)(2,1)S(1)}, u32[]{:S(2)}, u32[]{:S(2)}) collective-permute-start(bf16[4,32,768]{2,1,0:T(8,128)(2,1)S(1)} %get-tuple-element.14.refs_0_), channel_id=1, source_target_pairs={{0,16},{8,24},{16,32},{24,40},{32,48},{40,56},{48,0},{56,8},{1,17}... | collective-permute-start | bytes 589832 | tf_op jit(solution)/shard_map/ppermute | solution.py:19
  59.1 28.8 %collective-permute-start.13 = (bf16[4,32,768]{2,1,0:T(8,128)(2,1)S(1)}, bf16[4,32,768]{2,1,0:T(8,128)(2,1)S(1)}, u32[]{:S(2)}, u32[]{:S(2)}) collective-permute-start(bf16[4,32,768]{2,1,0:T(8,128)(2,1)S(1)} %get-tuple-element.14.refs_0_), channel_id=1, source_target_pairs={{0,32},{8,40},{16,48},{24,56},{32,0},{40,8},{48,16},{56,24},{1,33}... | collective-permute-start | bytes 589832 | tf_op jit(solution)/shard_map/ppermute | solution.py:19
  63.4 32.7 %collective-permute-start.14 = (bf16[4,32,768]{2,1,0:T(8,128)(2,1)S(1)}, bf16[4,32,768]{2,1,0:T(8,128)(2,1)S(1)}, u32[]{:S(2)}, u32[]{:S(2)}) collective-permute-start(bf16[4,32,768]{2,1,0:T(8,128)(2,1)S(1)} %get-tuple-element.14.refs_0_), channel_id=1, source_target_pairs={{0,48},{8,56},{16,0},{24,8},{32,16},{40,24},{48,32},{56,40},{1,49}... | collective-permute-start | bytes 589832 | tf_op jit(solution)/shard_map/ppermute | solution.py:19
  65.9 44.5 %collective-permute-start.15 = (bf16[4,32,768]{2,1,0:T(8,128)(2,1)S(1)}, bf16[4,32,768]{2,1,0:T(8,128)(2,1)S(1)}, u32[]{:S(2)}, u32[]{:S(2)}) collective-permute-start(bf16[4,32,768]{2,1,0:T(8,128)(2,1)S(1)} %get-tuple-element.14.refs_0_), channel_id=1, source_target_pairs={{0,8},{8,0},{16,24},{24,16},{32,40},{40,32},{48,56},{56,48},{1,9},... | collective-permute-start | bytes 589832 | tf_op jit(solution)/shard_map/ppermute | solution.py:19
  80.4 31.3 %collective-permute-start.16 = (bf16[4,32,768]{2,1,0:T(8,128)(2,1)S(1)}, bf16[4,32,768]{2,1,0:T(8,128)(2,1)S(1)}, u32[]{:S(2)}, u32[]{:S(2)}) collective-permute-start(bf16[4,32,768]{2,1,0:T(8,128)(2,1)S(1)} %collective-permute-done.12.refs_1_), channel_id=1, source_target_pairs={{0,8},{8,0},{16,24},{24,16},{32,40},{40,32},{48,56},{56,48},{1,9},... | collective-permute-start | bytes 589832 | tf_op jit(solution)/shard_map/ppermute | solution.py:19
  87.8 25.9 %collective-permute-start.17 = (bf16[4,32,768]{2,1,0:T(8,128)(2,1)S(1)}, bf16[4,32,768]{2,1,0:T(8,128)(2,1)S(1)}, u32[]{:S(2)}, u32[]{:S(2)}) collective-permute-start(bf16[4,32,768]{2,1,0:T(8,128)(2,1)S(1)} %collective-permute-done.13.refs_2_), channel_id=1, source_target_pairs={{0,8},{8,0},{16,24},{24,16},{32,40},{40,32},{48,56},{56,48},{1,9},... | collective-permute-start | bytes 589832 | tf_op jit(solution)/shard_map/ppermute | solution.py:19
  91.3 47.1 %copy-start.1 = (s32[2]{0:T(128)S(1)}, s32[2]{0:T(128)}, u32[]{:S(2)}) copy-start(s32[2]{0:T(128)} %window_ref.1) | copy-start | bytes 28
  91.5 2.9 %collective-permute-start.9 = (bf16[1,32,512]{2,1,0:T(8,128)(2,1)S(1)}, bf16[1,32,512]{2,1,0:T(8,128)(2,1)S(1)}, u32[]{:S(2)}, u32[]{:S(2)}) collective-permute-start(bf16[1,32,512]{2,1,0:T(8,128)(2,1)S(1)} %fusion.18), channel_id=1, source_target_pairs={{0,1},{1,0},{2,3},{3,2},{4,5},{5,4},{6,7},{7,6},{8,9},{9,8},{10,11... | collective-permute-start | bytes 98312 | tf_op jit(solution)/shard_map/ppermute | solution.py:19
  94.4 3.4 %collective-permute-start.10 = (bf16[2,32,512]{2,1,0:T(8,128)(2,1)S(1)}, bf16[2,32,512]{2,1,0:T(8,128)(2,1)S(1)}, u32[]{:S(2)}, u32[]{:S(2)}) collective-permute-start(bf16[2,32,512]{2,1,0:T(8,128)(2,1)S(1)} %pad_maximum_fusion.5), channel_id=1, source_target_pairs={{0,2},{1,3},{2,0},{3,1},{4,6},{5,7},{6,4},{7,5},{8,10},{9,11},{10,... | collective-permute-start | bytes 196616 | tf_op jit(solution)/shard_map/ppermute | solution.py:19
  96.1 3.9 %collective-permute-start = (s32[6]{0:T(128)S(1)}, s32[6]{0:T(128)S(1)}, u32[]{:S(2)}, u32[]{:S(2)}) collective-permute-start(s32[6]{0:T(128)S(1)} %copy-done.2), channel_id=1, source_target_pairs={{0,64},{64,128},{128,192},{192,0},{1,65},{65,129},{129,193},{193,1... | collective-permute-start | bytes 80 | tf_op jit(solution)/shard_map/ppermute | solution.py:19
  97.7 20.4 %collective-permute-start.18 = (bf16[4,32,768]{2,1,0:T(8,128)(2,1)S(1)}, bf16[4,32,768]{2,1,0:T(8,128)(2,1)S(1)}, u32[]{:S(2)}, u32[]{:S(2)}) collective-permute-start(bf16[4,32,768]{2,1,0:T(8,128)(2,1)S(1)} %collective-permute-done.14.refs_3_), channel_id=1, source_target_pairs={{0,8},{8,0},{16,24},{24,16},{32,40},{40,32},{48,56},{56,48},{1,9},... | collective-permute-start | bytes 589832 | tf_op jit(solution)/shard_map/ppermute | solution.py:19
  100.0 3.9 %collective-permute-start.1 = (s32[6]{0:T(128)S(1)}, s32[6]{0:T(128)S(1)}, u32[]{:S(2)}, u32[]{:S(2)}) collective-permute-start(s32[6]{0:T(128)S(1)} %copy-done.2), channel_id=1, source_target_pairs={{0,128},{64,192},{128,0},{192,64},{1,129},{65,193},{129,1},{193,65... | collective-permute-start | bytes 80 | tf_op jit(solution)/shard_map/ppermute | solution.py:19
  103.9 3.6 %collective-permute-start.2 = (s32[6]{0:T(128)S(1)}, s32[6]{0:T(128)S(1)}, u32[]{:S(2)}, u32[]{:S(2)}) collective-permute-start(s32[6]{0:T(128)S(1)} %copy-done.2), channel_id=1, source_target_pairs={{0,192},{64,0},{128,64},{192,128},{1,193},{65,1},{129,65},{193,129... | collective-permute-start | bytes 80 | tf_op jit(solution)/shard_map/ppermute | solution.py:19
  107.5 14.0 %collective-permute-start.19 = (bf16[2,32,1024]{2,1,0:T(8,128)(2,1)S(1)}, bf16[2,32,1024]{2,1,0:T(8,128)(2,1)S(1)}, u32[]{:S(2)}, u32[]{:S(2)}) collective-permute-start(bf16[2,32,1024]{2,1,0:T(8,128)(2,1)S(1)} %pad_maximum_fusion.3.refs_0_), channel_id=1, source_target_pairs={{0,16},{8,24},{16,32},{24,40},{32,48},{40,56},{48,0},{56,8},{1,17}... | collective-permute-start | bytes 393224 | tf_op jit(solution)/shard_map/ppermute | solution.py:19
  110.4 12.1 %collective-permute-start.20 = (bf16[2,32,1024]{2,1,0:T(8,128)(2,1)S(1)}, bf16[2,32,1024]{2,1,0:T(8,128)(2,1)S(1)}, u32[]{:S(2)}, u32[]{:S(2)}) collective-permute-start(bf16[2,32,1024]{2,1,0:T(8,128)(2,1)S(1)} %pad_maximum_fusion.3.refs_0_), channel_id=1, source_target_pairs={{0,32},{8,40},{16,48},{24,56},{32,0},{40,8},{48,16},{56,24},{1,33}... | collective-permute-start | bytes 393224 | tf_op jit(solution)/shard_map/ppermute | solution.py:19
  111.7 13.8 %collective-permute-start.21 = (bf16[2,32,1024]{2,1,0:T(8,128)(2,1)S(1)}, bf16[2,32,1024]{2,1,0:T(8,128)(2,1)S(1)}, u32[]{:S(2)}, u32[]{:S(2)}) collective-permute-start(bf16[2,32,1024]{2,1,0:T(8,128)(2,1)S(1)} %pad_maximum_fusion.3.refs_0_), channel_id=1, source_target_pairs={{0,48},{8,56},{16,0},{24,8},{32,16},{40,24},{48,32},{56,40},{1,49}... | collective-permute-start | bytes 393224 | tf_op jit(solution)/shard_map/ppermute | solution.py:19
  113.7 11.9 %collective-permute-start.11 = (bf16[4,32,512]{2,1,0:T(8,128)(2,1)S(1)}, bf16[4,32,512]{2,1,0:T(8,128)(2,1)S(1)}, u32[]{:S(2)}, u32[]{:S(2)}) collective-permute-start(bf16[4,32,512]{2,1,0:T(8,128)(2,1)S(1)} %pad_maximum_fusion.2.near_ref), channel_id=1, source_target_pairs={{0,6},{1,7},{2,4},{3,5},{4,2},{5,3},{6,0},{7,1},{8,14},{9,15},{10,... | collective-permute-start | bytes 393224 | tf_op jit(solution)/shard_map/ppermute | solution.py:19
  118.1 10.1 %collective-permute-start.22 = (bf16[2,32,1024]{2,1,0:T(8,128)(2,1)S(1)}, bf16[2,32,1024]{2,1,0:T(8,128)(2,1)S(1)}, u32[]{:S(2)}, u32[]{:S(2)}) collective-permute-start(bf16[2,32,1024]{2,1,0:T(8,128)(2,1)S(1)} %pad_maximum_fusion.3.refs_0_), channel_id=1, source_target_pairs={{0,8},{8,0},{16,24},{24,16},{32,40},{40,32},{48,56},{56,48},{1,9},... | collective-permute-start | bytes 393224 | tf_op jit(solution)/shard_map/ppermute | solution.py:19
  121.5 6.8 %collective-permute-start.23 = (bf16[2,32,1024]{2,1,0:T(8,128)(2,1)S(1)}, bf16[2,32,1024]{2,1,0:T(8,128)(2,1)S(1)}, u32[]{:S(2)}, u32[]{:S(2)}) collective-permute-start(bf16[2,32,1024]{2,1,0:T(8,128)(2,1)S(1)} %collective-permute-done.19.refs_1_), channel_id=1, source_target_pairs={{0,8},{8,0},{16,24},{24,16},{32,40},{40,32},{48,56},{56,48},{1,9},... | collective-permute-start | bytes 393224 | tf_op jit(solution)/shard_map/ppermute | solution.py:19
  122.6 5.6 %collective-permute-start.24 = (bf16[2,32,1024]{2,1,0:T(8,128)(2,1)S(1)}, bf16[2,32,1024]{2,1,0:T(8,128)(2,1)S(1)}, u32[]{:S(2)}, u32[]{:S(2)}) collective-permute-start(bf16[2,32,1024]{2,1,0:T(8,128)(2,1)S(1)} %collective-permute-done.20.refs_2_), channel_id=1, source_target_pairs={{0,8},{8,0},{16,24},{24,16},{32,40},{40,32},{48,56},{56,48},{1,9},... | collective-permute-start | bytes 393224 | tf_op jit(solution)/shard_map/ppermute | solution.py:19
  125.5 2.8 %collective-permute-start.25 = (bf16[2,32,1024]{2,1,0:T(8,128)(2,1)S(1)}, bf16[2,32,1024]{2,1,0:T(8,128)(2,1)S(1)}, u32[]{:S(2)}, u32[]{:S(2)}) collective-permute-start(bf16[2,32,1024]{2,1,0:T(8,128)(2,1)S(1)} %collective-permute-done.21.refs_3_), channel_id=1, source_target_pairs={{0,8},{8,0},{16,24},{24,16},{32,40},{40,32},{48,56},{56,48},{1,9},... | collective-permute-start | bytes 393224 | tf_op jit(solution)/shard_map/ppermute | solution.py:19
  131.0 19.1 %all-to-all-start.1 = ((bf16[32,12,512]{2,1,0:T(8,128)(2,1)}), bf16[32,12,512]{2,1,0:T(8,128)(2,1)S(1)}, u32[]{:S(2)}, u32[]{:S(2)}) async-start(bf16[32,12,512]{2,1,0:T(8,128)(2,1)} %shard_map.76), calls=%async_computation.1 | async-start | bytes 1048576 | tf_op jit(solution)/shard_map/all_to_all | solution.py:301

commit v4 on v3

--- a/solution.py
+++ b/solution.py
@@ -49,13 +49,13 @@
     for n, flip in enumerate((0, 1, 3, 2)):
         for half in range(2):
             start = (i ^ flip) * 2 + (j + half) % 2
-            ref, at = ((near_ref, 0), (next_ref, 0), (far_ref, 0), (far_ref, 2))[n]
-            at = (at + half) * width
+            ref = (near_ref, next_ref, far_ref, far_ref)[n]
+            at = half * width + (near_ref.shape[1] if n == 3 else 0)
             first = pl.multiple_of(start * width, 128)
             out_ref[:, pl.ds(first, width)] = ref[:, at : at + width]
 
 
-def row_tiles(meta, window_rows, columns):
+def row_tiles(meta, window_rows, columns, tile_owner):
     width = columns.shape[2] // 8
     smem, vmem = (pl.BlockSpec(memory_space=m) for m in (pltpu.SMEM, pltpu.VMEM))
     part = jax.ShapeDtypeStruct((32, width), BF16)
@@ -70,7 +70,10 @@
     mine = mine + shift(mine, "cp", lambda n: n ^ 2)
     mine = mine + shift(mine, "cp", lambda n: n ^ 6)
     quarter, mine = lax.optimization_barrier((quarter, mine))
-    near = jnp.concatenate([mine, shift(mine, "cp", lambda n: n ^ 1)], axis=1)
+    slots = tile_owner.shape[0]
+    tiles = jnp.repeat(jnp.stack([tile_owner // NCT, tile_owner % NCT], axis=1), 64, axis=1)
+    tiles = jnp.pad(tiles, ((0, 32 - slots), (0, 0))).astype(BF16)
+    near = jnp.concatenate([mine, shift(mine, "cp", lambda n: n ^ 1), tiles], axis=1)
     beside = shift(near, "vp", lambda n: n ^ 1)
     far = shift(jnp.concatenate([near, beside], axis=1), "vp", lambda n: n ^ 3)
     rows = pl.pallas_call(
@@ -80,7 +83,10 @@
         out_specs=vmem,
         compiler_params=pltpu.CompilerParams(vmem_limit_bytes=16 * 2**20),
     )(meta, near, beside, far)
-    return rows, quarter
+    tiles = [near[:slots, -128:], beside[:slots, -128:]]
+    tiles += [far[:slots, near.shape[1] - 128 : near.shape[1]], far[:slots, -128:]]
+    tiles = jnp.stack(tiles).astype(jnp.int32)
+    return rows, quarter, tiles[:, :, 0] * NCT + tiles[:, :, 64]
 
 
 def pair_block(left, right):
@@ -90,27 +96,59 @@
 
 def owner_of(ids_ref, i, slot):
     own = ids_ref.shape[1]
-    return ids_ref[(i + 4 - slot // own) % 4, slot % own]
-
-
-def exchange_kernel(meta_ref, ids_ref, basis_ref, near_ref, far_ref, *refs):
-    pieces, (out_ref, waves_ref) = refs[:8], refs[8:]
-    i, j, k = meta_ref[0], meta_ref[1], meta_ref[2]
+    flip = i ^ (slot // own)
+    return ids_ref[flip ^ (flip // 2), slot % own]
+
+
+def sum_kernel(arrived_ref, scale_ref, proj_ref, row_ref):
+    total = arrived_ref[0].astype(F32)
+    for n in range(1, arrived_ref.shape[0]):
+        total = total + arrived_ref[n].astype(F32)
+    total = (total * scale_ref[...]).astype(BF16)
+    width = proj_ref.shape[2]
+    proj_ref[0] = total[:, :width]
+    proj_ref[1] = total[:, width : 2 * width]
+    for n in range(row_ref.shape[0]):
+        row_ref[n] = total[:, 2 * width :]
+
+
+def rank_sums(arrived, scale):
+    groups, ranks, width = arrived.shape
+    vmem = pl.BlockSpec(memory_space=pltpu.VMEM)
+    return pl.pallas_call(
+        sum_kernel,
+        out_shape=(
+            jax.ShapeDtypeStruct((2, ranks, 1024), BF16),
+            jax.ShapeDtypeStruct((groups, ranks, width - 2048), BF16),
+        ),
+        in_specs=[vmem, vmem],
+        out_specs=(vmem, vmem),
+        compiler_params=pltpu.CompilerParams(vmem_limit_bytes=16 * 2**20),
+    )(arrived, scale)
+
+
+def exchange_kernel(meta_ref, ids_ref, whole_ref, row_ref, *refs):
+    pieces, (out_ref, waves_ref, basis_ref, done_ref) = refs[:8], refs[8:]
+    i, j = meta_ref[0], meta_ref[1]
+    count = basis_ref.shape[0]
+    first = pl.multiple_of(i * count, count)
+    copy = pltpu.make_async_copy(whole_ref.at[pl.ds(first, count)], basis_ref, done_ref)
+    copy.start()
     together = 4
+    for flip in range(2):
+        for n in range(4):
+            source = ((j // 2 + 4 - n) % 4) * 2 + (j + flip) % 2
+            waves_ref[pl.ds(source * 4, 4)] = pieces[4 * flip + n][...]
+    copy.wait()
     potential = None
     for n in range(8):
-        source = k ^ (n % 2) ^ (n // 2 % 2 * 2) ^ (n // 4 * 6)
-        piece = near_ref[n] if n < 4 else far_ref[n - 4]
+        piece = row_ref[n]
         ranks = jnp.concatenate([piece[:, m * 128 : (m + 1) * 128] for m in range(4)], axis=0)
-        basis = basis_ref[:, pl.ds(pl.multiple_of(source * 128, 128), 128)]
+        basis = basis_ref[:, n * 128 : (n + 1) * 128]
         term = lax.dot_general(
             ranks, basis, (((0,), (1,)), ((), ())), preferred_element_type=F32
         )
         potential = term if potential is None else potential + term
-    for flip in range(2):
-        for n in range(4):
-            source = ((j // 2 + 4 - n) % 4) * 2 + (j + flip) % 2
-            waves_ref[pl.ds(source * 4, 4)] = pieces[4 * flip + n][...]
     potential = potential.astype(BF16)
 
     def band_rows(first, tile):
@@ -136,20 +174,24 @@
             )
 
 
-def exchange_tiles(meta, ids, basis_rows, near, far, pieces):
+def exchange_tiles(meta, ids, basis, row_sums, pieces):
     slots = 4 * ids.shape[1]
     smem, vmem = (pl.BlockSpec(memory_space=m) for m in (pltpu.SMEM, pltpu.VMEM))
     return pl.pallas_call(
         exchange_kernel,
         out_shape=jax.ShapeDtypeStruct((slots, 16, 512), F32),
-        in_specs=[smem, smem, vmem, vmem, vmem] + [vmem] * 8,
+        in_specs=[smem, smem, pl.BlockSpec(memory_space=pl.ANY), vmem] + [vmem] * 8,
         out_specs=vmem,
-        scratch_shapes=[pltpu.VMEM((32,) + pieces[0].shape[1:], BF16)],
+        scratch_shapes=[
+            pltpu.VMEM((32,) + pieces[0].shape[1:], BF16),
+            pltpu.VMEM((basis.shape[0] // 4, basis.shape[1]), BF16),
+            pltpu.SemaphoreType.DMA(()),
+        ],
         compiler_params=pltpu.CompilerParams(vmem_limit_bytes=32 * 2**20),
         cost_estimate=pl.CostEstimate(
             flops=2 * slots * 64 * 128 * 768, bytes_accessed=2**22, transcendentals=0
         ),
-    )(meta, ids, basis_rows, near, far, *pieces)
+    )(meta, ids, basis, row_sums, *pieces)
 
 
 def direct_kernel(meta_ref, ids_ref, order_ref, exchange_ref, *refs):
@@ -197,9 +239,10 @@
         total = 2.0 * exchange_ref[part * own : (part + 1) * own] - direct
         for n in range(own):
             for q in range(2):
-                total_ref[part * 8 : (part + 1) * 8, q * own + n, :] = total[
-                    n, q * 8 : (q + 1) * 8
-                ]
+                for block in range(4):
+                    total_ref[
+                        part * 8 : (part + 1) * 8, block * 2 * own + q * own + n, :
+                    ] = total[n, q * 8 : (q + 1) * 8, block * 128 : (block + 1) * 128]
     out_ref[...] = total_ref[...].astype(BF16)
 
 
@@ -209,23 +252,16 @@
     smem, vmem = (pl.BlockSpec(memory_space=m) for m in (pltpu.SMEM, pltpu.VMEM))
     return pl.pallas_call(
         direct_kernel,
-        out_shape=jax.ShapeDtypeStruct((32, 2 * own, 512), BF16),
+        out_shape=jax.ShapeDtypeStruct((32, 8 * own, 128), BF16),
         in_specs=[smem, smem, vmem, vmem] + [vmem] * 8,
         out_specs=vmem,
         scratch_shapes=[
             pltpu.VMEM((8,) + pieces[0].shape, BF16),
             pltpu.VMEM((slots, 16, 512), BF16),
-            pltpu.VMEM((32, 2 * own, 512), F32),
+            pltpu.VMEM((32, 8 * own, 128), F32),
         ],
         compiler_params=pltpu.CompilerParams(vmem_limit_bytes=32 * 2**20),
     )(meta, ids, order, exchange, *pieces)
-
-
-def gather_pieces(array, axis):
-    step = [array] + [
-        shift(array, axis, lambda n, s=s: (n + 2 * s) % 8) for s in (1, 2, 3)
-    ]
-    return step + [shift(a, axis, lambda n: n ^ 1) for a in step]
 
 
 def shards(valence_wavefunction, cond_wave, screen_basis, screen, coulomb, window_rows, tile_owner):
@@ -239,13 +275,12 @@
     rank_quarter = R // 4
     rank_part = rank_quarter // 8
 
-    ids = jnp.stack(
-        [tile_owner] + [shift(tile_owner, "vp", lambda n, s=s: (n + s) % 4) for s in (1, 2, 3)]
-    )
     waves = jnp.concatenate([valence_wavefunction, cond_wave], axis=0)
     columns = lax.all_gather(waves, "vp", axis=0)
-    rows, quarter_waves = row_tiles(meta, window_rows, columns)
-    wave_pieces = gather_pieces(quarter_waves, "cp")
+    rows, quarter_waves, ids = row_tiles(meta, window_rows, columns, tile_owner)
+    wave_pieces = [quarter_waves] + [
+        shift(quarter_waves, "cp", lambda n, s=s: (n + 2 * s) % 8) for s in (2, 1, 3)
+    ]
 
     row_val = rows[:16].reshape(2, TV, grid_count).astype(F32)
     row_cond = rows[16:].reshape(2, TC, grid_count).astype(F32)
@@ -274,32 +309,39 @@
         ],
         axis=2,
     )
-    arrived = lax.all_to_all(sent, "ga", split_axis=0, concat_axis=0, tiled=True)
-    summed = arrived.astype(F32).sum(axis=0)
-
+    sent, wave_pieces = lax.optimization_barrier((sent, wave_pieces))
+    wave_pieces = [wave_pieces[n] for n in (0, 2, 1, 3)]
+    wave_pieces = wave_pieces + [shift(a, "cp", lambda n: n ^ 1) for a in wave_pieces]
     screen_part = lax.dynamic_slice_in_dim(
         screen, i * rank_quarter + k * rank_part, rank_part, 0
     )
     coulomb_part = lax.dynamic_slice_in_dim(coulomb, k * (R // 8), R // 8, 0)
-    val_sum = (summed[:, :1024] * screen_part[:, None]).astype(BF16)
-    cond_sum = summed[:, 1024:2048].astype(BF16)
-    row_sum = summed[:, 2048:].reshape(rank_part, 4, 128)
-    row_sum = (row_sum * coulomb_part.reshape(4, rank_part).T[:, :, None]).astype(BF16)
-
-    proj_pieces = gather_pieces(jnp.stack([val_sum, cond_sum]), "cp")
-    near = row_sum.reshape(1, rank_part, 512)
-    for bits in (1, 2):
-        near = jnp.concatenate([near, shift(near, "ga", lambda n, bits=bits: n ^ bits)])
-    far = shift(near, "ga", lambda n: n ^ 6)
-    basis_rows = lax.dynamic_slice_in_dim(screen_basis, i * quarter, quarter, 0)
-    exchange = exchange_tiles(meta, ids, basis_rows, near, far, wave_pieces)
-
+    scale = jnp.concatenate(
+        [
+            jnp.broadcast_to(screen_part[:, None], (rank_part, 1024)),
+            jnp.ones((rank_part, 1024), F32),
+            jnp.repeat(coulomb_part.reshape(4, rank_part).T, 128, axis=1),
+        ],
+        axis=1,
+    )
+    arrived = lax.all_to_all(sent, "ga", split_axis=0, concat_axis=0, tiled=True)
+    arrived, ids, scale = lax.optimization_barrier((arrived, ids, scale))
+    proj, row_copies = rank_sums(arrived, scale)
+    step = [proj] + [
+        shift(proj, "cp", lambda n, s=s: (n + 2 * s) % 8) for s in (1, 2, 3)
+    ]
+    row_sums = lax.all_to_all(row_copies, "ga", split_axis=0, concat_axis=0, tiled=True)
+    exchange = exchange_tiles(meta, ids, screen_basis, row_sums, wave_pieces)
+
+    step, exchange = lax.optimization_barrier((step, exchange))
+    proj_pieces = step + [shift(a, "cp", lambda n: n ^ 1) for a in step]
     order = jnp.arange(512, dtype=jnp.int32)
     source = (order // 8 % 8) * 64 + (order // 64) * 8 + order % 8
     order = (order[:, None] == source[None, :]).astype(BF16)
     tiles = kernel_tiles(meta, ids, order, exchange, proj_pieces)
     got = lax.all_to_all(tiles, ("vp", "ga"), split_axis=0, concat_axis=0, tiled=True)
-    kernel = got.astype(F32).sum(axis=0).reshape(2, own_slots, 512)
+    kernel = got.astype(F32).sum(axis=0).reshape(4, 2, own_slots, 128)
+    kernel = jnp.transpose(kernel, (1, 2, 0, 3)).reshape(2, own_slots, 512)
     live_tile = (tile_owner[None, :] >= window_rows[:, None])[:, :, None]
     return jnp.where(live_tile, kernel, jnp.zeros_like(kernel))
 

time: 151 us -> 131 us (0.87)
  starting transfers between devices: 76 us -> 46.8 us
  waiting for transfers between devices: 39.2 us -> 45.1 us
    ppermute x26 -> x20, starting transfers between devices: 64.1 us -> 34 us  [shift(): return lax.ppermute(array, axis, [(n, send_to(n)) for n in range(size)])]
    all_to_all x1, waiting for transfers between devices: 0.01 us -> 15.6 us  [shards(): lax.all_to_all(sent, 'ga', split_axis=0, concat_axis=0, tiled=True)]
    ppermute x26 -> x20, waiting for transfers between devices: 27.5 us -> 19.5 us  [shift(): return lax.ppermute(array, axis, [(n, send_to(n)) for n in range(size)])]
    all_to_all x0 -> x1, starting transfers between devices: none -> 3.58 us  [shards(): lax.all_to_all(row_copies, 'ga', split_axis=0, concat_axis=0, tiled=True)]
    unnamed x11 -> x13, local copies, waits for them, and re-layouts: 0.69 us -> 3.47 us
    all_to_all x1, starting transfers between devices: 7.32 us -> 5.03 us  [shards(): lax.all_to_all(tiles, ('vp', 'ga'), split_axis=0, concat_axis=0, tiled=True)]
    all_to_all x1, waiting for transfers between devices: 11.7 us -> 10.1 us  [shards(): lax.all_to_all(tiles, ('vp', 'ga'), split_axis=0, concat_axis=0, tiled=True)]
    dynamic_slice x1 -> x0, local copies, waits for them, and re-layouts: 1.53 us -> none  [shards(): basis_rows = lax.dynamic_slice_in_dim(screen_basis, i * quarter, quarter, 0)]
  transfers between devices with their start and end apart: 28 -> 23, of which waited for: 14 -> 13; matrix products, arithmetic and copies ran while one was open for 3% -> 10% of each run, Pallas kernels for 2% -> 2%
where the time goes in v4:
time: 131 us
  starting transfers between devices  46.8 us (36%)
  waiting for transfers between devices  45.1 us (34%)
  blocking collectives  12.9 us (10%)
  Pallas kernels  7.51 us (6%)
  other arithmetic  7.32 us (6%)
  local copies, waits for them, and re-layouts  6.18 us (5%)
  matrix products  4.7 us (4%)
    ppermute x20, starting transfers between devices, shift(): return lax.ppermute(array, axis, [(n, send_to(n)) for n in range(size)])  34 us
    ppermute x20, waiting for transfers between devices, shift(): return lax.ppermute(array, axis, [(n, send_to(n)) for n in range(size)])  19.5 us
    all_to_all x1, waiting for transfers between devices, shards(): lax.all_to_all(sent, 'ga', split_axis=0, concat_axis=0, tiled=True)  15.6 us
    all_gather x1, blocking collectives, shards(): columns = lax.all_gather(waves, 'vp', axis=0)  12.9 us
    all_to_all x1, waiting for transfers between devices, shards(): lax.all_to_all(tiles, ('vp', 'ga'), split_axis=0, concat_axis=0, tiled=True)  10.1 us
    all_to_all x1, starting transfers between devices, shards(): lax.all_to_all(tiles, ('vp', 'ga'), split_axis=0, concat_axis=0, tiled=True)  5.03 us
    dot_general x3, matrix products, project(): lax.dot_general(basis, flat, (((0,), (1,)), ((), ())), preferred_element_...  4.7 us
    all_to_all x1, starting transfers between devices, shards(): lax.all_to_all(sent, 'ga', split_axis=0, concat_axis=0, tiled=True)  4.19 us
  transfers between devices with their start and end apart: 23, of which 13 were waited for; matrix products, arithmetic and copies ran while one was open for 10% of the time, Pallas kernels for 2%

profile of v4, /device:TPU:1, one launch (start us, length us, event | category | flops | bytes accessed | tf_op | source)
XLA Modules:
  0.0 130.9 jit_solution(4545374958539072175)
XLA Ops:
  0.0 1.0 pad_maximum_fusion.2
  1.0 12.9 %all-gather = bf16[128,3072]{1,0:T(8,128)(2,1)S(1)} all-gather(bf16[32,3072]{1,0:T(8,128)(2,1)S(1)} %pad_maximum_fusion.2), channel_id=2, replica_groups=mesh['vp'=4,'cp'=8,'ga'=8] {'vp'}, dimensions={0}, use_global_device_ids=true | all-gather | bytes 983040 | tf_op jit(solution)/shard_map/all_gather | solution.py:279
  14.0 0.7 copy-done.1
  14.6 0.6 shard_map.73
  15.3 4.4 %collective-permute-start = (bf16[32,384]{1,0:T(8,128)(2,1)S(1)}, bf16[32,384]{1,0:T(8,128)(2,1)S(1)}, u32[]{:S(2)}, u32[]{:S(2)}) collective-permute-start(bf16[32,384]{1,0:T(8,128)(2,1)S(1)} %get-tuple-element.27), channel_id=1, source_target_pairs={{0,8},{8,0},{16,24},{24,16},{32,40},{40,32},{48,56},{56,48},{1,9},... | collective-permute-start | bytes 73736 | tf_op jit(solution)/shard_map/ppermute | solution.py:19
  19.6 0.8 collective-permute-done
  20.5 1.0 collective-permute-start.1
  21.5 2.8 %collective-permute-done.1 = bf16[32,384]{1,0:T(8,128)(2,1)S(1)} collective-permute-done((bf16[32,384]{1,0:T(8,128)(2,1)S(1)}, bf16[32,384]{1,0:T(8,128)(2,1)S(1)}, u32[]{:S(2)}, u32[]{:S(2)}) %collective-permute-start.1) | collective-permute-done | bytes 24608 | tf_op jit(solution)/shard_map/ppermute | solution.py:19
  24.4 3.9 %collective-permute-start.2 = (bf16[32,384]{1,0:T(8,128)(2,1)S(1)}, bf16[32,384]{1,0:T(8,128)(2,1)S(1)}, u32[]{:S(2)}, u32[]{:S(2)}) collective-permute-start(bf16[32,384]{1,0:T(8,128)(2,1)S(1)} %add.80), channel_id=1, source_target_pairs={{0,48},{8,56},{16,32},{24,40},{32,16},{40,24},{48,0},{56,8},{1,49}... | collective-permute-start | bytes 73736 | tf_op jit(solution)/shard_map/ppermute | solution.py:19
  28.2 0.7 fusion.30
  28.9 0.6 collective-permute-done.2
  29.5 2.5 %collective-permute-start.3 = (bf16[32,384]{1,0:T(8,128)(2,1)S(1)}, bf16[32,384]{1,0:T(8,128)(2,1)S(1)}, u32[]{:S(2)}, u32[]{:S(2)}) collective-permute-start(bf16[32,384]{1,0:T(8,128)(2,1)S(1)} %add.81), channel_id=1, source_target_pairs={{0,8},{8,0},{16,24},{24,16},{32,40},{40,32},{48,56},{56,48},{1,9},... | collective-permute-start | bytes 73736 | tf_op jit(solution)/shard_map/ppermute | solution.py:19
  32.2 0.6 collective-permute-done.3
  32.8 1.7 %collective-permute-start.4 = (bf16[32,896]{1,0:T(8,128)(2,1)S(1)}, bf16[32,896]{1,0:T(8,128)(2,1)S(1)}, u32[]{:S(2)}, u32[]{:S(2)}) collective-permute-start(bf16[32,896]{1,0:T(8,128)(2,1)S(1)} %pad_maximum_fusion.4.near_ref), channel_id=1, source_target_pairs={{0,64},{64,0},{128,192},{192,128},{1,65},{65,1},{129,193},{193,129... | collective-permute-start | bytes 172040 | tf_op jit(solution)/shard_map/ppermute | solution.py:19
  34.5 1.6 %collective-permute-done.4.next_ref = bf16[32,896]{1,0:T(8,128)(2,1)S(1)} collective-permute-done((bf16[32,896]{1,0:T(8,128)(2,1)S(1)}, bf16[32,896]{1,0:T(8,128)(2,1)S(1)}, u32[]{:S(2)}, u32[]{:S(2)}) %collective-permute-start.4) | collective-permute-done | bytes 57376 | tf_op jit(solution)/shard_map/ppermute | solution.py:19
  36.1 2.8 %collective-permute-start.5 = (bf16[32,1792]{1,0:T(8,128)(2,1)S(1)}, bf16[32,1792]{1,0:T(8,128)(2,1)S(1)}, u32[]{:S(2)}, u32[]{:S(2)}) collective-permute-start(bf16[32,1792]{1,0:T(8,128)(2,1)S(1)} %pad_maximum_fusion.3), channel_id=1, source_target_pairs={{0,192},{64,128},{128,64},{192,0},{1,193},{65,129},{129,65},{193,1... | collective-permute-start | bytes 344072 | tf_op jit(solution)/shard_map/ppermute | solution.py:19
  39.0 4.8 %collective-permute-start.6 = (bf16[4,32,768]{2,1,0:T(8,128)(2,1)S(1)}, bf16[4,32,768]{2,1,0:T(8,128)(2,1)S(1)}, u32[]{:S(2)}, u32[]{:S(2)}) collective-permute-start(bf16[4,32,768]{2,1,0:T(8,128)(2,1)S(1)} %get-tuple-element.36.refs_0_), channel_id=1, source_target_pairs={{0,32},{8,40},{16,48},{24,56},{32,0},{40,8},{48,16},{56,24},{1,33}... | collective-permute-start | bytes 589832 | tf_op jit(solution)/shard_map/ppermute | solution.py:19
  43.8 1.2 collective-permute-start.7
  45.0 2.4 %collective-permute-start.8 = (bf16[4,32,768]{2,1,0:T(8,128)(2,1)S(1)}, bf16[4,32,768]{2,1,0:T(8,128)(2,1)S(1)}, u32[]{:S(2)}, u32[]{:S(2)}) collective-permute-start(bf16[4,32,768]{2,1,0:T(8,128)(2,1)S(1)} %get-tuple-element.36.refs_0_), channel_id=1, source_target_pairs={{0,48},{8,56},{16,0},{24,8},{32,16},{40,24},{48,32},{56,40},{1,49}... | collective-permute-start | bytes 589832 | tf_op jit(solution)/shard_map/ppermute | solution.py:19
  47.4 0.6 shard_map.74
  48.1 1.7 %multiply_convert_fusion = bf16[8,2,8,8,3072]{4,3,2,1,0:T(8,128)(2,1)S(1)} fusion(f32[8,8,3072]{2,1,0:T(8,128)S(1)} %convert.14, f32[2,8,3072]{2,1,0:T(8,128)S(1)} %get-tuple-element.47), kind=kLoop, calls=%fused_computation | loop fusion | flops 6291456 | bytes 7274496 | tf_op jit(solution)/shard_map/convert_element_type | solution.py:292
  49.7 1.3 multiply_convert_fusion.1
  51.0 1.9 %fusion.7 = bf16[256,1024]{1,0:T(8,128)(2,1)S(1)} fusion(bf16[1024,3072]{1,0:T(8,128)(2,1)S(1)} %bitcast.62, bf16[3072,1024]{1,0:T(8,128)(2,1)S(1)} %bitcast.59, s32[]{:T(128)S(6)} %select_n.59), kind=kOutput, calls=%fused_computation.9 | convolution fusion | flops 1610874880 | bytes 8388612 | tf_op jit(solution)/shard_map/dot_general | solution.py:293
  52.9 1.9 %fusion.4 = bf16[256,1024]{1,0:T(8,128)(2,1)S(1)} fusion(bf16[1024,3072]{1,0:T(8,128)(2,1)S(1)} %bitcast.63, bf16[3072,1024]{1,0:T(8,128)(2,1)S(1)} %bitcast.59, s32[]{:T(128)S(6)} %select_n.59), kind=kOutput, calls=%fused_computation.8 | convolution fusion | flops 1610874880 | bytes 8388612 | tf_op jit(solution)/shard_map/dot_general | solution.py:293
  55.0 1.0 fusion.10
  56.3 1.2 pad_maximum_fusion
  57.5 5.5 %collective-permute-done.8.refs_3_ = bf16[4,32,768]{2,1,0:T(8,128)(2,1)S(1)} collective-permute-done((bf16[4,32,768]{2,1,0:T(8,128)(2,1)S(1)}, bf16[4,32,768]{2,1,0:T(8,128)(2,1)S(1)}, u32[]{:S(2)}, u32[]{:S(2)}) %collective-permute-start.8) | collective-permute-done | bytes 196640 | tf_op jit(solution)/shard_map/ppermute | solution.py:19
  63.0 4.2 %all-to-all-start = ((bf16[8,32,2560]{2,1,0:T(8,128)(2,1)}), bf16[8,32,2560]{2,1,0:T(8,128)(2,1)S(1)}, u32[]{:S(2)}, u32[]{:S(2)}) async-start(bf16[8,32,2560]{2,1,0:T(8,128)(2,1)} %pad_maximum_fusion), calls=%async_computation | async-start | bytes 2621440 | tf_op jit(solution)/shard_map/all_to_all | solution.py:327
  67.2 0.8 dynamic_slice.11
  68.3 0.8 dynamic_slice.10
  69.4 15.6 %all-to-all-done.arrived_ref = bf16[8,32,2560]{2,1,0:T(8,128)(2,1)S(1)} async-done(((bf16[8,32,2560]{2,1,0:T(8,128)(2,1)}), bf16[8,32,2560]{2,1,0:T(8,128)(2,1)S(1)}, u32[]{:S(2)}, u32[]{:S(2)}) %all-to-all-start) | async-done | bytes 1310752 | tf_op jit(solution)/shard_map/all_to_all | solution.py:327
  85.0 0.7 shard_map.75
  85.7 3.6 %all-to-all-start.1 = ((bf16[8,32,512]{2,1,0:T(8,128)(2,1)}), bf16[8,32,512]{2,1,0:T(8,128)(2,1)S(1)}, u32[]{:S(2)}, u32[]{:S(2)}) async-start(bf16[8,32,512]{2,1,0:T(8,128)(2,1)} %get-tuple-element.35), calls=%async_computation.1 | async-start | bytes 524288 | tf_op jit(solution)/shard_map/all_to_all | solution.py:333
  89.3 1.6 %collective-permute-start.12 = (bf16[4,32,768]{2,1,0:T(8,128)(2,1)S(1)}, bf16[4,32,768]{2,1,0:T(8,128)(2,1)S(1)}, u32[]{:S(2)}, u32[]{:S(2)}) collective-permute-start(bf16[4,32,768]{2,1,0:T(8,128)(2,1)S(1)} %get-tuple-element.36.refs_0_), channel_id=1, source_target_pairs={{0,8},{8,0},{16,24},{24,16},{32,40},{40,32},{48,56},{56,48},{1,9},... | collective-permute-start | bytes 589832 | tf_op jit(solution)/shard_map/ppermute | solution.py:19
  91.0 0.4 collective-permute-start.14
  91.5 3.3 %collective-permute-start.10 = (bf16[2,32,1024]{2,1,0:T(8,128)(2,1)S(1)}, bf16[2,32,1024]{2,1,0:T(8,128)(2,1)S(1)}, u32[]{:S(2)}, u32[]{:S(2)}) collective-permute-start(bf16[2,32,1024]{2,1,0:T(8,128)(2,1)S(1)} %get-tuple-element.41.refs_0_), channel_id=1, source_target_pairs={{0,32},{8,40},{16,48},{24,56},{32,0},{40,8},{48,16},{56,24},{1,33}... | collective-permute-start | bytes 393224 | tf_op jit(solution)/shard_map/ppermute | solution.py:19
  94.8 1.6 %collective-permute-start.11 = (bf16[2,32,1024]{2,1,0:T(8,128)(2,1)S(1)}, bf16[2,32,1024]{2,1,0:T(8,128)(2,1)S(1)}, u32[]{:S(2)}, u32[]{:S(2)}) collective-permute-start(bf16[2,32,1024]{2,1,0:T(8,128)(2,1)S(1)} %get-tuple-element.41.refs_0_), channel_id=1, source_target_pairs={{0,48},{8,56},{16,0},{24,8},{32,16},{40,24},{48,32},{56,40},{1,49}... | collective-permute-start | bytes 393224 | tf_op jit(solution)/shard_map/ppermute | solution.py:19
  96.4 0.8 collective-permute-start.9
  97.2 2.8 %copy-done = bf16[3072,1024]{1,0:T(8,128)(2,1)S(1)} copy-done((bf16[3072,1024]{1,0:T(8,128)(2,1)S(1)}, bf16[3072,1024]{1,0:T(8,128)(2,1)}, u32[]{:S(2)}) %copy-start) | copy-done | bytes 6291480
  100.0 2.6 %shard_map.76.exchange_ref = f32[24,16,512]{2,1,0:T(8,128)S(1)} custom-call(s32[3]{0:T(128)S(1)} %pad_add_fusion.meta_ref, s32[4,6]{1,0:T(4,128)S(1)} %fusion.15.ids_ref, bf16[3072,1024]{1,0:T(8,128)(2,1)S(1)} %copy-done, bf16[8,32,512]{2,1,0:T(8,128)(2,1)S(1)} %all-to-all-done.1.row_ref, bf16[4,32,768]{2,1,0:T(8,128)(2,1)S(1)} %get-tuple-element.36.refs_0_, ...), custom_call_target="tpu_custom_call" | custom-call | flops 301989888 | bytes 4194304 | tf_op jit(solution)/shard_map/pallas_call | solution.py:180
  102.6 6.4 %collective-permute-done.11.refs_3_ = bf16[2,32,1024]{2,1,0:T(8,128)(2,1)S(1)} collective-permute-done((bf16[2,32,1024]{2,1,0:T(8,128)(2,1)S(1)}, bf16[2,32,1024]{2,1,0:T(8,128)(2,1)S(1)}, u32[]{:S(2)}, u32[]{:S(2)}) %collective-permute-start.11) | collective-permute-done | bytes 131104 | tf_op jit(solution)/shard_map/ppermute | solution.py:19
  109.0 1.1 collective-permute-start.16
  110.1 0.5 collective-permute-start.18
  111.1 0.4 collective-permute-done.17.refs_5_
  111.9 2.9 %shard_map.77 = bf16[32,48,128]{2,1,0:T(8,128)(2,1)} custom-call(s32[3]{0:T(128)S(1)} %pad_add_fusion.meta_ref, s32[4,6]{1,0:T(4,128)S(1)} %fusion.15.ids_ref, bf16[512,512]{1,0:T(8,128)(2,1)S(1)} %fusion.11.order_ref, f32[24,16,512]{2,1,0:T(8,128)S(1)} %shard_map.76.exchange_ref, bf16[2,32,1024]{2,1,0:T(8,128)(2,1)S(1)} %get-tuple-element.41.refs_0_, ...), custom_call_target="tpu_custom_call" | custom-call | tf_op jit(solution)/shard_map/pallas_call | solution.py:253
  114.9 5.0 %all-to-all-start.2 = ((bf16[32,48,128]{2,1,0:T(8,128)(2,1)}), bf16[32,48,128]{2,1,0:T(8,128)(2,1)S(1)}, u32[]{:S(2)}, u32[]{:S(2)}) async-start(bf16[32,48,128]{2,1,0:T(8,128)(2,1)} %shard_map.77), calls=%async_computation.2 | async-start | bytes 786432 | tf_op jit(solution)/shard_map/all_to_all | solution.py:342
  120.0 10.1 %all-to-all-done.2 = bf16[32,48,128]{2,1,0:T(8,128)(2,1)S(1)} async-done(((bf16[32,48,128]{2,1,0:T(8,128)(2,1)}), bf16[32,48,128]{2,1,0:T(8,128)(2,1)S(1)}, u32[]{:S(2)}, u32[]{:S(2)}) %all-to-all-start.2) | async-done | bytes 393248 | tf_op jit(solution)/shard_map/all_to_all | solution.py:342
  130.2 0.7 broadcast_select_fusion
  (67 shorter events, 3.3 us)
Async XLA Ops:
  14.0 0.7 copy-start.1
  15.3 5.2 %collective-permute-start = (bf16[32,384]{1,0:T(8,128)(2,1)S(1)}, bf16[32,384]{1,0:T(8,128)(2,1)S(1)}, u32[]{:S(2)}, u32[]{:S(2)}) collective-permute-start(bf16[32,384]{1,0:T(8,128)(2,1)S(1)} %get-tuple-element.27), channel_id=1, source_target_pairs={{0,8},{8,0},{16,24},{24,16},{32,40},{40,32},{48,56},{56,48},{1,9},... | collective-permute-start | bytes 73736 | tf_op jit(solution)/shard_map/ppermute | solution.py:19
  20.5 3.9 %collective-permute-start.1 = (bf16[32,384]{1,0:T(8,128)(2,1)S(1)}, bf16[32,384]{1,0:T(8,128)(2,1)S(1)}, u32[]{:S(2)}, u32[]{:S(2)}) collective-permute-start(bf16[32,384]{1,0:T(8,128)(2,1)S(1)} %add.79), channel_id=1, source_target_pairs={{0,16},{8,24},{16,0},{24,8},{32,48},{40,56},{48,32},{56,40},{1,17}... | collective-permute-start | bytes 73736 | tf_op jit(solution)/shard_map/ppermute | solution.py:19
  24.4 5.1 %collective-permute-start.2 = (bf16[32,384]{1,0:T(8,128)(2,1)S(1)}, bf16[32,384]{1,0:T(8,128)(2,1)S(1)}, u32[]{:S(2)}, u32[]{:S(2)}) collective-permute-start(bf16[32,384]{1,0:T(8,128)(2,1)S(1)} %add.80), channel_id=1, source_target_pairs={{0,48},{8,56},{16,32},{24,40},{32,16},{40,24},{48,0},{56,8},{1,49}... | collective-permute-start | bytes 73736 | tf_op jit(solution)/shard_map/ppermute | solution.py:19
  29.5 3.3 %collective-permute-start.3 = (bf16[32,384]{1,0:T(8,128)(2,1)S(1)}, bf16[32,384]{1,0:T(8,128)(2,1)S(1)}, u32[]{:S(2)}, u32[]{:S(2)}) collective-permute-start(bf16[32,384]{1,0:T(8,128)(2,1)S(1)} %add.81), channel_id=1, source_target_pairs={{0,8},{8,0},{16,24},{24,16},{32,40},{40,32},{48,56},{56,48},{1,9},... | collective-permute-start | bytes 73736 | tf_op jit(solution)/shard_map/ppermute | solution.py:19
  32.8 3.3 %collective-permute-start.4 = (bf16[32,896]{1,0:T(8,128)(2,1)S(1)}, bf16[32,896]{1,0:T(8,128)(2,1)S(1)}, u32[]{:S(2)}, u32[]{:S(2)}) collective-permute-start(bf16[32,896]{1,0:T(8,128)(2,1)S(1)} %pad_maximum_fusion.4.near_ref), channel_id=1, source_target_pairs={{0,64},{64,0},{128,192},{192,128},{1,65},{65,1},{129,193},{193,129... | collective-permute-start | bytes 172040 | tf_op jit(solution)/shard_map/ppermute | solution.py:19
  36.1 11.4 %collective-permute-start.5 = (bf16[32,1792]{1,0:T(8,128)(2,1)S(1)}, bf16[32,1792]{1,0:T(8,128)(2,1)S(1)}, u32[]{:S(2)}, u32[]{:S(2)}) collective-permute-start(bf16[32,1792]{1,0:T(8,128)(2,1)S(1)} %pad_maximum_fusion.3), channel_id=1, source_target_pairs={{0,192},{64,128},{128,64},{192,0},{1,193},{65,129},{129,65},{193,1... | collective-permute-start | bytes 344072 | tf_op jit(solution)/shard_map/ppermute | solution.py:19
  39.0 18.4 %collective-permute-start.6 = (bf16[4,32,768]{2,1,0:T(8,128)(2,1)S(1)}, bf16[4,32,768]{2,1,0:T(8,128)(2,1)S(1)}, u32[]{:S(2)}, u32[]{:S(2)}) collective-permute-start(bf16[4,32,768]{2,1,0:T(8,128)(2,1)S(1)} %get-tuple-element.36.refs_0_), channel_id=1, source_target_pairs={{0,32},{8,40},{16,48},{24,56},{32,0},{40,8},{48,16},{56,24},{1,33}... | collective-permute-start | bytes 589832 | tf_op jit(solution)/shard_map/ppermute | solution.py:19
  43.8 13.6 %collective-permute-start.7 = (bf16[4,32,768]{2,1,0:T(8,128)(2,1)S(1)}, bf16[4,32,768]{2,1,0:T(8,128)(2,1)S(1)}, u32[]{:S(2)}, u32[]{:S(2)}) collective-permute-start(bf16[4,32,768]{2,1,0:T(8,128)(2,1)S(1)} %get-tuple-element.36.refs_0_), channel_id=1, source_target_pairs={{0,16},{8,24},{16,32},{24,40},{32,48},{40,56},{48,0},{56,8},{1,17}... | collective-permute-start | bytes 589832 | tf_op jit(solution)/shard_map/ppermute | solution.py:19
  45.0 17.9 %collective-permute-start.8 = (bf16[4,32,768]{2,1,0:T(8,128)(2,1)S(1)}, bf16[4,32,768]{2,1,0:T(8,128)(2,1)S(1)}, u32[]{:S(2)}, u32[]{:S(2)}) collective-permute-start(bf16[4,32,768]{2,1,0:T(8,128)(2,1)S(1)} %get-tuple-element.36.refs_0_), channel_id=1, source_target_pairs={{0,48},{8,56},{16,0},{24,8},{32,16},{40,24},{48,32},{56,40},{1,49}... | collective-permute-start | bytes 589832 | tf_op jit(solution)/shard_map/ppermute | solution.py:19
  48.0 3.0 %slice-start = ((s8[6291456]{0:T(1024)(128)(4,1)}), s8[4194304]{0:T(1024)(128)(4,1)S(1)}, s32[]{:S(2)}) async-start(s8[6291456]{0:T(1024)(128)(4,1)} %bitcast.58), calls=%async_computation.3 | async-start | bytes 8388608
  48.1 2.9 %slice-start.1 = ((s8[6291456]{0:T(1024)(128)(4,1)}), s8[2097152]{0:T(1024)(128)(4,1)S(1)}, s32[]{:S(2)}) async-start(s8[6291456]{0:T(1024)(128)(4,1)} %bitcast.58), calls=%async_computation.4 | async-start | bytes 4194304
  63.0 22.0 %all-to-all-start = ((bf16[8,32,2560]{2,1,0:T(8,128)(2,1)}), bf16[8,32,2560]{2,1,0:T(8,128)(2,1)S(1)}, u32[]{:S(2)}, u32[]{:S(2)}) async-start(bf16[8,32,2560]{2,1,0:T(8,128)(2,1)} %pad_maximum_fusion), calls=%async_computation | async-start | bytes 2621440 | tf_op jit(solution)/shard_map/all_to_all | solution.py:327
  85.7 11.4 %all-to-all-start.1 = ((bf16[8,32,512]{2,1,0:T(8,128)(2,1)}), bf16[8,32,512]{2,1,0:T(8,128)(2,1)S(1)}, u32[]{:S(2)}, u32[]{:S(2)}) async-start(bf16[8,32,512]{2,1,0:T(8,128)(2,1)} %get-tuple-element.35), calls=%async_computation.1 | async-start | bytes 524288 | tf_op jit(solution)/shard_map/all_to_all | solution.py:333
  89.3 5.5 %collective-permute-start.12 = (bf16[4,32,768]{2,1,0:T(8,128)(2,1)S(1)}, bf16[4,32,768]{2,1,0:T(8,128)(2,1)S(1)}, u32[]{:S(2)}, u32[]{:S(2)}) collective-permute-start(bf16[4,32,768]{2,1,0:T(8,128)(2,1)S(1)} %get-tuple-element.36.refs_0_), channel_id=1, source_target_pairs={{0,8},{8,0},{16,24},{24,16},{32,40},{40,32},{48,56},{56,48},{1,9},... | collective-permute-start | bytes 589832 | tf_op jit(solution)/shard_map/ppermute | solution.py:19
  90.9 5.5 %collective-permute-start.13 = (bf16[4,32,768]{2,1,0:T(8,128)(2,1)S(1)}, bf16[4,32,768]{2,1,0:T(8,128)(2,1)S(1)}, u32[]{:S(2)}, u32[]{:S(2)}) collective-permute-start(bf16[4,32,768]{2,1,0:T(8,128)(2,1)S(1)} %collective-permute-done.7.refs_1_), channel_id=1, source_target_pairs={{0,8},{8,0},{16,24},{24,16},{32,40},{40,32},{48,56},{56,48},{1,9},... | collective-permute-start | bytes 589832 | tf_op jit(solution)/shard_map/ppermute | solution.py:19
  91.0 6.2 %collective-permute-start.14 = (bf16[4,32,768]{2,1,0:T(8,128)(2,1)S(1)}, bf16[4,32,768]{2,1,0:T(8,128)(2,1)S(1)}, u32[]{:S(2)}, u32[]{:S(2)}) collective-permute-start(bf16[4,32,768]{2,1,0:T(8,128)(2,1)S(1)} %collective-permute-done.6.refs_2_), channel_id=1, source_target_pairs={{0,8},{8,0},{16,24},{24,16},{32,40},{40,32},{48,56},{56,48},{1,9},... | collective-permute-start | bytes 589832 | tf_op jit(solution)/shard_map/ppermute | solution.py:19
  91.4 5.8 %collective-permute-start.15 = (bf16[4,32,768]{2,1,0:T(8,128)(2,1)S(1)}, bf16[4,32,768]{2,1,0:T(8,128)(2,1)S(1)}, u32[]{:S(2)}, u32[]{:S(2)}) collective-permute-start(bf16[4,32,768]{2,1,0:T(8,128)(2,1)S(1)} %collective-permute-done.8.refs_3_), channel_id=1, source_target_pairs={{0,8},{8,0},{16,24},{24,16},{32,40},{40,32},{48,56},{56,48},{1,9},... | collective-permute-start | bytes 589832 | tf_op jit(solution)/shard_map/ppermute | solution.py:19
  91.5 11.1 %collective-permute-start.10 = (bf16[2,32,1024]{2,1,0:T(8,128)(2,1)S(1)}, bf16[2,32,1024]{2,1,0:T(8,128)(2,1)S(1)}, u32[]{:S(2)}, u32[]{:S(2)}) collective-permute-start(bf16[2,32,1024]{2,1,0:T(8,128)(2,1)S(1)} %get-tuple-element.41.refs_0_), channel_id=1, source_target_pairs={{0,32},{8,40},{16,48},{24,56},{32,0},{40,8},{48,16},{56,24},{1,33}... | collective-permute-start | bytes 393224 | tf_op jit(solution)/shard_map/ppermute | solution.py:19
  94.8 14.2 %collective-permute-start.11 = (bf16[2,32,1024]{2,1,0:T(8,128)(2,1)S(1)}, bf16[2,32,1024]{2,1,0:T(8,128)(2,1)S(1)}, u32[]{:S(2)}, u32[]{:S(2)}) collective-permute-start(bf16[2,32,1024]{2,1,0:T(8,128)(2,1)S(1)} %get-tuple-element.41.refs_0_), channel_id=1, source_target_pairs={{0,48},{8,56},{16,0},{24,8},{32,16},{40,24},{48,32},{56,40},{1,49}... | collective-permute-start | bytes 393224 | tf_op jit(solution)/shard_map/ppermute | solution.py:19
  96.4 12.6 %collective-permute-start.9 = (bf16[2,32,1024]{2,1,0:T(8,128)(2,1)S(1)}, bf16[2,32,1024]{2,1,0:T(8,128)(2,1)S(1)}, u32[]{:S(2)}, u32[]{:S(2)}) collective-permute-start(bf16[2,32,1024]{2,1,0:T(8,128)(2,1)S(1)} %get-tuple-element.41.refs_0_), channel_id=1, source_target_pairs={{0,16},{8,24},{16,32},{24,40},{32,48},{40,56},{48,0},{56,8},{1,17}... | collective-permute-start | bytes 393224 | tf_op jit(solution)/shard_map/ppermute | solution.py:19
  97.1 22.8 %copy-start.2 = (s32[2]{0:T(128)S(1)}, s32[2]{0:T(128)}, u32[]{:S(2)}) copy-start(s32[2]{0:T(128)} %window_ref.1) | copy-start | bytes 28
  97.2 22.8 %copy-start.3 = (s32[6]{0:T(128)S(1)}, s32[6]{0:T(128)}, u32[]{:S(2)}) copy-start(s32[6]{0:T(128)} %param.13) | copy-start | bytes 76
  97.2 2.8 %copy-start = (bf16[3072,1024]{1,0:T(8,128)(2,1)S(1)}, bf16[3072,1024]{1,0:T(8,128)(2,1)}, u32[]{:S(2)}) copy-start(bf16[3072,1024]{1,0:T(8,128)(2,1)} %whole_ref.1) | copy-start | bytes 18874372
  109.0 2.0 %collective-permute-start.16 = (bf16[2,32,1024]{2,1,0:T(8,128)(2,1)S(1)}, bf16[2,32,1024]{2,1,0:T(8,128)(2,1)S(1)}, u32[]{:S(2)}, u32[]{:S(2)}) collective-permute-start(bf16[2,32,1024]{2,1,0:T(8,128)(2,1)S(1)} %get-tuple-element.41.refs_0_), channel_id=1, source_target_pairs={{0,8},{8,0},{16,24},{24,16},{32,40},{40,32},{48,56},{56,48},{1,9},... | collective-permute-start | bytes 393224 | tf_op jit(solution)/shard_map/ppermute | solution.py:19
  110.1 1.3 %collective-permute-start.17 = (bf16[2,32,1024]{2,1,0:T(8,128)(2,1)S(1)}, bf16[2,32,1024]{2,1,0:T(8,128)(2,1)S(1)}, u32[]{:S(2)}, u32[]{:S(2)}) collective-permute-start(bf16[2,32,1024]{2,1,0:T(8,128)(2,1)S(1)} %collective-permute-done.9.refs_1_), channel_id=1, source_target_pairs={{0,8},{8,0},{16,24},{24,16},{32,40},{40,32},{48,56},{56,48},{1,9},... | collective-permute-start | bytes 393224 | tf_op jit(solution)/shard_map/ppermute | solution.py:19
  110.1 1.5 %collective-permute-start.18 = (bf16[2,32,1024]{2,1,0:T(8,128)(2,1)S(1)}, bf16[2,32,1024]{2,1,0:T(8,128)(2,1)S(1)}, u32[]{:S(2)}, u32[]{:S(2)}) collective-permute-start(bf16[2,32,1024]{2,1,0:T(8,128)(2,1)S(1)} %collective-permute-done.10.refs_2_), channel_id=1, source_target_pairs={{0,8},{8,0},{16,24},{24,16},{32,40},{40,32},{48,56},{56,48},{1,9},... | collective-permute-start | bytes 393224 | tf_op jit(solution)/shard_map/ppermute | solution.py:19
  110.6 1.3 %collective-permute-start.19 = (bf16[2,32,1024]{2,1,0:T(8,128)(2,1)S(1)}, bf16[2,32,1024]{2,1,0:T(8,128)(2,1)S(1)}, u32[]{:S(2)}, u32[]{:S(2)}) collective-permute-start(bf16[2,32,1024]{2,1,0:T(8,128)(2,1)S(1)} %collective-permute-done.11.refs_3_), channel_id=1, source_target_pairs={{0,8},{8,0},{16,24},{24,16},{32,40},{40,32},{48,56},{56,48},{1,9},... | collective-permute-start | bytes 393224 | tf_op jit(solution)/shard_map/ppermute | solution.py:19
  114.9 15.2 %all-to-all-start.2 = ((bf16[32,48,128]{2,1,0:T(8,128)(2,1)}), bf16[32,48,128]{2,1,0:T(8,128)(2,1)S(1)}, u32[]{:S(2)}, u32[]{:S(2)}) async-start(bf16[32,48,128]{2,1,0:T(8,128)(2,1)} %shard_map.77), calls=%async_computation.2 | async-start | bytes 786432 | tf_op jit(solution)/shard_map/all_to_all | solution.py:342

commit v5 on v4

--- a/solution.py
+++ b/solution.py
@@ -24,14 +24,14 @@
     return device // 8, device % 8, tile % 2
 
 
-def pick_kernel(meta_ref, window_ref, columns_ref, mine_ref, other_ref, quarter_ref):
+def pick_kernel(meta_ref, columns_ref, mine_ref, other_ref, quarter_ref):
     i, j = meta_ref[0], meta_ref[1]
     width = 2 * mine_ref.shape[1]
     first_lane = pl.multiple_of(i * width, 128)
     picked = []
     for first in (0, 16):
         for q in range(2):
-            block = window_ref[q]
+            block = meta_ref[3 + q]
             at, column, half = bands_of(block // NCT if first == 0 else block % NCT)
             both = columns_ref[at, first : first + 16, pl.ds(first_lane, width)].astype(F32)
             rows = jnp.where(half == 0, both[:8], both[8:])
@@ -43,29 +43,17 @@
     other_ref[...] = jnp.where(j % 2 == 0, high, low).astype(BF16)
 
 
-def place_kernel(meta_ref, near_ref, next_ref, far_ref, out_ref):
-    i, j = meta_ref[0], meta_ref[1]
-    width = out_ref.shape[1] // 8
-    for n, flip in enumerate((0, 1, 3, 2)):
-        for half in range(2):
-            start = (i ^ flip) * 2 + (j + half) % 2
-            ref = (near_ref, next_ref, far_ref, far_ref)[n]
-            at = half * width + (near_ref.shape[1] if n == 3 else 0)
-            first = pl.multiple_of(start * width, 128)
-            out_ref[:, pl.ds(first, width)] = ref[:, at : at + width]
-
-
-def row_tiles(meta, window_rows, columns, tile_owner):
+def row_tiles(meta, columns, tile_owner):
     width = columns.shape[2] // 8
     smem, vmem = (pl.BlockSpec(memory_space=m) for m in (pltpu.SMEM, pltpu.VMEM))
     part = jax.ShapeDtypeStruct((32, width), BF16)
     mine, other, quarter = pl.pallas_call(
         pick_kernel,
         out_shape=(part, part, jax.ShapeDtypeStruct((4, 32, 2 * width), BF16)),
-        in_specs=[smem, smem, vmem],
+        in_specs=[smem, vmem],
         out_specs=(vmem, vmem, vmem),
         compiler_params=pltpu.CompilerParams(vmem_limit_bytes=16 * 2**20),
-    )(meta, window_rows, columns)
+    )(meta, columns)
     mine = mine + shift(other, "cp", lambda n: n ^ 1)
     mine = mine + shift(mine, "cp", lambda n: n ^ 2)
     mine = mine + shift(mine, "cp", lambda n: n ^ 6)
@@ -76,17 +64,90 @@
     near = jnp.concatenate([mine, shift(mine, "cp", lambda n: n ^ 1), tiles], axis=1)
     beside = shift(near, "vp", lambda n: n ^ 1)
     far = shift(jnp.concatenate([near, beside], axis=1), "vp", lambda n: n ^ 3)
-    rows = pl.pallas_call(
-        place_kernel,
-        out_shape=jax.ShapeDtypeStruct((32, columns.shape[2]), BF16),
-        in_specs=[smem] + [vmem] * 3,
-        out_specs=vmem,
-        compiler_params=pltpu.CompilerParams(vmem_limit_bytes=16 * 2**20),
-    )(meta, near, beside, far)
     tiles = [near[:slots, -128:], beside[:slots, -128:]]
     tiles += [far[:slots, near.shape[1] - 128 : near.shape[1]], far[:slots, -128:]]
     tiles = jnp.stack(tiles).astype(jnp.int32)
-    return rows, quarter, tiles[:, :, 0] * NCT + tiles[:, :, 64]
+    return (near, beside, far), quarter, tiles[:, :, 0] * NCT + tiles[:, :, 64]
+
+
+def project_kernel(
+    meta_ref, near_ref, next_ref, far_ref, columns_ref, whole_ref, out_ref,
+    rows_ref, band_ref, pair_ref, basis_ref, done_ref,
+):
+    i, j = meta_ref[0], meta_ref[1]
+    ranks = basis_ref.shape[2]
+    copies = []
+    for n in range(4):
+        first = pl.multiple_of((i + n) % 4 * ranks, ranks)
+        copies.append(
+            pltpu.make_async_copy(
+                whole_ref.at[:, pl.ds(first, ranks)], basis_ref.at[n], done_ref.at[n]
+            )
+        )
+        copies[n].start()
+    width = rows_ref.shape[1] // 8
+    for n, flip in enumerate((0, 1, 3, 2)):
+        for half in range(2):
+            start = (i ^ flip) * 2 + (j + half) % 2
+            ref = (near_ref, next_ref, far_ref, far_ref)[n]
+            at = half * width + (near_ref.shape[1] if n == 3 else 0)
+            first = pl.multiple_of(start * width, 128)
+            rows_ref[:, pl.ds(first, width)] = ref[:, at : at + width].astype(F32)
+    for kind in range(2):
+        rows = rows_ref[kind * 16 : kind * 16 + 16]
+        for at in range(4):
+            slot = (kind * 4 + at) % 2
+            band_ref[slot] = columns_ref[at, kind * 16 : kind * 16 + 16].astype(F32)
+            for band in range(0, 16, 2):
+                for q in range(2):
+                    row = rows[q * 8 : q * 8 + 8]
+                    first = band // 8 * 128 + q * 64 + band % 8 * 8
+                    pair_ref[slot, first : first + 16] = jnp.concatenate(
+                        [band_ref[slot, n : n + 1] * row for n in (band, band + 1)], axis=0
+                    ).astype(BF16)
+            if kind == 0 and at == 0:
+                copies[0].wait()
+            part = jnp.dot(pair_ref[slot], basis_ref[0], preferred_element_type=F32)
+            part = part.T.astype(BF16).reshape(8, ranks // 8, 256)
+            first = (kind * 4 + at) * 256
+            out_ref[:, :, first : first + 256] = part
+    rows = rows_ref[:16]
+    upper = lax.broadcasted_iota(jnp.int32, rows.shape, 0) < 8
+    for c in range(8):
+        other = jnp.where(upper, rows_ref[16 + c : 17 + c], rows_ref[24 + c : 25 + c])
+        pair_ref[0, c * 16 : c * 16 + 16] = (rows * other).astype(BF16)
+    for n in range(4):
+        if n:
+            copies[n].wait()
+        part = jnp.dot(pair_ref[0, :128], basis_ref[n], preferred_element_type=F32)
+        part = part.astype(BF16)
+        for m in range(4):
+            for side in range(2):
+                out_ref[(i + n) % 4 * 2 + side, :, 2048 + m * 128 : 2176 + m * 128] = part[
+                    m * 32 : m * 32 + 32, side * 128 : side * 128 + 128
+                ]
+
+
+def project_bands(meta, row_parts, columns, basis):
+    smem, vmem = (pl.BlockSpec(memory_space=m) for m in (pltpu.SMEM, pltpu.VMEM))
+    grid_count = columns.shape[2]
+    return pl.pallas_call(
+        project_kernel,
+        out_shape=jax.ShapeDtypeStruct((8, R // 32, 2560), BF16),
+        in_specs=[smem] + [vmem] * 4 + [pl.BlockSpec(memory_space=pl.ANY)],
+        out_specs=vmem,
+        scratch_shapes=[
+            pltpu.VMEM((32, grid_count), F32),
+            pltpu.VMEM((2, 16, grid_count), F32),
+            pltpu.VMEM((2, 256, grid_count), BF16),
+            pltpu.VMEM((4, grid_count, R // 4), BF16),
+            pltpu.SemaphoreType.DMA((4,)),
+        ],
+        compiler_params=pltpu.CompilerParams(vmem_limit_bytes=54 * 2**20),
+        cost_estimate=pl.CostEstimate(
+            flops=2 * 2560 * grid_count * R // 4, bytes_accessed=2**23, transcendentals=0
+        ),
+    )(meta, *row_parts, columns, basis)
 
 
 def pair_block(left, right):
@@ -146,7 +207,7 @@
         ranks = jnp.concatenate([piece[:, m * 128 : (m + 1) * 128] for m in range(4)], axis=0)
         basis = basis_ref[:, n * 128 : (n + 1) * 128]
         term = lax.dot_general(
-            ranks, basis, (((0,), (1,)), ((), ())), preferred_element_type=F32
+            ranks, basis, (((1,), (1,)), ((), ())), preferred_element_type=F32
         )
         potential = term if potential is None else potential + term
     potential = potential.astype(BF16)
@@ -268,7 +329,7 @@
     i = lax.axis_index("vp")
     j = lax.axis_index("cp")
     k = lax.axis_index("ga")
-    meta = jnp.stack([i, j, k]).astype(jnp.int32)
+    meta = jnp.concatenate([jnp.stack([i, j, k]).astype(jnp.int32), window_rows])
     own_slots = tile_owner.shape[0]
     grid_count = valence_wavefunction.shape[1]
     quarter = grid_count // 4
@@ -277,39 +338,16 @@
 
     waves = jnp.concatenate([valence_wavefunction, cond_wave], axis=0)
     columns = lax.all_gather(waves, "vp", axis=0)
-    rows, quarter_waves, ids = row_tiles(meta, window_rows, columns, tile_owner)
+    row_parts, quarter_waves, ids = row_tiles(meta, columns, tile_owner)
     wave_pieces = [quarter_waves] + [
         shift(quarter_waves, "cp", lambda n, s=s: (n + 2 * s) % 8) for s in (2, 1, 3)
     ]
 
-    row_val = rows[:16].reshape(2, TV, grid_count).astype(F32)
-    row_cond = rows[16:].reshape(2, TC, grid_count).astype(F32)
-    col_val = columns[:, :16].reshape(8, TV, grid_count).astype(F32)
-    col_cond = columns[:, 16:].reshape(8, TC, grid_count).astype(F32)
-    basis_ranks = lax.dynamic_slice_in_dim(screen_basis, i * rank_quarter, rank_quarter, 1)
-
-    def project(pairs, basis):
-        flat = pairs.astype(BF16).reshape(-1, grid_count)
-        return lax.dot_general(
-            basis, flat, (((0,), (1,)), ((), ())), preferred_element_type=F32
-        ).astype(BF16)
-
-    val_part = project(col_val[:, None, :, None] * row_val[None, :, None, :], basis_ranks)
-    cond_part = project(row_cond[None, :, :, None] * col_cond[:, None, None, :], basis_ranks)
-    row_part = project(
-        jnp.swapaxes(row_cond, 0, 1)[:, :, None] * row_val[None], screen_basis
+    row_parts, wave_pieces[1] = lax.optimization_barrier((row_parts, wave_pieces[1]))
+    sent = project_bands(meta, row_parts, columns, screen_basis)
+    sent, wave_pieces[1], wave_pieces[2], wave_pieces[3] = lax.optimization_barrier(
+        (sent, wave_pieces[1], wave_pieces[2], wave_pieces[3])
     )
-    row_part = row_part.reshape(8, 4, rank_part, 128)
-    row_part = jnp.swapaxes(row_part, 1, 2).reshape(8, rank_part, 512)
-    sent = jnp.concatenate(
-        [
-            val_part.reshape(8, rank_part, 1024),
-            cond_part.reshape(8, rank_part, 1024),
-            row_part,
-        ],
-        axis=2,
-    )
-    sent, wave_pieces = lax.optimization_barrier((sent, wave_pieces))
     wave_pieces = [wave_pieces[n] for n in (0, 2, 1, 3)]
     wave_pieces = wave_pieces + [shift(a, "cp", lambda n: n ^ 1) for a in wave_pieces]
     screen_part = lax.dynamic_slice_in_dim(
@@ -320,7 +358,7 @@
         [
             jnp.broadcast_to(screen_part[:, None], (rank_part, 1024)),
             jnp.ones((rank_part, 1024), F32),
-            jnp.repeat(coulomb_part.reshape(4, rank_part).T, 128, axis=1),
+            jnp.tile(jnp.broadcast_to(coulomb_part, (rank_part, R // 8)), (1, 4)),
         ],
         axis=1,
     )
@@ -336,7 +374,7 @@
     step, exchange = lax.optimization_barrier((step, exchange))
     proj_pieces = step + [shift(a, "cp", lambda n: n ^ 1) for a in step]
     order = jnp.arange(512, dtype=jnp.int32)
-    source = (order // 8 % 8) * 64 + (order // 64) * 8 + order % 8
+    source = (order // 8 % 8) * 64 + (order % 8) * 8 + order // 64
     order = (order[:, None] == source[None, :]).astype(BF16)
     tiles = kernel_tiles(meta, ids, order, exchange, proj_pieces)
     got = lax.all_to_all(tiles, ("vp", "ga"), split_axis=0, concat_axis=0, tiled=True)

time: 131 us -> 129 us (0.985)
  Pallas kernels: 7.51 us -> 16.2 us
  other arithmetic: 7.32 us -> 2.35 us
  matrix products: 4.7 us -> 0 us
  waiting for transfers between devices: 45.1 us -> 41.2 us
  starting transfers between devices: 46.8 us -> 49.3 us
    pallas_call x1, Pallas kernels: 0.57 us -> 9.29 us  [project_bands(): pl.pallas_call(project_kernel, out_shape=jax.ShapeDtypeStruct((8, R // 32...]
    dot_general x3 -> x0, matrix products: 4.7 us -> none  [project(): lax.dot_general(basis, flat, (((0,), (1,)), ((), ())), preferred_element_...]
    convert_element_type x6 -> x0, other arithmetic: 3.17 us -> none  [the longest x3 3.02 us: project(): flat = pairs.astype(BF16).reshape(-1, grid_count)]
    all_to_all x1, waiting for transfers between devices: 15.6 us -> 13.5 us  [shards(): lax.all_to_all(sent, 'ga', split_axis=0, concat_axis=0, tiled=True)]
    ppermute x20, waiting for transfers between devices: 19.5 us -> 17.6 us  [shift(): return lax.ppermute(array, axis, [(n, send_to(n)) for n in range(size)])]
    all_to_all x1, starting transfers between devices: 5.03 us -> 6.57 us  [shards(): lax.all_to_all(tiles, ('vp', 'ga'), split_axis=0, concat_axis=0, tiled=True)]
    another operation x3, local copies, waits for them, and re-layouts: 0.09 us -> 1.44 us  [row_tiles(): tiles = jnp.stack(tiles).astype(jnp.int32)]
    unnamed x13 -> x20, local copies, waits for them, and re-layouts: 3.47 us -> 3.41 us
  transfers between devices with their start and end apart: 23 -> 23, of which waited for: 13 -> 13; matrix products, arithmetic and copies ran while one was open for 10% -> 2% of each run, Pallas kernels for 2% -> 9%
where the time goes in v5:
time: 129 us; the launch traced here: 128 us
  starting transfers between devices  49.3 us (38%)
  waiting for transfers between devices  41.2 us (32%)
  Pallas kernels  16.2 us (13%)
  blocking collectives  12.9 us (10%)
  local copies, waits for them, and re-layouts  6.11 us (5%)
  other arithmetic  2.35 us (2%)
    ppermute x20, starting transfers between devices, shift(): return lax.ppermute(array, axis, [(n, send_to(n)) for n in range(size)])  34.4 us
    ppermute x20, waiting for transfers between devices, shift(): return lax.ppermute(array, axis, [(n, send_to(n)) for n in range(size)])  17.6 us
    all_to_all x1, waiting for transfers between devices, shards(): lax.all_to_all(sent, 'ga', split_axis=0, concat_axis=0, tiled=True)  13.5 us
    all_gather x1, blocking collectives, shards(): columns = lax.all_gather(waves, 'vp', axis=0)  12.9 us
    all_to_all x1, waiting for transfers between devices, shards(): lax.all_to_all(tiles, ('vp', 'ga'), split_axis=0, concat_axis=0, tiled=True)  10.1 us
    pallas_call x1, Pallas kernels, project_bands(): pl.pallas_call(project_kernel, out_shape=jax.ShapeDtypeStruct((8, R // 32...  9.29 us
    all_to_all x1, starting transfers between devices, shards(): lax.all_to_all(tiles, ('vp', 'ga'), split_axis=0, concat_axis=0, tiled=True)  6.57 us
    all_to_all x1, starting transfers between devices, shards(): lax.all_to_all(sent, 'ga', split_axis=0, concat_axis=0, tiled=True)  4.19 us
  transfers between devices with their start and end apart: 23, of which 13 were waited for; matrix products, arithmetic and copies ran while one was open for 2% of the time, Pallas kernels for 9%

profile of v5, /device:TPU:1, one launch (start us, length us, event | category | flops | bytes accessed | tf_op | source)
XLA Modules:
  0.0 128.3 jit_solution(6763255792227835828)
XLA Ops:
  0.0 1.0 pad_maximum_fusion
  1.0 12.9 %all-gather = bf16[128,3072]{1,0:T(8,128)(2,1)S(1)} all-gather(bf16[32,3072]{1,0:T(8,128)(2,1)S(1)} %pad_maximum_fusion), channel_id=2, replica_groups=mesh['vp'=4,'cp'=8,'ga'=8] {'vp'}, dimensions={0}, use_global_device_ids=true | all-gather | bytes 983040 | tf_op jit(solution)/shard_map/all_gather | solution.py:340
  14.0 0.6 shard_map.73
  14.7 4.4 %collective-permute-start = (bf16[32,384]{1,0:T(8,128)(2,1)S(1)}, bf16[32,384]{1,0:T(8,128)(2,1)S(1)}, u32[]{:S(2)}, u32[]{:S(2)}) collective-permute-start(bf16[32,384]{1,0:T(8,128)(2,1)S(1)} %get-tuple-element.30), channel_id=1, source_target_pairs={{0,8},{8,0},{16,24},{24,16},{32,40},{40,32},{48,56},{56,48},{1,9},... | collective-permute-start | bytes 73736 | tf_op jit(solution)/shard_map/ppermute | solution.py:19
  19.0 0.8 collective-permute-done
  19.9 1.0 collective-permute-start.1
  20.9 2.8 %collective-permute-done.1 = bf16[32,384]{1,0:T(8,128)(2,1)S(1)} collective-permute-done((bf16[32,384]{1,0:T(8,128)(2,1)S(1)}, bf16[32,384]{1,0:T(8,128)(2,1)S(1)}, u32[]{:S(2)}, u32[]{:S(2)}) %collective-permute-start.1) | collective-permute-done | bytes 24608 | tf_op jit(solution)/shard_map/ppermute | solution.py:19
  23.8 3.9 %collective-permute-start.2 = (bf16[32,384]{1,0:T(8,128)(2,1)S(1)}, bf16[32,384]{1,0:T(8,128)(2,1)S(1)}, u32[]{:S(2)}, u32[]{:S(2)}) collective-permute-start(bf16[32,384]{1,0:T(8,128)(2,1)S(1)} %add.76), channel_id=1, source_target_pairs={{0,48},{8,56},{16,32},{24,40},{32,16},{40,24},{48,0},{56,8},{1,49}... | collective-permute-start | bytes 73736 | tf_op jit(solution)/shard_map/ppermute | solution.py:19
  27.6 1.2 collective-permute-done.2
  28.8 2.5 %collective-permute-start.3 = (bf16[32,384]{1,0:T(8,128)(2,1)S(1)}, bf16[32,384]{1,0:T(8,128)(2,1)S(1)}, u32[]{:S(2)}, u32[]{:S(2)}) collective-permute-start(bf16[32,384]{1,0:T(8,128)(2,1)S(1)} %add.77), channel_id=1, source_target_pairs={{0,8},{8,0},{16,24},{24,16},{32,40},{40,32},{48,56},{56,48},{1,9},... | collective-permute-start | bytes 73736 | tf_op jit(solution)/shard_map/ppermute | solution.py:19
  31.3 0.1 copy.10
  31.6 0.6 collective-permute-done.3
  32.2 1.8 %collective-permute-start.4 = (bf16[32,896]{1,0:T(8,128)(2,1)S(1)}, bf16[32,896]{1,0:T(8,128)(2,1)S(1)}, u32[]{:S(2)}, u32[]{:S(2)}) collective-permute-start(bf16[32,896]{1,0:T(8,128)(2,1)S(1)} %pad_maximum_fusion.2.near_ref), channel_id=1, source_target_pairs={{0,64},{64,0},{128,192},{192,128},{1,65},{65,1},{129,193},{193,129... | collective-permute-start | bytes 172040 | tf_op jit(solution)/shard_map/ppermute | solution.py:19
  34.0 4.7 %collective-permute-start.6 = (bf16[4,32,768]{2,1,0:T(8,128)(2,1)S(1)}, bf16[4,32,768]{2,1,0:T(8,128)(2,1)S(1)}, u32[]{:S(2)}, u32[]{:S(2)}) collective-permute-start(bf16[4,32,768]{2,1,0:T(8,128)(2,1)S(1)} %get-tuple-element.32.refs_0_), channel_id=1, source_target_pairs={{0,32},{8,40},{16,48},{24,56},{32,0},{40,8},{48,16},{56,24},{1,33}... | collective-permute-start | bytes 589832 | tf_op jit(solution)/shard_map/ppermute | solution.py:19
  38.7 1.4 %collective-permute-start.5 = (bf16[32,1792]{1,0:T(8,128)(2,1)S(1)}, bf16[32,1792]{1,0:T(8,128)(2,1)S(1)}, u32[]{:S(2)}, u32[]{:S(2)}) collective-permute-start(bf16[32,1792]{1,0:T(8,128)(2,1)S(1)} %pad_maximum_fusion.1), channel_id=1, source_target_pairs={{0,192},{64,128},{128,64},{192,0},{1,193},{65,129},{129,65},{193,1... | collective-permute-start | bytes 344072 | tf_op jit(solution)/shard_map/ppermute | solution.py:19
  40.1 1.2 collective-permute-start.7
  41.3 2.4 %collective-permute-start.8 = (bf16[4,32,768]{2,1,0:T(8,128)(2,1)S(1)}, bf16[4,32,768]{2,1,0:T(8,128)(2,1)S(1)}, u32[]{:S(2)}, u32[]{:S(2)}) collective-permute-start(bf16[4,32,768]{2,1,0:T(8,128)(2,1)S(1)} %get-tuple-element.32.refs_0_), channel_id=1, source_target_pairs={{0,48},{8,56},{16,0},{24,8},{32,16},{40,24},{48,32},{56,40},{1,49}... | collective-permute-start | bytes 589832 | tf_op jit(solution)/shard_map/ppermute | solution.py:19
  43.7 0.3 collective-permute-done.5.far_ref
  44.0 0.6 copy-done.9
  44.6 9.3 %shard_map.74 = bf16[8,32,2560]{2,1,0:T(8,128)(2,1)} custom-call(s32[5]{0:T(128)} %copy-done.3, bf16[32,896]{1,0:T(8,128)(2,1)} %copy-done.6, bf16[32,896]{1,0:T(8,128)(2,1)} %copy-done.5, bf16[32,1792]{1,0:T(8,128)(2,1)} %copy-done.9, bf16[4,32,3072]{2,1,0:T(8,128)(2,1)} %bitcast.20, bf16[3072,1024]{1,0:T(8,128)(2,1)} %whole_ref.3), custom_call_target="tpu_custom_call" | custom-call | flops 4026531840 | bytes 8388608 | tf_op jit(solution)/shard_map/pallas_call | solution.py:134
  53.9 3.9 %collective-permute-done.8.refs_3_ = bf16[4,32,768]{2,1,0:T(8,128)(2,1)S(1)} collective-permute-done((bf16[4,32,768]{2,1,0:T(8,128)(2,1)S(1)}, bf16[4,32,768]{2,1,0:T(8,128)(2,1)S(1)}, u32[]{:S(2)}, u32[]{:S(2)}) %collective-permute-start.8) | collective-permute-done | bytes 196640 | tf_op jit(solution)/shard_map/ppermute | solution.py:19
  57.8 4.2 %all-to-all-start = ((bf16[8,32,2560]{2,1,0:T(8,128)(2,1)}), bf16[8,32,2560]{2,1,0:T(8,128)(2,1)S(1)}, u32[]{:S(2)}, u32[]{:S(2)}) async-start(bf16[8,32,2560]{2,1,0:T(8,128)(2,1)} %shard_map.74), calls=%async_computation | async-start | bytes 2621440 | tf_op jit(solution)/shard_map/all_to_all | solution.py:365
  62.2 0.8 dynamic_slice.6
  63.1 0.7 slice_bitcast_fusion.2
  63.8 0.7 slice_bitcast_fusion.1
  64.5 0.2 fusion.1.ids_ref
  64.7 13.5 %all-to-all-done.arrived_ref = bf16[8,32,2560]{2,1,0:T(8,128)(2,1)S(1)} async-done(((bf16[8,32,2560]{2,1,0:T(8,128)(2,1)}), bf16[8,32,2560]{2,1,0:T(8,128)(2,1)S(1)}, u32[]{:S(2)}, u32[]{:S(2)}) %all-to-all-start) | async-done | bytes 1310752 | tf_op jit(solution)/shard_map/all_to_all | solution.py:365
  78.2 0.7 shard_map.75
  78.9 4.1 %all-to-all-start.1 = ((bf16[8,32,512]{2,1,0:T(8,128)(2,1)}), bf16[8,32,512]{2,1,0:T(8,128)(2,1)S(1)}, u32[]{:S(2)}, u32[]{:S(2)}) async-start(bf16[8,32,512]{2,1,0:T(8,128)(2,1)} %get-tuple-element.42), calls=%async_computation.1 | async-start | bytes 524288 | tf_op jit(solution)/shard_map/all_to_all | solution.py:371
  83.1 2.9 %collective-permute-start.12 = (bf16[4,32,768]{2,1,0:T(8,128)(2,1)S(1)}, bf16[4,32,768]{2,1,0:T(8,128)(2,1)S(1)}, u32[]{:S(2)}, u32[]{:S(2)}) collective-permute-start(bf16[4,32,768]{2,1,0:T(8,128)(2,1)S(1)} %get-tuple-element.32.refs_0_), channel_id=1, source_target_pairs={{0,8},{8,0},{16,24},{24,16},{32,40},{40,32},{48,56},{56,48},{1,9},... | collective-permute-start | bytes 589832 | tf_op jit(solution)/shard_map/ppermute | solution.py:19
  86.1 0.4 collective-permute-start.14
  86.6 4.3 %collective-permute-start.10 = (bf16[2,32,1024]{2,1,0:T(8,128)(2,1)S(1)}, bf16[2,32,1024]{2,1,0:T(8,128)(2,1)S(1)}, u32[]{:S(2)}, u32[]{:S(2)}) collective-permute-start(bf16[2,32,1024]{2,1,0:T(8,128)(2,1)S(1)} %get-tuple-element.47.refs_0_), channel_id=1, source_target_pairs={{0,32},{8,40},{16,48},{24,56},{32,0},{40,8},{48,16},{56,24},{1,33}... | collective-permute-start | bytes 393224 | tf_op jit(solution)/shard_map/ppermute | solution.py:19
  90.9 0.6 collective-permute-start.11
  91.5 1.8 %collective-permute-start.9 = (bf16[2,32,1024]{2,1,0:T(8,128)(2,1)S(1)}, bf16[2,32,1024]{2,1,0:T(8,128)(2,1)S(1)}, u32[]{:S(2)}, u32[]{:S(2)}) collective-permute-start(bf16[2,32,1024]{2,1,0:T(8,128)(2,1)S(1)} %get-tuple-element.47.refs_0_), channel_id=1, source_target_pairs={{0,16},{8,24},{16,32},{24,40},{32,48},{40,56},{48,0},{56,8},{1,17}... | collective-permute-start | bytes 393224 | tf_op jit(solution)/shard_map/ppermute | solution.py:19
  93.3 2.8 %copy-done.1 = bf16[3072,1024]{1,0:T(8,128)(2,1)S(1)} copy-done((bf16[3072,1024]{1,0:T(8,128)(2,1)S(1)}, bf16[3072,1024]{1,0:T(8,128)(2,1)}, u32[]{:S(2)}) %copy-start.1) | copy-done | bytes 6291480
  96.1 2.6 %shard_map.76.exchange_ref = f32[24,16,512]{2,1,0:T(8,128)S(1)} custom-call(s32[5]{0:T(128)S(1)} %copy-done.4, s32[4,6]{1,0:T(4,128)S(1)} %fusion.1.ids_ref, bf16[3072,1024]{1,0:T(8,128)(2,1)S(1)} %copy-done.1, bf16[8,32,512]{2,1,0:T(8,128)(2,1)S(1)} %all-to-all-done.1.row_ref, bf16[4,32,768]{2,1,0:T(8,128)(2,1)S(1)} %get-tuple-element.32.refs_0_, ...), custom_call_target="tpu_custom_call" | custom-call | flops 301989888 | bytes 4194304 | tf_op jit(solution)/shard_map/pallas_call | solution.py:241
  98.7 6.7 %collective-permute-done.11.refs_3_ = bf16[2,32,1024]{2,1,0:T(8,128)(2,1)S(1)} collective-permute-done((bf16[2,32,1024]{2,1,0:T(8,128)(2,1)S(1)}, bf16[2,32,1024]{2,1,0:T(8,128)(2,1)S(1)}, u32[]{:S(2)}, u32[]{:S(2)}) %collective-permute-start.11) | collective-permute-done | bytes 131104 | tf_op jit(solution)/shard_map/ppermute | solution.py:19
  105.4 0.5 collective-permute-start.16
  106.0 0.5 collective-permute-start.18
  106.5 0.1 fusion.order_ref
  106.6 0.3 collective-permute-done.16.refs_4_
  107.0 0.4 collective-permute-done.17.refs_5_
  107.3 0.2 collective-permute-done.18.refs_6_
  107.5 0.3 collective-permute-done.19.refs_7_
  107.8 2.9 %shard_map.77 = bf16[32,48,128]{2,1,0:T(8,128)(2,1)} custom-call(s32[5]{0:T(128)S(1)} %copy-done.4, s32[4,6]{1,0:T(4,128)S(1)} %fusion.1.ids_ref, bf16[512,512]{1,0:T(8,128)(2,1)S(1)} %fusion.order_ref, f32[24,16,512]{2,1,0:T(8,128)S(1)} %shard_map.76.exchange_ref, bf16[2,32,1024]{2,1,0:T(8,128)(2,1)S(1)} %get-tuple-element.47.refs_0_, ...), custom_call_target="tpu_custom_call" | custom-call | tf_op jit(solution)/shard_map/pallas_call | solution.py:314
  110.8 6.6 %all-to-all-start.2 = ((bf16[32,48,128]{2,1,0:T(8,128)(2,1)}), bf16[32,48,128]{2,1,0:T(8,128)(2,1)S(1)}, u32[]{:S(2)}, u32[]{:S(2)}) async-start(bf16[32,48,128]{2,1,0:T(8,128)(2,1)} %shard_map.77), calls=%async_computation.2 | async-start | bytes 786432 | tf_op jit(solution)/shard_map/all_to_all | solution.py:380
  117.4 10.1 %all-to-all-done.2 = bf16[32,48,128]{2,1,0:T(8,128)(2,1)S(1)} async-done(((bf16[32,48,128]{2,1,0:T(8,128)(2,1)}), bf16[32,48,128]{2,1,0:T(8,128)(2,1)S(1)}, u32[]{:S(2)}, u32[]{:S(2)}) %all-to-all-start.2) | async-done | bytes 393248 | tf_op jit(solution)/shard_map/all_to_all | solution.py:380
  127.6 0.7 broadcast_select_fusion
  (58 shorter events, 1.1 us)
Async XLA Ops:
  0.0 62.1 %copy-start = (f32[1024]{0:T(1024)S(1)}, f32[1024]{0:T(1024)}, u32[]{:S(2)}) copy-start(f32[1024]{0:T(1024)} %param.11) | copy-start | bytes 12292
  0.0 13.9 %copy-start.7 = (s32[2]{0:T(128)S(1)}, s32[2]{0:T(128)}, u32[]{:S(2)}) copy-start(s32[2]{0:T(128)} %param.12) | copy-start | bytes 28
  0.0 27.6 %copy-start.8 = (s32[6]{0:T(128)S(1)}, s32[6]{0:T(128)}, u32[]{:S(2)}) copy-start(s32[6]{0:T(128)} %param.13) | copy-start | bytes 76
  13.9 30.0 %copy-start.2 = (bf16[128,3072]{1,0:T(8,128)(2,1)}, bf16[128,3072]{1,0:T(8,128)(2,1)S(1)}, u32[]{:S(2)}) copy-start(bf16[128,3072]{1,0:T(8,128)(2,1)S(1)} %all-gather) | copy-start | bytes 2359300
  14.0 30.0 %copy-start.3 = (s32[5]{0:T(128)}, s32[5]{0:T(128)S(1)}, u32[]{:S(2)}) copy-start(s32[5]{0:T(128)S(1)} %pad_add_fusion.meta_ref) | copy-start | bytes 64
  14.7 5.2 %collective-permute-start = (bf16[32,384]{1,0:T(8,128)(2,1)S(1)}, bf16[32,384]{1,0:T(8,128)(2,1)S(1)}, u32[]{:S(2)}, u32[]{:S(2)}) collective-permute-start(bf16[32,384]{1,0:T(8,128)(2,1)S(1)} %get-tuple-element.30), channel_id=1, source_target_pairs={{0,8},{8,0},{16,24},{24,16},{32,40},{40,32},{48,56},{56,48},{1,9},... | collective-permute-start | bytes 73736 | tf_op jit(solution)/shard_map/ppermute | solution.py:19
  19.9 3.9 %collective-permute-start.1 = (bf16[32,384]{1,0:T(8,128)(2,1)S(1)}, bf16[32,384]{1,0:T(8,128)(2,1)S(1)}, u32[]{:S(2)}, u32[]{:S(2)}) collective-permute-start(bf16[32,384]{1,0:T(8,128)(2,1)S(1)} %add.75), channel_id=1, source_target_pairs={{0,16},{8,24},{16,0},{24,8},{32,48},{40,56},{48,32},{56,40},{1,17}... | collective-permute-start | bytes 73736 | tf_op jit(solution)/shard_map/ppermute | solution.py:19
  23.8 5.1 %collective-permute-start.2 = (bf16[32,384]{1,0:T(8,128)(2,1)S(1)}, bf16[32,384]{1,0:T(8,128)(2,1)S(1)}, u32[]{:S(2)}, u32[]{:S(2)}) collective-permute-start(bf16[32,384]{1,0:T(8,128)(2,1)S(1)} %add.76), channel_id=1, source_target_pairs={{0,48},{8,56},{16,32},{24,40},{32,16},{40,24},{48,0},{56,8},{1,49}... | collective-permute-start | bytes 73736 | tf_op jit(solution)/shard_map/ppermute | solution.py:19
  28.8 3.3 %collective-permute-start.3 = (bf16[32,384]{1,0:T(8,128)(2,1)S(1)}, bf16[32,384]{1,0:T(8,128)(2,1)S(1)}, u32[]{:S(2)}, u32[]{:S(2)}) collective-permute-start(bf16[32,384]{1,0:T(8,128)(2,1)S(1)} %add.77), channel_id=1, source_target_pairs={{0,8},{8,0},{16,24},{24,16},{32,40},{40,32},{48,56},{56,48},{1,9},... | collective-permute-start | bytes 73736 | tf_op jit(solution)/shard_map/ppermute | solution.py:19
  32.2 11.8 %copy-start.6 = (bf16[32,896]{1,0:T(8,128)(2,1)}, bf16[32,896]{1,0:T(8,128)(2,1)S(1)}, u32[]{:S(2)}) copy-start(bf16[32,896]{1,0:T(8,128)(2,1)S(1)} %pad_maximum_fusion.2.near_ref) | copy-start | bytes 172036
  32.2 6.5 %collective-permute-start.4 = (bf16[32,896]{1,0:T(8,128)(2,1)S(1)}, bf16[32,896]{1,0:T(8,128)(2,1)S(1)}, u32[]{:S(2)}, u32[]{:S(2)}) collective-permute-start(bf16[32,896]{1,0:T(8,128)(2,1)S(1)} %pad_maximum_fusion.2.near_ref), channel_id=1, source_target_pairs={{0,64},{64,0},{128,192},{192,128},{1,65},{65,1},{129,193},{193,129... | collective-permute-start | bytes 172040 | tf_op jit(solution)/shard_map/ppermute | solution.py:19
  34.0 10.0 %collective-permute-start.6 = (bf16[4,32,768]{2,1,0:T(8,128)(2,1)S(1)}, bf16[4,32,768]{2,1,0:T(8,128)(2,1)S(1)}, u32[]{:S(2)}, u32[]{:S(2)}) collective-permute-start(bf16[4,32,768]{2,1,0:T(8,128)(2,1)S(1)} %get-tuple-element.32.refs_0_), channel_id=1, source_target_pairs={{0,32},{8,40},{16,48},{24,56},{32,0},{40,8},{48,16},{56,24},{1,33}... | collective-permute-start | bytes 589832 | tf_op jit(solution)/shard_map/ppermute | solution.py:19
  38.7 5.3 %copy-start.5 = (bf16[32,896]{1,0:T(8,128)(2,1)}, bf16[32,896]{1,0:T(8,128)(2,1)S(1)}, u32[]{:S(2)}) copy-start(bf16[32,896]{1,0:T(8,128)(2,1)S(1)} %collective-permute-done.4.next_ref) | copy-start | bytes 172036
  38.7 5.2 %collective-permute-start.5 = (bf16[32,1792]{1,0:T(8,128)(2,1)S(1)}, bf16[32,1792]{1,0:T(8,128)(2,1)S(1)}, u32[]{:S(2)}, u32[]{:S(2)}) collective-permute-start(bf16[32,1792]{1,0:T(8,128)(2,1)S(1)} %pad_maximum_fusion.1), channel_id=1, source_target_pairs={{0,192},{64,128},{128,64},{192,0},{1,193},{65,129},{129,65},{193,1... | collective-permute-start | bytes 344072 | tf_op jit(solution)/shard_map/ppermute | solution.py:19
  40.1 13.8 %collective-permute-start.7 = (bf16[4,32,768]{2,1,0:T(8,128)(2,1)S(1)}, bf16[4,32,768]{2,1,0:T(8,128)(2,1)S(1)}, u32[]{:S(2)}, u32[]{:S(2)}) collective-permute-start(bf16[4,32,768]{2,1,0:T(8,128)(2,1)S(1)} %get-tuple-element.32.refs_0_), channel_id=1, source_target_pairs={{0,16},{8,24},{16,32},{24,40},{32,48},{40,56},{48,0},{56,8},{1,17}... | collective-permute-start | bytes 589832 | tf_op jit(solution)/shard_map/ppermute | solution.py:19
  41.3 16.5 %collective-permute-start.8 = (bf16[4,32,768]{2,1,0:T(8,128)(2,1)S(1)}, bf16[4,32,768]{2,1,0:T(8,128)(2,1)S(1)}, u32[]{:S(2)}, u32[]{:S(2)}) collective-permute-start(bf16[4,32,768]{2,1,0:T(8,128)(2,1)S(1)} %get-tuple-element.32.refs_0_), channel_id=1, source_target_pairs={{0,48},{8,56},{16,0},{24,8},{32,16},{40,24},{48,32},{56,40},{1,49}... | collective-permute-start | bytes 589832 | tf_op jit(solution)/shard_map/ppermute | solution.py:19
  44.0 0.6 copy-start.9
  57.8 20.4 %all-to-all-start = ((bf16[8,32,2560]{2,1,0:T(8,128)(2,1)}), bf16[8,32,2560]{2,1,0:T(8,128)(2,1)S(1)}, u32[]{:S(2)}, u32[]{:S(2)}) async-start(bf16[8,32,2560]{2,1,0:T(8,128)(2,1)} %shard_map.74), calls=%async_computation | async-start | bytes 2621440 | tf_op jit(solution)/shard_map/all_to_all | solution.py:365
  63.0 30.2 %copy-start.4 = (s32[5]{0:T(128)S(1)}, s32[5]{0:T(128)}, u32[]{:S(2)}) copy-start(s32[5]{0:T(128)} %copy-done.3) | copy-start | bytes 64
  78.9 14.3 %all-to-all-start.1 = ((bf16[8,32,512]{2,1,0:T(8,128)(2,1)}), bf16[8,32,512]{2,1,0:T(8,128)(2,1)S(1)}, u32[]{:S(2)}, u32[]{:S(2)}) async-start(bf16[8,32,512]{2,1,0:T(8,128)(2,1)} %get-tuple-element.42), calls=%async_computation.1 | async-start | bytes 524288 | tf_op jit(solution)/shard_map/all_to_all | solution.py:371
  83.1 7.8 %collective-permute-start.12 = (bf16[4,32,768]{2,1,0:T(8,128)(2,1)S(1)}, bf16[4,32,768]{2,1,0:T(8,128)(2,1)S(1)}, u32[]{:S(2)}, u32[]{:S(2)}) collective-permute-start(bf16[4,32,768]{2,1,0:T(8,128)(2,1)S(1)} %get-tuple-element.32.refs_0_), channel_id=1, source_target_pairs={{0,8},{8,0},{16,24},{24,16},{32,40},{40,32},{48,56},{56,48},{1,9},... | collective-permute-start | bytes 589832 | tf_op jit(solution)/shard_map/ppermute | solution.py:19
  86.0 5.5 %collective-permute-start.13 = (bf16[4,32,768]{2,1,0:T(8,128)(2,1)S(1)}, bf16[4,32,768]{2,1,0:T(8,128)(2,1)S(1)}, u32[]{:S(2)}, u32[]{:S(2)}) collective-permute-start(bf16[4,32,768]{2,1,0:T(8,128)(2,1)S(1)} %collective-permute-done.7.refs_1_), channel_id=1, source_target_pairs={{0,8},{8,0},{16,24},{24,16},{32,40},{40,32},{48,56},{56,48},{1,9},... | collective-permute-start | bytes 589832 | tf_op jit(solution)/shard_map/ppermute | solution.py:19
  86.1 7.2 %collective-permute-start.14 = (bf16[4,32,768]{2,1,0:T(8,128)(2,1)S(1)}, bf16[4,32,768]{2,1,0:T(8,128)(2,1)S(1)}, u32[]{:S(2)}, u32[]{:S(2)}) collective-permute-start(bf16[4,32,768]{2,1,0:T(8,128)(2,1)S(1)} %collective-permute-done.6.refs_2_), channel_id=1, source_target_pairs={{0,8},{8,0},{16,24},{24,16},{32,40},{40,32},{48,56},{56,48},{1,9},... | collective-permute-start | bytes 589832 | tf_op jit(solution)/shard_map/ppermute | solution.py:19
  86.5 6.8 %collective-permute-start.15 = (bf16[4,32,768]{2,1,0:T(8,128)(2,1)S(1)}, bf16[4,32,768]{2,1,0:T(8,128)(2,1)S(1)}, u32[]{:S(2)}, u32[]{:S(2)}) collective-permute-start(bf16[4,32,768]{2,1,0:T(8,128)(2,1)S(1)} %collective-permute-done.8.refs_3_), channel_id=1, source_target_pairs={{0,8},{8,0},{16,24},{24,16},{32,40},{40,32},{48,56},{56,48},{1,9},... | collective-permute-start | bytes 589832 | tf_op jit(solution)/shard_map/ppermute | solution.py:19
  86.6 12.1 %collective-permute-start.10 = (bf16[2,32,1024]{2,1,0:T(8,128)(2,1)S(1)}, bf16[2,32,1024]{2,1,0:T(8,128)(2,1)S(1)}, u32[]{:S(2)}, u32[]{:S(2)}) collective-permute-start(bf16[2,32,1024]{2,1,0:T(8,128)(2,1)S(1)} %get-tuple-element.47.refs_0_), channel_id=1, source_target_pairs={{0,32},{8,40},{16,48},{24,56},{32,0},{40,8},{48,16},{56,24},{1,33}... | collective-permute-start | bytes 393224 | tf_op jit(solution)/shard_map/ppermute | solution.py:19
  90.9 14.6 %collective-permute-start.11 = (bf16[2,32,1024]{2,1,0:T(8,128)(2,1)S(1)}, bf16[2,32,1024]{2,1,0:T(8,128)(2,1)S(1)}, u32[]{:S(2)}, u32[]{:S(2)}) collective-permute-start(bf16[2,32,1024]{2,1,0:T(8,128)(2,1)S(1)} %get-tuple-element.47.refs_0_), channel_id=1, source_target_pairs={{0,48},{8,56},{16,0},{24,8},{32,16},{40,24},{48,32},{56,40},{1,49}... | collective-permute-start | bytes 393224 | tf_op jit(solution)/shard_map/ppermute | solution.py:19
  91.5 14.0 %collective-permute-start.9 = (bf16[2,32,1024]{2,1,0:T(8,128)(2,1)S(1)}, bf16[2,32,1024]{2,1,0:T(8,128)(2,1)S(1)}, u32[]{:S(2)}, u32[]{:S(2)}) collective-permute-start(bf16[2,32,1024]{2,1,0:T(8,128)(2,1)S(1)} %get-tuple-element.47.refs_0_), channel_id=1, source_target_pairs={{0,16},{8,24},{16,32},{24,40},{32,48},{40,56},{48,0},{56,8},{1,17}... | collective-permute-start | bytes 393224 | tf_op jit(solution)/shard_map/ppermute | solution.py:19
  93.3 2.8 %copy-start.1 = (bf16[3072,1024]{1,0:T(8,128)(2,1)S(1)}, bf16[3072,1024]{1,0:T(8,128)(2,1)}, u32[]{:S(2)}) copy-start(bf16[3072,1024]{1,0:T(8,128)(2,1)} %whole_ref.3) | copy-start | bytes 18874372
  105.4 1.5 %collective-permute-start.16 = (bf16[2,32,1024]{2,1,0:T(8,128)(2,1)S(1)}, bf16[2,32,1024]{2,1,0:T(8,128)(2,1)S(1)}, u32[]{:S(2)}, u32[]{:S(2)}) collective-permute-start(bf16[2,32,1024]{2,1,0:T(8,128)(2,1)S(1)} %get-tuple-element.47.refs_0_), channel_id=1, source_target_pairs={{0,8},{8,0},{16,24},{24,16},{32,40},{40,32},{48,56},{56,48},{1,9},... | collective-permute-start | bytes 393224 | tf_op jit(solution)/shard_map/ppermute | solution.py:19
  106.0 1.3 %collective-permute-start.17 = (bf16[2,32,1024]{2,1,0:T(8,128)(2,1)S(1)}, bf16[2,32,1024]{2,1,0:T(8,128)(2,1)S(1)}, u32[]{:S(2)}, u32[]{:S(2)}) collective-permute-start(bf16[2,32,1024]{2,1,0:T(8,128)(2,1)S(1)} %collective-permute-done.9.refs_1_), channel_id=1, source_target_pairs={{0,8},{8,0},{16,24},{24,16},{32,40},{40,32},{48,56},{56,48},{1,9},... | collective-permute-start | bytes 393224 | tf_op jit(solution)/shard_map/ppermute | solution.py:19
  106.0 1.5 %collective-permute-start.18 = (bf16[2,32,1024]{2,1,0:T(8,128)(2,1)S(1)}, bf16[2,32,1024]{2,1,0:T(8,128)(2,1)S(1)}, u32[]{:S(2)}, u32[]{:S(2)}) collective-permute-start(bf16[2,32,1024]{2,1,0:T(8,128)(2,1)S(1)} %collective-permute-done.10.refs_2_), channel_id=1, source_target_pairs={{0,8},{8,0},{16,24},{24,16},{32,40},{40,32},{48,56},{56,48},{1,9},... | collective-permute-start | bytes 393224 | tf_op jit(solution)/shard_map/ppermute | solution.py:19
  106.5 1.3 %collective-permute-start.19 = (bf16[2,32,1024]{2,1,0:T(8,128)(2,1)S(1)}, bf16[2,32,1024]{2,1,0:T(8,128)(2,1)S(1)}, u32[]{:S(2)}, u32[]{:S(2)}) collective-permute-start(bf16[2,32,1024]{2,1,0:T(8,128)(2,1)S(1)} %collective-permute-done.11.refs_3_), channel_id=1, source_target_pairs={{0,8},{8,0},{16,24},{24,16},{32,40},{40,32},{48,56},{56,48},{1,9},... | collective-permute-start | bytes 393224 | tf_op jit(solution)/shard_map/ppermute | solution.py:19
  110.8 16.7 %all-to-all-start.2 = ((bf16[32,48,128]{2,1,0:T(8,128)(2,1)}), bf16[32,48,128]{2,1,0:T(8,128)(2,1)S(1)}, u32[]{:S(2)}, u32[]{:S(2)}) async-start(bf16[32,48,128]{2,1,0:T(8,128)(2,1)} %shard_map.77), calls=%async_computation.2 | async-start | bytes 786432 | tf_op jit(solution)/shard_map/all_to_all | solution.py:380

commit v6 on v5

--- a/solution.py
+++ b/solution.py
@@ -24,9 +24,9 @@
     return device // 8, device % 8, tile % 2
 
 
-def pick_kernel(meta_ref, columns_ref, mine_ref, other_ref, quarter_ref):
+def pick_kernel(meta_ref, columns_ref, mine_ref, quarter_ref):
     i, j = meta_ref[0], meta_ref[1]
-    width = 2 * mine_ref.shape[1]
+    width = mine_ref.shape[1]
     first_lane = pl.multiple_of(i * width, 128)
     picked = []
     for first in (0, 16):
@@ -37,44 +37,45 @@
             rows = jnp.where(half == 0, both[:8], both[8:])
             picked.append(jnp.where(column == j, rows, jnp.zeros_like(rows)))
     quarter_ref[...] = columns_ref[:, :, pl.ds(first_lane, width)]
-    rows = jnp.concatenate(picked, axis=0)
-    low, high = rows[:, : width // 2], rows[:, width // 2 :]
-    mine_ref[...] = jnp.where(j % 2 == 0, low, high).astype(BF16)
-    other_ref[...] = jnp.where(j % 2 == 0, high, low).astype(BF16)
+    mine_ref[...] = jnp.concatenate(picked, axis=0).astype(BF16)
 
 
 def row_tiles(meta, columns, tile_owner):
-    width = columns.shape[2] // 8
+    width = columns.shape[2] // 4
     smem, vmem = (pl.BlockSpec(memory_space=m) for m in (pltpu.SMEM, pltpu.VMEM))
-    part = jax.ShapeDtypeStruct((32, width), BF16)
-    mine, other, quarter = pl.pallas_call(
+    mine, quarter = pl.pallas_call(
         pick_kernel,
-        out_shape=(part, part, jax.ShapeDtypeStruct((4, 32, 2 * width), BF16)),
+        out_shape=(
+            jax.ShapeDtypeStruct((32, width), BF16),
+            jax.ShapeDtypeStruct((4, 32, width), BF16),
+        ),
         in_specs=[smem, vmem],
-        out_specs=(vmem, vmem, vmem),
+        out_specs=(vmem, vmem),
         compiler_params=pltpu.CompilerParams(vmem_limit_bytes=16 * 2**20),
     )(meta, columns)
-    mine = mine + shift(other, "cp", lambda n: n ^ 1)
     mine = mine + shift(mine, "cp", lambda n: n ^ 2)
+    quarter, mine = lax.optimization_barrier((quarter, mine))
     mine = mine + shift(mine, "cp", lambda n: n ^ 6)
-    quarter, mine = lax.optimization_barrier((quarter, mine))
+    mine = mine + shift(mine, "cp", lambda n: n ^ 1)
     slots = tile_owner.shape[0]
     tiles = jnp.repeat(jnp.stack([tile_owner // NCT, tile_owner % NCT], axis=1), 64, axis=1)
     tiles = jnp.pad(tiles, ((0, 32 - slots), (0, 0))).astype(BF16)
-    near = jnp.concatenate([mine, shift(mine, "cp", lambda n: n ^ 1), tiles], axis=1)
+    near = jnp.concatenate([mine, tiles], axis=1)
     beside = shift(near, "vp", lambda n: n ^ 1)
+    across = shift(quarter, "cp", lambda n: (n + 4) % 8)
+    beside, across = lax.optimization_barrier((beside, across))
     far = shift(jnp.concatenate([near, beside], axis=1), "vp", lambda n: n ^ 3)
     tiles = [near[:slots, -128:], beside[:slots, -128:]]
     tiles += [far[:slots, near.shape[1] - 128 : near.shape[1]], far[:slots, -128:]]
     tiles = jnp.stack(tiles).astype(jnp.int32)
-    return (near, beside, far), quarter, tiles[:, :, 0] * NCT + tiles[:, :, 64]
+    return (near, beside, far), (quarter, across), tiles[:, :, 0] * NCT + tiles[:, :, 64]
 
 
 def project_kernel(
     meta_ref, near_ref, next_ref, far_ref, columns_ref, whole_ref, out_ref,
     rows_ref, band_ref, pair_ref, basis_ref, done_ref,
 ):
-    i, j = meta_ref[0], meta_ref[1]
+    i = meta_ref[0]
     ranks = basis_ref.shape[2]
     copies = []
     for n in range(4):
@@ -85,14 +86,12 @@
             )
         )
         copies[n].start()
-    width = rows_ref.shape[1] // 8
+    width = rows_ref.shape[1] // 4
     for n, flip in enumerate((0, 1, 3, 2)):
-        for half in range(2):
-            start = (i ^ flip) * 2 + (j + half) % 2
-            ref = (near_ref, next_ref, far_ref, far_ref)[n]
-            at = half * width + (near_ref.shape[1] if n == 3 else 0)
-            first = pl.multiple_of(start * width, 128)
-            rows_ref[:, pl.ds(first, width)] = ref[:, at : at + width].astype(F32)
+        ref = (near_ref, next_ref, far_ref, far_ref)[n]
+        at = near_ref.shape[1] if n == 3 else 0
+        first = pl.multiple_of((i ^ flip) * width, 128)
+        rows_ref[:, pl.ds(first, width)] = ref[:, at : at + width].astype(F32)
     for kind in range(2):
         rows = rows_ref[kind * 16 : kind * 16 + 16]
         for at in range(4):
@@ -339,11 +338,10 @@
     waves = jnp.concatenate([valence_wavefunction, cond_wave], axis=0)
     columns = lax.all_gather(waves, "vp", axis=0)
     row_parts, quarter_waves, ids = row_tiles(meta, columns, tile_owner)
-    wave_pieces = [quarter_waves] + [
-        shift(quarter_waves, "cp", lambda n, s=s: (n + 2 * s) % 8) for s in (2, 1, 3)
+    wave_pieces = list(quarter_waves) + [
+        shift(quarter_waves[0], "cp", lambda n, s=s: (n + 2 * s) % 8) for s in (1, 3)
     ]
 
-    row_parts, wave_pieces[1] = lax.optimization_barrier((row_parts, wave_pieces[1]))
     sent = project_bands(meta, row_parts, columns, screen_basis)
     sent, wave_pieces[1], wave_pieces[2], wave_pieces[3] = lax.optimization_barrier(
         (sent, wave_pieces[1], wave_pieces[2], wave_pieces[3])

time: 129 us -> 127 us (0.984)
  waiting for transfers between devices: 41.2 us -> 32.2 us
  starting transfers between devices: 49.3 us -> 56.5 us
    ppermute x20 -> x19, waiting for transfers between devices: 17.6 us -> 8.65 us  [shift(): return lax.ppermute(array, axis, [(n, send_to(n)) for n in range(size)])]
    ppermute x20 -> x19, starting transfers between devices: 34.4 us -> 40.2 us  [shift(): return lax.ppermute(array, axis, [(n, send_to(n)) for n in range(size)])]
  transfers between devices with their start and end apart: 23 -> 22, of which waited for: 13 -> 11; matrix products, arithmetic and copies ran while one was open for 2% -> 3% of each run, Pallas kernels for 9% -> 9%
where the time goes in v6:
time: 127 us
  starting transfers between devices  56.5 us (44%)
  waiting for transfers between devices  32.2 us (25%)
  Pallas kernels  16.2 us (13%)
  blocking collectives  12.9 us (10%)
  local copies, waits for them, and re-layouts  6.14 us (5%)
  other arithmetic  2.37 us (2%)
    ppermute x19, starting transfers between devices, shift(): return lax.ppermute(array, axis, [(n, send_to(n)) for n in range(size)])  40.2 us
    all_to_all x1, waiting for transfers between devices, shards(): lax.all_to_all(sent, 'ga', split_axis=0, concat_axis=0, tiled=True)  13.4 us
    all_gather x1, blocking collectives, shards(): columns = lax.all_gather(waves, 'vp', axis=0)  12.9 us
    all_to_all x1, waiting for transfers between devices, shards(): lax.all_to_all(tiles, ('vp', 'ga'), split_axis=0, concat_axis=0, tiled=True)  10.1 us
    pallas_call x1, Pallas kernels, project_bands(): pl.pallas_call(project_kernel, out_shape=jax.ShapeDtypeStruct((8, R // 32...  9.28 us
    ppermute x19, waiting for transfers between devices, shift(): return lax.ppermute(array, axis, [(n, send_to(n)) for n in range(size)])  8.65 us
    all_to_all x1, starting transfers between devices, shards(): lax.all_to_all(tiles, ('vp', 'ga'), split_axis=0, concat_axis=0, tiled=True)  7.75 us
    all_to_all x1, starting transfers between devices, shards(): lax.all_to_all(sent, 'ga', split_axis=0, concat_axis=0, tiled=True)  4.42 us
  transfers between devices with their start and end apart: 22, of which 11 were waited for; matrix products, arithmetic and copies ran while one was open for 3% of the time, Pallas kernels for 9%

profile of v6, /device:TPU:1, one launch (start us, length us, event | category | flops | bytes accessed | tf_op | source)
XLA Modules:
  0.0 126.6 jit_solution(9410216523009060799)
XLA Ops:
  0.0 1.0 pad_maximum_fusion
  1.0 12.9 %all-gather = bf16[128,3072]{1,0:T(8,128)(2,1)S(1)} all-gather(bf16[32,3072]{1,0:T(8,128)(2,1)S(1)} %pad_maximum_fusion), channel_id=2, replica_groups=mesh['vp'=4,'cp'=8,'ga'=8] {'vp'}, dimensions={0}, use_global_device_ids=true | all-gather | bytes 983040 | tf_op jit(solution)/shard_map/all_gather | solution.py:339
  14.0 0.6 shard_map.73
  14.7 3.1 %collective-permute-start = (bf16[32,768]{1,0:T(8,128)(2,1)S(1)}, bf16[32,768]{1,0:T(8,128)(2,1)S(1)}, u32[]{:S(2)}, u32[]{:S(2)}) collective-permute-start(bf16[32,768]{1,0:T(8,128)(2,1)S(1)} %get-tuple-element.26), channel_id=1, source_target_pairs={{0,16},{8,24},{16,0},{24,8},{32,48},{40,56},{48,32},{56,40},{1,17}... | collective-permute-start | bytes 147464 | tf_op jit(solution)/shard_map/ppermute | solution.py:19
  17.7 1.5 %collective-permute-done = bf16[32,768]{1,0:T(8,128)(2,1)S(1)} collective-permute-done((bf16[32,768]{1,0:T(8,128)(2,1)S(1)}, bf16[32,768]{1,0:T(8,128)(2,1)S(1)}, u32[]{:S(2)}, u32[]{:S(2)}) %collective-permute-start) | collective-permute-done | bytes 49184 | tf_op jit(solution)/shard_map/ppermute | solution.py:19
  19.2 5.6 %collective-permute-start.1 = (bf16[32,768]{1,0:T(8,128)(2,1)S(1)}, bf16[32,768]{1,0:T(8,128)(2,1)S(1)}, u32[]{:S(2)}, u32[]{:S(2)}) collective-permute-start(bf16[32,768]{1,0:T(8,128)(2,1)S(1)} %add.75), channel_id=1, source_target_pairs={{0,48},{8,56},{16,32},{24,40},{32,16},{40,24},{48,0},{56,8},{1,49}... | collective-permute-start | bytes 147464 | tf_op jit(solution)/shard_map/ppermute | solution.py:19
  24.8 0.9 collective-permute-start.4
  25.7 1.1 collective-permute-done.1
  26.8 10.2 %collective-permute-start.2 = (bf16[32,768]{1,0:T(8,128)(2,1)S(1)}, bf16[32,768]{1,0:T(8,128)(2,1)S(1)}, u32[]{:S(2)}, u32[]{:S(2)}) collective-permute-start(bf16[32,768]{1,0:T(8,128)(2,1)S(1)} %add.76), channel_id=1, source_target_pairs={{0,8},{8,0},{16,24},{24,16},{32,40},{40,32},{48,56},{56,48},{1,9},... | collective-permute-start | bytes 147464 | tf_op jit(solution)/shard_map/ppermute | solution.py:19
  37.0 0.1 copy.10
  37.2 0.1 reshape.88
  37.3 0.6 collective-permute-done.2
  37.9 0.1 collective-permute-start.3
  38.0 3.0 %collective-permute-done.3.next_ref = bf16[32,896]{1,0:T(8,128)(2,1)S(1)} collective-permute-done((bf16[32,896]{1,0:T(8,128)(2,1)S(1)}, bf16[32,896]{1,0:T(8,128)(2,1)S(1)}, u32[]{:S(2)}, u32[]{:S(2)}) %collective-permute-start.3) | collective-permute-done | bytes 57376 | tf_op jit(solution)/shard_map/ppermute | solution.py:19
  41.1 0.8 collective-permute-start.5
  41.9 1.4 %collective-permute-start.6 = (bf16[4,32,768]{2,1,0:T(8,128)(2,1)S(1)}, bf16[4,32,768]{2,1,0:T(8,128)(2,1)S(1)}, u32[]{:S(2)}, u32[]{:S(2)}) collective-permute-start(bf16[4,32,768]{2,1,0:T(8,128)(2,1)S(1)} %get-tuple-element.28.refs_0_), channel_id=1, source_target_pairs={{0,16},{8,24},{16,32},{24,40},{32,48},{40,56},{48,0},{56,8},{1,17}... | collective-permute-start | bytes 589832 | tf_op jit(solution)/shard_map/ppermute | solution.py:19
  43.3 2.9 %collective-permute-start.7 = (bf16[4,32,768]{2,1,0:T(8,128)(2,1)S(1)}, bf16[4,32,768]{2,1,0:T(8,128)(2,1)S(1)}, u32[]{:S(2)}, u32[]{:S(2)}) collective-permute-start(bf16[4,32,768]{2,1,0:T(8,128)(2,1)S(1)} %get-tuple-element.28.refs_0_), channel_id=1, source_target_pairs={{0,48},{8,56},{16,0},{24,8},{32,16},{40,24},{48,32},{56,40},{1,49}... | collective-permute-start | bytes 589832 | tf_op jit(solution)/shard_map/ppermute | solution.py:19
  46.2 0.6 copy-done.9
  46.8 9.3 %shard_map.74 = bf16[8,32,2560]{2,1,0:T(8,128)(2,1)} custom-call(s32[5]{0:T(128)} %copy-done.3, bf16[32,896]{1,0:T(8,128)(2,1)} %copy-done.6, bf16[32,896]{1,0:T(8,128)(2,1)} %copy-done.5, bf16[32,1792]{1,0:T(8,128)(2,1)} %copy-done.9, bf16[4,32,3072]{2,1,0:T(8,128)(2,1)} %bitcast.20, bf16[3072,1024]{1,0:T(8,128)(2,1)} %whole_ref.3), custom_call_target="tpu_custom_call" | custom-call | flops 4026531840 | bytes 8388608 | tf_op jit(solution)/shard_map/pallas_call | solution.py:133
  56.1 4.4 %all-to-all-start = ((bf16[8,32,2560]{2,1,0:T(8,128)(2,1)}), bf16[8,32,2560]{2,1,0:T(8,128)(2,1)S(1)}, u32[]{:S(2)}, u32[]{:S(2)}) async-start(bf16[8,32,2560]{2,1,0:T(8,128)(2,1)} %shard_map.74), calls=%async_computation | async-start | bytes 2621440 | tf_op jit(solution)/shard_map/all_to_all | solution.py:363
  60.6 0.1 stack.39
  60.7 0.8 dynamic_slice.6
  61.6 0.7 slice_bitcast_fusion.2
  62.3 0.7 slice_bitcast_fusion.1
  63.0 0.2 fusion.1.ids_ref
  63.2 13.4 %all-to-all-done.arrived_ref = bf16[8,32,2560]{2,1,0:T(8,128)(2,1)S(1)} async-done(((bf16[8,32,2560]{2,1,0:T(8,128)(2,1)}), bf16[8,32,2560]{2,1,0:T(8,128)(2,1)S(1)}, u32[]{:S(2)}, u32[]{:S(2)}) %all-to-all-start) | async-done | bytes 1310752 | tf_op jit(solution)/shard_map/all_to_all | solution.py:363
  76.6 0.7 shard_map.75
  77.4 4.1 %all-to-all-start.1 = ((bf16[8,32,512]{2,1,0:T(8,128)(2,1)}), bf16[8,32,512]{2,1,0:T(8,128)(2,1)S(1)}, u32[]{:S(2)}, u32[]{:S(2)}) async-start(bf16[8,32,512]{2,1,0:T(8,128)(2,1)} %get-tuple-element.36), calls=%async_computation.1 | async-start | bytes 524288 | tf_op jit(solution)/shard_map/all_to_all | solution.py:369
  81.5 2.8 %collective-permute-start.11 = (bf16[4,32,768]{2,1,0:T(8,128)(2,1)S(1)}, bf16[4,32,768]{2,1,0:T(8,128)(2,1)S(1)}, u32[]{:S(2)}, u32[]{:S(2)}) collective-permute-start(bf16[4,32,768]{2,1,0:T(8,128)(2,1)S(1)} %get-tuple-element.28.refs_0_), channel_id=1, source_target_pairs={{0,8},{8,0},{16,24},{24,16},{32,40},{40,32},{48,56},{56,48},{1,9},... | collective-permute-start | bytes 589832 | tf_op jit(solution)/shard_map/ppermute | solution.py:19
  84.3 0.3 collective-permute-start.12
  84.6 0.2 collective-permute-start.13
  84.8 0.3 collective-permute-start.14
  85.1 3.9 %collective-permute-start.10 = (bf16[2,32,1024]{2,1,0:T(8,128)(2,1)S(1)}, bf16[2,32,1024]{2,1,0:T(8,128)(2,1)S(1)}, u32[]{:S(2)}, u32[]{:S(2)}) collective-permute-start(bf16[2,32,1024]{2,1,0:T(8,128)(2,1)S(1)} %get-tuple-element.41.refs_0_), channel_id=1, source_target_pairs={{0,48},{8,56},{16,0},{24,8},{32,16},{40,24},{48,32},{56,40},{1,49}... | collective-permute-start | bytes 393224 | tf_op jit(solution)/shard_map/ppermute | solution.py:19
  89.0 3.5 %collective-permute-start.9 = (bf16[2,32,1024]{2,1,0:T(8,128)(2,1)S(1)}, bf16[2,32,1024]{2,1,0:T(8,128)(2,1)S(1)}, u32[]{:S(2)}, u32[]{:S(2)}) collective-permute-start(bf16[2,32,1024]{2,1,0:T(8,128)(2,1)S(1)} %get-tuple-element.41.refs_0_), channel_id=1, source_target_pairs={{0,32},{8,40},{16,48},{24,56},{32,0},{40,8},{48,16},{56,24},{1,33}... | collective-permute-start | bytes 393224 | tf_op jit(solution)/shard_map/ppermute | solution.py:19
  92.6 2.8 %copy-done.1 = bf16[3072,1024]{1,0:T(8,128)(2,1)S(1)} copy-done((bf16[3072,1024]{1,0:T(8,128)(2,1)S(1)}, bf16[3072,1024]{1,0:T(8,128)(2,1)}, u32[]{:S(2)}) %copy-start.1) | copy-done | bytes 6291480
  95.3 2.6 %shard_map.76.exchange_ref = f32[24,16,512]{2,1,0:T(8,128)S(1)} custom-call(s32[5]{0:T(128)S(1)} %copy-done.4, s32[4,6]{1,0:T(4,128)S(1)} %fusion.1.ids_ref, bf16[3072,1024]{1,0:T(8,128)(2,1)S(1)} %copy-done.1, bf16[8,32,512]{2,1,0:T(8,128)(2,1)S(1)} %all-to-all-done.1.row_ref, bf16[4,32,768]{2,1,0:T(8,128)(2,1)S(1)} %get-tuple-element.28.refs_0_, ...), custom_call_target="tpu_custom_call" | custom-call | flops 301989888 | bytes 4194304 | tf_op jit(solution)/shard_map/pallas_call | solution.py:240
  98.0 1.3 %collective-permute-done.9.refs_2_ = bf16[2,32,1024]{2,1,0:T(8,128)(2,1)S(1)} collective-permute-done((bf16[2,32,1024]{2,1,0:T(8,128)(2,1)S(1)}, bf16[2,32,1024]{2,1,0:T(8,128)(2,1)S(1)}, u32[]{:S(2)}, u32[]{:S(2)}) %collective-permute-start.9) | collective-permute-done | bytes 131104 | tf_op jit(solution)/shard_map/ppermute | solution.py:19
  99.3 3.8 %collective-permute-start.15 = (bf16[2,32,1024]{2,1,0:T(8,128)(2,1)S(1)}, bf16[2,32,1024]{2,1,0:T(8,128)(2,1)S(1)}, u32[]{:S(2)}, u32[]{:S(2)}) collective-permute-start(bf16[2,32,1024]{2,1,0:T(8,128)(2,1)S(1)} %get-tuple-element.41.refs_0_), channel_id=1, source_target_pairs={{0,8},{8,0},{16,24},{24,16},{32,40},{40,32},{48,56},{56,48},{1,9},... | collective-permute-start | bytes 393224 | tf_op jit(solution)/shard_map/ppermute | solution.py:19
  103.0 0.5 collective-permute-start.17
  103.5 0.1 fusion.order_ref
  103.7 0.3 collective-permute-done.15.refs_4_
  104.0 0.4 collective-permute-done.16.refs_5_
  104.4 0.2 collective-permute-done.17.refs_6_
  104.6 0.3 collective-permute-done.18.refs_7_
  104.9 2.9 %shard_map.77 = bf16[32,48,128]{2,1,0:T(8,128)(2,1)} custom-call(s32[5]{0:T(128)S(1)} %copy-done.4, s32[4,6]{1,0:T(4,128)S(1)} %fusion.1.ids_ref, bf16[512,512]{1,0:T(8,128)(2,1)S(1)} %fusion.order_ref, f32[24,16,512]{2,1,0:T(8,128)S(1)} %shard_map.76.exchange_ref, bf16[2,32,1024]{2,1,0:T(8,128)(2,1)S(1)} %get-tuple-element.41.refs_0_, ...), custom_call_target="tpu_custom_call" | custom-call | tf_op jit(solution)/shard_map/pallas_call | solution.py:313
  107.8 7.8 %all-to-all-start.2 = ((bf16[32,48,128]{2,1,0:T(8,128)(2,1)}), bf16[32,48,128]{2,1,0:T(8,128)(2,1)S(1)}, u32[]{:S(2)}, u32[]{:S(2)}) async-start(bf16[32,48,128]{2,1,0:T(8,128)(2,1)} %shard_map.77), calls=%async_computation.2 | async-start | bytes 786432 | tf_op jit(solution)/shard_map/all_to_all | solution.py:378
  115.7 10.1 %all-to-all-done.2 = bf16[32,48,128]{2,1,0:T(8,128)(2,1)S(1)} async-done(((bf16[32,48,128]{2,1,0:T(8,128)(2,1)}), bf16[32,48,128]{2,1,0:T(8,128)(2,1)S(1)}, u32[]{:S(2)}, u32[]{:S(2)}) %all-to-all-start.2) | async-done | bytes 393248 | tf_op jit(solution)/shard_map/all_to_all | solution.py:378
  125.9 0.7 broadcast_select_fusion
  (56 shorter events, 0.7 us)
Async XLA Ops:
  0.0 60.6 %copy-start = (f32[1024]{0:T(1024)S(1)}, f32[1024]{0:T(1024)}, u32[]{:S(2)}) copy-start(f32[1024]{0:T(1024)} %param.11) | copy-start | bytes 12292
  0.0 13.9 %copy-start.7 = (s32[2]{0:T(128)S(1)}, s32[2]{0:T(128)}, u32[]{:S(2)}) copy-start(s32[2]{0:T(128)} %param.12) | copy-start | bytes 28
  0.0 24.8 %copy-start.8 = (s32[6]{0:T(128)S(1)}, s32[6]{0:T(128)}, u32[]{:S(2)}) copy-start(s32[6]{0:T(128)} %param.13) | copy-start | bytes 76
  13.9 32.2 %copy-start.2 = (bf16[128,3072]{1,0:T(8,128)(2,1)}, bf16[128,3072]{1,0:T(8,128)(2,1)S(1)}, u32[]{:S(2)}) copy-start(bf16[128,3072]{1,0:T(8,128)(2,1)S(1)} %all-gather) | copy-start | bytes 2359300
  14.0 32.1 %copy-start.3 = (s32[5]{0:T(128)}, s32[5]{0:T(128)S(1)}, u32[]{:S(2)}) copy-start(s32[5]{0:T(128)S(1)} %pad_add_fusion.meta_ref) | copy-start | bytes 64
  14.7 4.6 %collective-permute-start = (bf16[32,768]{1,0:T(8,128)(2,1)S(1)}, bf16[32,768]{1,0:T(8,128)(2,1)S(1)}, u32[]{:S(2)}, u32[]{:S(2)}) collective-permute-start(bf16[32,768]{1,0:T(8,128)(2,1)S(1)} %get-tuple-element.26), channel_id=1, source_target_pairs={{0,16},{8,24},{16,0},{24,8},{32,48},{40,56},{48,32},{56,40},{1,17}... | collective-permute-start | bytes 147464 | tf_op jit(solution)/shard_map/ppermute | solution.py:19
  19.2 7.6 %collective-permute-start.1 = (bf16[32,768]{1,0:T(8,128)(2,1)S(1)}, bf16[32,768]{1,0:T(8,128)(2,1)S(1)}, u32[]{:S(2)}, u32[]{:S(2)}) collective-permute-start(bf16[32,768]{1,0:T(8,128)(2,1)S(1)} %add.75), channel_id=1, source_target_pairs={{0,48},{8,56},{16,32},{24,40},{32,16},{40,24},{48,0},{56,8},{1,49}... | collective-permute-start | bytes 147464 | tf_op jit(solution)/shard_map/ppermute | solution.py:19
  24.8 16.3 %collective-permute-start.4 = (bf16[4,32,768]{2,1,0:T(8,128)(2,1)S(1)}, bf16[4,32,768]{2,1,0:T(8,128)(2,1)S(1)}, u32[]{:S(2)}, u32[]{:S(2)}) collective-permute-start(bf16[4,32,768]{2,1,0:T(8,128)(2,1)S(1)} %get-tuple-element.28.refs_0_), channel_id=1, source_target_pairs={{0,32},{8,40},{16,48},{24,56},{32,0},{40,8},{48,16},{56,24},{1,33}... | collective-permute-start | bytes 589832 | tf_op jit(solution)/shard_map/ppermute | solution.py:19
  26.8 11.1 %collective-permute-start.2 = (bf16[32,768]{1,0:T(8,128)(2,1)S(1)}, bf16[32,768]{1,0:T(8,128)(2,1)S(1)}, u32[]{:S(2)}, u32[]{:S(2)}) collective-permute-start(bf16[32,768]{1,0:T(8,128)(2,1)S(1)} %add.76), channel_id=1, source_target_pairs={{0,8},{8,0},{16,24},{24,16},{32,40},{40,32},{48,56},{56,48},{1,9},... | collective-permute-start | bytes 147464 | tf_op jit(solution)/shard_map/ppermute | solution.py:19
  37.9 8.2 %copy-start.6 = (bf16[32,896]{1,0:T(8,128)(2,1)}, bf16[32,896]{1,0:T(8,128)(2,1)S(1)}, u32[]{:S(2)}) copy-start(bf16[32,896]{1,0:T(8,128)(2,1)S(1)} %pad_maximum_fusion.2.near_ref) | copy-start | bytes 172036
  37.9 3.1 %collective-permute-start.3 = (bf16[32,896]{1,0:T(8,128)(2,1)S(1)}, bf16[32,896]{1,0:T(8,128)(2,1)S(1)}, u32[]{:S(2)}, u32[]{:S(2)}) collective-permute-start(bf16[32,896]{1,0:T(8,128)(2,1)S(1)} %pad_maximum_fusion.2.near_ref), channel_id=1, source_target_pairs={{0,64},{64,0},{128,192},{192,128},{1,65},{65,1},{129,193},{193,129... | collective-permute-start | bytes 172040 | tf_op jit(solution)/shard_map/ppermute | solution.py:19
  41.1 5.1 %copy-start.5 = (bf16[32,896]{1,0:T(8,128)(2,1)}, bf16[32,896]{1,0:T(8,128)(2,1)S(1)}, u32[]{:S(2)}) copy-start(bf16[32,896]{1,0:T(8,128)(2,1)S(1)} %collective-permute-done.3.next_ref) | copy-start | bytes 172036
  41.1 5.1 %collective-permute-start.5 = (bf16[32,1792]{1,0:T(8,128)(2,1)S(1)}, bf16[32,1792]{1,0:T(8,128)(2,1)S(1)}, u32[]{:S(2)}, u32[]{:S(2)}) collective-permute-start(bf16[32,1792]{1,0:T(8,128)(2,1)S(1)} %pad_maximum_fusion.1), channel_id=1, source_target_pairs={{0,192},{64,128},{128,64},{192,0},{1,193},{65,129},{129,65},{193,1... | collective-permute-start | bytes 344072 | tf_op jit(solution)/shard_map/ppermute | solution.py:19
  41.9 14.3 %collective-permute-start.6 = (bf16[4,32,768]{2,1,0:T(8,128)(2,1)S(1)}, bf16[4,32,768]{2,1,0:T(8,128)(2,1)S(1)}, u32[]{:S(2)}, u32[]{:S(2)}) collective-permute-start(bf16[4,32,768]{2,1,0:T(8,128)(2,1)S(1)} %get-tuple-element.28.refs_0_), channel_id=1, source_target_pairs={{0,16},{8,24},{16,32},{24,40},{32,48},{40,56},{48,0},{56,8},{1,17}... | collective-permute-start | bytes 589832 | tf_op jit(solution)/shard_map/ppermute | solution.py:19
  43.3 12.9 %collective-permute-start.7 = (bf16[4,32,768]{2,1,0:T(8,128)(2,1)S(1)}, bf16[4,32,768]{2,1,0:T(8,128)(2,1)S(1)}, u32[]{:S(2)}, u32[]{:S(2)}) collective-permute-start(bf16[4,32,768]{2,1,0:T(8,128)(2,1)S(1)} %get-tuple-element.28.refs_0_), channel_id=1, source_target_pairs={{0,48},{8,56},{16,0},{24,8},{32,16},{40,24},{48,32},{56,40},{1,49}... | collective-permute-start | bytes 589832 | tf_op jit(solution)/shard_map/ppermute | solution.py:19
  46.2 0.6 copy-start.9
  56.1 20.5 %all-to-all-start = ((bf16[8,32,2560]{2,1,0:T(8,128)(2,1)}), bf16[8,32,2560]{2,1,0:T(8,128)(2,1)S(1)}, u32[]{:S(2)}, u32[]{:S(2)}) async-start(bf16[8,32,2560]{2,1,0:T(8,128)(2,1)} %shard_map.74), calls=%async_computation | async-start | bytes 2621440 | tf_op jit(solution)/shard_map/all_to_all | solution.py:363
  61.6 30.9 %copy-start.4 = (s32[5]{0:T(128)S(1)}, s32[5]{0:T(128)}, u32[]{:S(2)}) copy-start(s32[5]{0:T(128)} %copy-done.3) | copy-start | bytes 64
  77.4 15.2 %all-to-all-start.1 = ((bf16[8,32,512]{2,1,0:T(8,128)(2,1)}), bf16[8,32,512]{2,1,0:T(8,128)(2,1)S(1)}, u32[]{:S(2)}, u32[]{:S(2)}) async-start(bf16[8,32,512]{2,1,0:T(8,128)(2,1)} %get-tuple-element.36), calls=%async_computation.1 | async-start | bytes 524288 | tf_op jit(solution)/shard_map/all_to_all | solution.py:369
  81.5 7.5 %collective-permute-start.11 = (bf16[4,32,768]{2,1,0:T(8,128)(2,1)S(1)}, bf16[4,32,768]{2,1,0:T(8,128)(2,1)S(1)}, u32[]{:S(2)}, u32[]{:S(2)}) collective-permute-start(bf16[4,32,768]{2,1,0:T(8,128)(2,1)S(1)} %get-tuple-element.28.refs_0_), channel_id=1, source_target_pairs={{0,8},{8,0},{16,24},{24,16},{32,40},{40,32},{48,56},{56,48},{1,9},... | collective-permute-start | bytes 589832 | tf_op jit(solution)/shard_map/ppermute | solution.py:19
  84.3 4.7 %collective-permute-start.12 = (bf16[4,32,768]{2,1,0:T(8,128)(2,1)S(1)}, bf16[4,32,768]{2,1,0:T(8,128)(2,1)S(1)}, u32[]{:S(2)}, u32[]{:S(2)}) collective-permute-start(bf16[4,32,768]{2,1,0:T(8,128)(2,1)S(1)} %collective-permute-done.6.refs_1_), channel_id=1, source_target_pairs={{0,8},{8,0},{16,24},{24,16},{32,40},{40,32},{48,56},{56,48},{1,9},... | collective-permute-start | bytes 589832 | tf_op jit(solution)/shard_map/ppermute | solution.py:19
  84.6 7.9 %collective-permute-start.13 = (bf16[4,32,768]{2,1,0:T(8,128)(2,1)S(1)}, bf16[4,32,768]{2,1,0:T(8,128)(2,1)S(1)}, u32[]{:S(2)}, u32[]{:S(2)}) collective-permute-start(bf16[4,32,768]{2,1,0:T(8,128)(2,1)S(1)} %collective-permute-done.4.refs_2_), channel_id=1, source_target_pairs={{0,8},{8,0},{16,24},{24,16},{32,40},{40,32},{48,56},{56,48},{1,9},... | collective-permute-start | bytes 589832 | tf_op jit(solution)/shard_map/ppermute | solution.py:19
  84.8 7.7 %collective-permute-start.14 = (bf16[4,32,768]{2,1,0:T(8,128)(2,1)S(1)}, bf16[4,32,768]{2,1,0:T(8,128)(2,1)S(1)}, u32[]{:S(2)}, u32[]{:S(2)}) collective-permute-start(bf16[4,32,768]{2,1,0:T(8,128)(2,1)S(1)} %collective-permute-done.7.refs_3_), channel_id=1, source_target_pairs={{0,8},{8,0},{16,24},{24,16},{32,40},{40,32},{48,56},{56,48},{1,9},... | collective-permute-start | bytes 589832 | tf_op jit(solution)/shard_map/ppermute | solution.py:19
  85.1 12.9 %collective-permute-start.10 = (bf16[2,32,1024]{2,1,0:T(8,128)(2,1)S(1)}, bf16[2,32,1024]{2,1,0:T(8,128)(2,1)S(1)}, u32[]{:S(2)}, u32[]{:S(2)}) collective-permute-start(bf16[2,32,1024]{2,1,0:T(8,128)(2,1)S(1)} %get-tuple-element.41.refs_0_), channel_id=1, source_target_pairs={{0,48},{8,56},{16,0},{24,8},{32,16},{40,24},{48,32},{56,40},{1,49}... | collective-permute-start | bytes 393224 | tf_op jit(solution)/shard_map/ppermute | solution.py:19
  89.0 9.0 %collective-permute-start.8 = (bf16[2,32,1024]{2,1,0:T(8,128)(2,1)S(1)}, bf16[2,32,1024]{2,1,0:T(8,128)(2,1)S(1)}, u32[]{:S(2)}, u32[]{:S(2)}) collective-permute-start(bf16[2,32,1024]{2,1,0:T(8,128)(2,1)S(1)} %get-tuple-element.41.refs_0_), channel_id=1, source_target_pairs={{0,16},{8,24},{16,32},{24,40},{32,48},{40,56},{48,0},{56,8},{1,17}... | collective-permute-start | bytes 393224 | tf_op jit(solution)/shard_map/ppermute | solution.py:19
  89.0 10.2 %collective-permute-start.9 = (bf16[2,32,1024]{2,1,0:T(8,128)(2,1)S(1)}, bf16[2,32,1024]{2,1,0:T(8,128)(2,1)S(1)}, u32[]{:S(2)}, u32[]{:S(2)}) collective-permute-start(bf16[2,32,1024]{2,1,0:T(8,128)(2,1)S(1)} %get-tuple-element.41.refs_0_), channel_id=1, source_target_pairs={{0,32},{8,40},{16,48},{24,56},{32,0},{40,8},{48,16},{56,24},{1,33}... | collective-permute-start | bytes 393224 | tf_op jit(solution)/shard_map/ppermute | solution.py:19
  92.5 2.8 %copy-start.1 = (bf16[3072,1024]{1,0:T(8,128)(2,1)S(1)}, bf16[3072,1024]{1,0:T(8,128)(2,1)}, u32[]{:S(2)}) copy-start(bf16[3072,1024]{1,0:T(8,128)(2,1)} %whole_ref.3) | copy-start | bytes 18874372
  99.3 4.8 %collective-permute-start.15 = (bf16[2,32,1024]{2,1,0:T(8,128)(2,1)S(1)}, bf16[2,32,1024]{2,1,0:T(8,128)(2,1)S(1)}, u32[]{:S(2)}, u32[]{:S(2)}) collective-permute-start(bf16[2,32,1024]{2,1,0:T(8,128)(2,1)S(1)} %get-tuple-element.41.refs_0_), channel_id=1, source_target_pairs={{0,8},{8,0},{16,24},{24,16},{32,40},{40,32},{48,56},{56,48},{1,9},... | collective-permute-start | bytes 393224 | tf_op jit(solution)/shard_map/ppermute | solution.py:19
  103.0 1.3 %collective-permute-start.16 = (bf16[2,32,1024]{2,1,0:T(8,128)(2,1)S(1)}, bf16[2,32,1024]{2,1,0:T(8,128)(2,1)S(1)}, u32[]{:S(2)}, u32[]{:S(2)}) collective-permute-start(bf16[2,32,1024]{2,1,0:T(8,128)(2,1)S(1)} %collective-permute-done.8.refs_1_), channel_id=1, source_target_pairs={{0,8},{8,0},{16,24},{24,16},{32,40},{40,32},{48,56},{56,48},{1,9},... | collective-permute-start | bytes 393224 | tf_op jit(solution)/shard_map/ppermute | solution.py:19
  103.0 1.5 %collective-permute-start.17 = (bf16[2,32,1024]{2,1,0:T(8,128)(2,1)S(1)}, bf16[2,32,1024]{2,1,0:T(8,128)(2,1)S(1)}, u32[]{:S(2)}, u32[]{:S(2)}) collective-permute-start(bf16[2,32,1024]{2,1,0:T(8,128)(2,1)S(1)} %collective-permute-done.9.refs_2_), channel_id=1, source_target_pairs={{0,8},{8,0},{16,24},{24,16},{32,40},{40,32},{48,56},{56,48},{1,9},... | collective-permute-start | bytes 393224 | tf_op jit(solution)/shard_map/ppermute | solution.py:19
  103.5 1.3 %collective-permute-start.18 = (bf16[2,32,1024]{2,1,0:T(8,128)(2,1)S(1)}, bf16[2,32,1024]{2,1,0:T(8,128)(2,1)S(1)}, u32[]{:S(2)}, u32[]{:S(2)}) collective-permute-start(bf16[2,32,1024]{2,1,0:T(8,128)(2,1)S(1)} %collective-permute-done.10.refs_3_), channel_id=1, source_target_pairs={{0,8},{8,0},{16,24},{24,16},{32,40},{40,32},{48,56},{56,48},{1,9},... | collective-permute-start | bytes 393224 | tf_op jit(solution)/shard_map/ppermute | solution.py:19
  107.8 17.9 %all-to-all-start.2 = ((bf16[32,48,128]{2,1,0:T(8,128)(2,1)}), bf16[32,48,128]{2,1,0:T(8,128)(2,1)S(1)}, u32[]{:S(2)}, u32[]{:S(2)}) async-start(bf16[32,48,128]{2,1,0:T(8,128)(2,1)} %shard_map.77), calls=%async_computation.2 | async-start | bytes 786432 | tf_op jit(solution)/shard_map/all_to_all | solution.py:378
